TPU v7x, 256 devices: a whole 4x4x8 slice. The times are simulated.
256 devices in a mesh: user: 32 (over z, x), item: 4 (over y), rep: 2 (over core).
Axes of the slice: x: 4, y: 4, z: 8, core: 2. Of those that a mesh axis runs over, the one named last changes fastest.
Arguments:
- item_factors: bfloat16 [131072, 256], P(('user', 'item'))
- user_factors: bfloat16 [4096, 256], P(('user', 'item', 'rep')), may hold values from -6 to 6
- strengths: bfloat16 [4096, 1024], P(('user', 'item', 'rep')), may hold values from 0.5 to 40
- requests: int32 [256, 128], P(('user', 'item', 'rep')), may hold values from -1 to 7, as said below
- user_slots: int32 [4096, 8], P(('user', 'item', 'rep')), may hold values from 0 to 127, as said below
Outputs:
- user_new: float32 [4096, 256], P(('user', 'item', 'rep'))
- item_partial: float32 [131072, 256], P(('user', 'item'))
Inputs may be any that keep to these rules, and one draw needn't show every extreme that they name: `requests`: entry [d, o] names the one tile of owner o that device d reads, or is -1; every row has at least 8 entries that are not -1. `user_slots`: each row holds 8 different owners o, each with requests[u // 16, o] >= 0.
All inputs are finite; a program needn't handle non-finite values.
Results may differ from a plain program's by a relative error of at most 0.0051.
Values may be sent and summed in bfloat16 or wider, within the bound.
No kernel may reach another device: no remote copies, remote signals or barrier semaphores. Data moves between devices by JAX's collectives and lax.ppermute only.
A program may use at most 64 MiB of HBM per device.

v0:
```python
import functools

import jax
import jax.numpy as jnp
from jax import lax
from jax.experimental import pallas as pl
from jax.experimental.pallas import tpu as pltpu
from jax.sharding import Mesh, PartitionSpec as P

TILE = 128
RANK = 256
USERS = 16
SLOTS = 8
NZ, NX, NY = 8, 4, 4
PLANE = NX * NY
LINE_USERS = NZ * USERS
PLANE_ITEMS = PLANE * TILE
PENALTY = 1.0
EVERY = ("z", "x", "y", "c")
BF, F32 = jnp.bfloat16, jnp.float32
HIGH = lax.Precision.HIGHEST
WIDE = SLOTS * TILE + RANK + 2 * TILE
EXTRA = 16
VMEM_LIMIT = 16 * 2**20
HALF = LINE_USERS // 2


def ring_pairs(distance, phase):
    pairs = []
    for z in range(NZ):
        for x in range(NX):
            for y in range(NY):
                for c in range(2):
                    along_y = (c == 0) == (phase == 0)
                    x2 = x if along_y else (x + distance) % NX
                    y2 = (y + distance) % NY if along_y else y
                    pairs.append((((z * NX + x) * NY + y) * 2 + c, ((z * NX + x2) * NY + y2) * 2 + c))
    return pairs


def line_permute(value, partner):
    return lax.ppermute(value, "z", [(s, partner(s)) for s in range(NZ)])


def line_gather(value):
    for k in (1, 2, 4):
        value = jnp.concatenate([value, line_permute(value, lambda s: s ^ k)], axis=0)
    return value


def line_sum(keep, give):
    mine = keep + line_permute(give, lambda s: s ^ 1)
    others = [line_permute(mine, lambda s: (s + k) % NZ) for k in (2, 4, 6)]
    total = mine + others[0] + others[1] + others[2]
    return total, line_permute(total, lambda s: s ^ 1)


def split_halves(place_ref, part, keep_out, give_out):
    side = lax.rem(place_ref[0], 2)
    keep_out[...] = part[pl.ds(pl.multiple_of(side * HALF, HALF), HALF), :]
    give_out[...] = part[pl.ds(pl.multiple_of((1 - side) * HALF, HALF), HALF), :]


def join_halves(place_ref, mine_ref, other_ref, part):
    side = lax.rem(place_ref[0], 2)
    part[pl.ds(pl.multiple_of(side * HALF, HALF), HALF), :] = mine_ref[...]
    part[pl.ds(pl.multiple_of((1 - side) * HALF, HALF), HALF), :] = other_ref[...]


def swap_cores(value):
    return lax.ppermute(value, "c", [(0, 1), (1, 0)])


def against(vectors, block):
    return lax.dot_general(vectors, block, (((1,), (1,)), ((), ())), preferred_element_type=F32)


def weights_kernel(place_ref, pay_ref, weights_out, start_out, asked_out):
    z = place_ref[0]
    for s in range(NZ):
        place = lax.bitwise_xor(z, s)
        rows = pl.ds(s * USERS, USERS)
        start_out[rows, :] = pay_ref[place, :, SLOTS * TILE : SLOTS * TILE + RANK].astype(F32)
        slots = pay_ref[place, :, SLOTS * TILE + RANK : SLOTS * TILE + RANK + TILE].astype(F32)
        asked_out[s : s + 1, :] = pay_ref[place, :, WIDE - TILE :].astype(F32)[:1]
        owners = [jnp.broadcast_to(slots[:, k : k + 1], (USERS, TILE)) for k in range(SLOTS)]
        values = [pay_ref[place, :, k * TILE : (k + 1) * TILE].astype(F32) for k in range(SLOTS)]
        for j in range(PLANE):
            owner = (z * PLANE + j).astype(F32)
            total = jnp.zeros((USERS, TILE), F32)
            for k in range(SLOTS):
                total = jnp.where(owners[k] == owner, values[k], total)
            weights_out[rows, j * TILE : (j + 1) * TILE] = total.astype(BF)


def first_kernel(code_ref, row_ref, place_ref, start_ref, weights_ref, gram_a, gram_b, *rest):
    sources = rest[:10]
    keep_out, give_out, tiles, part, sems = rest[10:]

    def visit(index, carry):
        s = lax.div(index, PLANE)
        code = code_ref[index]
        row = pl.multiple_of(row_ref[index] * TILE, TILE)
        target = tiles.at[pl.ds(pl.multiple_of(index * TILE, TILE), TILE)]

        def choose(low, high):
            if high - low == 1:
                pltpu.make_async_copy(sources[low].at[pl.ds(row, TILE)], target, sems.at[s]).start()
                return
            middle = (low + high) // 2
            lax.cond(code < middle, lambda: choose(low, middle), lambda: choose(middle, high))

        choose(0, 10)
        return carry

    lax.fori_loop(0, NZ * PLANE, visit, 0)
    gram = gram_a[...] + gram_b[...]
    part[...] = -jnp.dot(start_ref[...], gram, precision=HIGH, preferred_element_type=F32)
    for s in range(NZ):
        rows = pl.ds(s * USERS, USERS)
        here = pl.ds(s * PLANE_ITEMS, PLANE_ITEMS)
        pltpu.make_async_copy(sources[0], tiles.at[here], sems.at[s]).wait()
        block = tiles[here, :]
        weights = weights_ref[rows, :].astype(F32)
        confidence = jnp.where(weights > 0.0, 1.0 + weights, 0.0).astype(BF)
        scaled = (weights * against(start_ref[rows, :].astype(BF), block)).astype(BF)
        both = jnp.dot(
            jnp.concatenate([confidence, scaled], axis=0), block, preferred_element_type=F32
        )
        part[rows, :] += both[:USERS] - both[USERS:]
    split_halves(place_ref, part, keep_out, give_out)


def second_kernel(
    place_ref, mine_ref, other_ref, start_ref, gram_a, gram_b, weights_ref, tiles,
    residual_out, keep_out, give_out, part,
):
    join_halves(place_ref, mine_ref, other_ref, residual_out)
    residual = residual_out[...] - PENALTY * start_ref[...]
    residual_out[...] = residual
    gram = gram_a[...] + gram_b[...]
    part[...] = jnp.dot(residual, gram, precision=HIGH, preferred_element_type=F32)
    for s in range(NZ):
        rows = pl.ds(s * USERS, USERS)
        block = tiles[pl.ds(s * PLANE_ITEMS, PLANE_ITEMS), :]
        weights = weights_ref[rows, :].astype(F32)
        scaled = (weights * against(residual_out[rows, :].astype(BF), block)).astype(BF)
        part[rows, :] += jnp.dot(scaled, block, preferred_element_type=F32)
    split_halves(place_ref, part, keep_out, give_out)


def third_kernel(
    place_ref, mine_ref, other_ref, start_ref, residual_ref, gram_a, gram_b, weights_ref, tiles,
    value_out, direction_out, norm_out, curve_out, part, column,
):
    join_halves(place_ref, mine_ref, other_ref, part)
    direction = residual_ref[...]
    image = part[...] + PENALTY * direction
    norm_now = jnp.sum(direction * direction, axis=1, keepdims=True)
    step = norm_now / jnp.sum(direction * image, axis=1, keepdims=True)
    value_out[...] = start_ref[...] + step * direction
    residual = direction - step * image
    norm_next = jnp.sum(residual * residual, axis=1, keepdims=True)
    direction = residual + (norm_next / norm_now) * direction
    direction_out[...] = direction
    norm_out[...] = jnp.broadcast_to(norm_next, (LINE_USERS, TILE))
    gram = gram_a[...] + gram_b[...]
    image = jnp.dot(direction, gram, precision=HIGH, preferred_element_type=F32)
    column[...] = jnp.broadcast_to(
        jnp.sum(direction * image, axis=1, keepdims=True), (LINE_USERS, TILE)
    )
    for s in range(NZ):
        rows = pl.ds(s * USERS, USERS)
        block = tiles[pl.ds(s * PLANE_ITEMS, PLANE_ITEMS), :]
        weights = weights_ref[rows, :].astype(F32)
        fitted = against(direction_out[rows, :].astype(BF), block)
        scaled = (weights * fitted).astype(BF).astype(F32)
        column[rows, :] += jnp.broadcast_to(
            jnp.sum(scaled * fitted, axis=1, keepdims=True), (USERS, TILE)
        )
    curve_out[...] = column[...].T[:8, :]


def fourth_kernel(
    place_ref, curve_ref, value_ref, direction_ref, norm_ref, weights_ref, asked_ref, tiles,
    solved_out, send_out, solved,
):
    z = place_ref[0]
    curve = jnp.broadcast_to(curve_ref[:1, :], (TILE, LINE_USERS)).T[:, :1]
    direction = direction_ref[...]
    curve = curve + PENALTY * jnp.sum(direction * direction, axis=1, keepdims=True)
    step = norm_ref[:, :1] / curve
    solved[...] = value_ref[...] + step * direction
    solved_out[...] = solved[pl.ds(pl.multiple_of(z * USERS, USERS), USERS), :]
    for j in range(PLANE):
        send_out[j, LINE_USERS:, :] = jnp.zeros((EXTRA, TILE + RANK), BF)
        send_out[j, LINE_USERS:, :TILE] = jnp.broadcast_to(
            asked_ref[j : j + 1, :], (EXTRA, TILE)
        ).astype(BF)
    for s in range(NZ):
        rows = pl.ds(s * USERS, USERS)
        block = tiles[pl.ds(s * PLANE_ITEMS, PLANE_ITEMS), :]
        weights = weights_ref[rows, :].astype(F32)
        confidence = (1.0 + weights).astype(BF).astype(F32)
        rounded = solved[rows, :].astype(BF)
        coeffs = confidence - weights * against(rounded, block)
        coeffs = jnp.where(weights > 0.0, coeffs, 0.0).astype(BF)
        for j in range(PLANE):
            send_out[j, rows, :TILE] = coeffs[:, j * TILE : (j + 1) * TILE]
            send_out[j, rows, TILE:] = rounded


def owner_kernel(got_ref, out_ref, coeffs, rounded):
    for p in range(PLANE):
        coeffs[:, p * LINE_USERS : (p + 1) * LINE_USERS] = (
            got_ref[p, :LINE_USERS, :TILE].astype(F32).T
        )
        rounded[p * LINE_USERS : (p + 1) * LINE_USERS, :] = got_ref[p, :LINE_USERS, TILE:]
    asked = jnp.concatenate(
        [got_ref[p, LINE_USERS : LINE_USERS + 8, :TILE].astype(F32)[:1] for p in range(PLANE)], axis=1
    )
    for t in range(out_ref.shape[0] // TILE):
        picked = jnp.where(asked == float(t), coeffs[...], 0.0).astype(BF)
        out_ref[t * TILE : (t + 1) * TILE, :] = jnp.dot(
            picked, rounded[...], preferred_element_type=F32
        )


def call(kernel, outs, operands, spaces, out_spaces, scratch, prefetch=0):
    memory = {"v": pltpu.VMEM, "a": pl.ANY}
    return pl.pallas_call(
        kernel,
        out_shape=outs,
        grid_spec=pltpu.PrefetchScalarGridSpec(
            num_scalar_prefetch=prefetch,
            grid=(1,),
            in_specs=[spec(memory[m]) for m in spaces],
            out_specs=[spec(memory[m]) for m in out_spaces],
            scratch_shapes=scratch,
        ),
        compiler_params=pltpu.CompilerParams(vmem_limit_bytes=VMEM_LIMIT),
    )(*operands)


def spec(space):
    return pl.BlockSpec(memory_space=space)


def shards(item_factors, user_factors, strengths, requests, user_slots):
    z, x, y, c = (lax.axis_index(name) for name in EVERY)
    shape = jax.ShapeDtypeStruct
    pay = jnp.concatenate(
        [
            strengths,
            user_factors,
            jnp.pad(user_slots, ((0, 0), (0, TILE - SLOTS))).astype(BF),
            jnp.broadcast_to(requests, (USERS, TILE)).astype(BF),
        ],
        axis=1,
    )
    half_rows = item_factors.shape[0] // 2
    half = lax.dynamic_slice_in_dim(item_factors, c * half_rows, half_rows, 0)
    near = jnp.concatenate(
        [half] + [lax.ppermute(half, EVERY, ring_pairs(d, 0)) for d in (1, -1, 2)], axis=0
    )
    near, pay = lax.optimization_barrier((near, pay))
    pays = line_gather(pay[None])
    up = lax.ppermute(near, EVERY, ring_pairs(1, 1))
    down = lax.ppermute(near, EVERY, ring_pairs(-1, 1))
    middle = near.shape[0] // 2
    far_a = lax.ppermute(up[:middle], EVERY, ring_pairs(1, 1))
    far_b = lax.ppermute(down[middle:], EVERY, ring_pairs(-1, 1))
    own = [near, up, down, far_a, far_b]
    other = [swap_cores(v) for v in own]
    gram_a = sum(
        lax.dot_general(v, v, (((0,), (0,)), ((), ())), preferred_element_type=F32) for v in own
    )
    gram_b = swap_cores(gram_a)

    place = z[None].astype(jnp.int32)
    vectors = shape((LINE_USERS, RANK), F32)
    halves = shape((HALF, RANK), F32)
    weights, start, asked = call(
        weights_kernel,
        [shape((LINE_USERS, PLANE_ITEMS), BF), vectors, shape((NZ, TILE), F32)],
        [place, pays],
        "v",
        "vvv",
        [],
        prefetch=1,
    )
    asked = lax.dynamic_slice(asked, (0, z * PLANE), (NZ, PLANE))
    asked_rows = jnp.repeat(asked.T, USERS, axis=1)
    tile = jnp.maximum(asked.astype(jnp.int32), 0)
    part_of = tile // 4
    j = jnp.arange(PLANE, dtype=jnp.int32)[None, :]
    along_x = (j // NY - x) % NX
    along_y = (j % NY - y) % NY
    first = jnp.where(part_of == 0, along_y, along_x)
    second = jnp.where(part_of == 0, along_x, along_y)

    def slot(delta):
        return jnp.where(delta == 3, 1, jnp.where(delta == 0, 0, delta + 1))

    first, second = slot(first), slot(second)
    code = jnp.where(second < 3, second, 3 + first // 2) + jnp.where(part_of == c, 0, 5)
    row = jnp.where(second < 3, first, first % 2) * 4 + tile % 4
    part = pltpu.VMEM(vectors.shape, F32)
    keep, give, tiles = call(
        first_kernel,
        [halves, halves, shape((NZ * PLANE_ITEMS, RANK), BF)],
        [code.reshape(-1), row.reshape(-1), place, start, weights, gram_a, gram_b, *own, *other],
        "vvvv" + "a" * 10,
        "vvv",
        [part, pltpu.SemaphoreType.DMA((NZ,))],
        prefetch=3,
    )
    residual, keep, give = call(
        second_kernel,
        [vectors, halves, halves],
        [place, *line_sum(keep, give), start, gram_a, gram_b, weights, tiles],
        "v" * 7,
        "vvv",
        [part],
        prefetch=1,
    )
    value, direction, norm, curve = call(
        third_kernel,
        [vectors, vectors, shape((LINE_USERS, TILE), F32), shape((8, LINE_USERS), F32)],
        [place, *line_sum(keep, give), start, residual, gram_a, gram_b, weights, tiles],
        "v" * 8,
        "vvvv",
        [part, pltpu.VMEM((LINE_USERS, TILE), F32)],
        prefetch=1,
    )
    for k in (1, 2, 4):
        curve = curve + line_permute(curve, lambda s: s ^ k)
    solved, send = call(
        fourth_kernel,
        [shape((USERS, RANK), F32), shape((PLANE, LINE_USERS + EXTRA, TILE + RANK), BF)],
        [place, curve, value, direction, norm, weights, asked_rows, tiles],
        "v" * 7,
        "vv",
        [part],
        prefetch=1,
    )
    got = lax.all_to_all(send, ("x", "y"), split_axis=0, concat_axis=0, tiled=True)
    [sums] = call(
        owner_kernel,
        [shape(item_factors.shape, F32)],
        [got],
        "v",
        "v",
        [
            pltpu.VMEM((TILE, PLANE * LINE_USERS), F32),
            pltpu.VMEM((PLANE * LINE_USERS, RANK), BF),
        ],
    )
    return solved, sums + swap_cores(sums)


def solution(mesh):
    cut = Mesh(mesh.devices.reshape(NZ, NX, NY, 2), EVERY)
    every, owner = P(EVERY, None), P(("z", "x", "y"), None)
    return jax.shard_map(
        shards,
        mesh=cut,
        in_specs=(owner, every, every, every, every),
        out_specs=(every, owner),
        check_vma=False,
    )
```

profile of v0, /device:TPU:1, one launch (start us, length us, event | category | flops | bytes accessed | tf_op | source)
XLA Modules:
  0.0 172.5 jit_solution(13357180033786344243)
XLA Ops:
  1.7 2.1 %collective-permute-start = (bf16[512,256]{1,0:T(8,128)(2,1)S(1)}, bf16[512,256]{1,0:T(8,128)(2,1)S(1)}, u32[]{:S(2)}, u32[]{:S(2)}) collective-permute-start(bf16[512,256]{1,0:T(8,128)(2,1)S(1)} %constant_dynamic-slice_fusion), channel_id=1, source_target_pairs={{0,2},{1,9},{2,4},{3,11},{4,6},{5,13},{6,0},{7,15},{8,10},{9,17},{... | collective-permute-start | bytes 786440 | tf_op jit(solution)/shard_map/ppermute | solution.py:264
  3.8 1.4 collective-permute-start.1
  5.2 1.6 collective-permute-start.2
  9.3 3.8 %collective-permute-done.2 = bf16[512,256]{1,0:T(8,128)(2,1)S(1)} collective-permute-done((bf16[512,256]{1,0:T(8,128)(2,1)S(1)}, bf16[512,256]{1,0:T(8,128)(2,1)S(1)}, u32[]{:S(2)}, u32[]{:S(2)}) %collective-permute-start.2) | collective-permute-done | bytes 262176 | tf_op jit(solution)/shard_map/ppermute | solution.py:264
  14.3 1.8 %collective-permute-start.7 = (bf16[2048,256]{1,0:T(8,128)(2,1)S(1)}, bf16[2048,256]{1,0:T(8,128)(2,1)}, u32[]{:S(2)}, u32[]{:S(2)}) collective-permute-start(bf16[2048,256]{1,0:T(8,128)(2,1)S(1)} %pad_maximum_fusion.rest_0_), channel_id=1, source_target_pairs={{0,24},{1,7},{2,26},{3,1},{4,28},{5,3},{6,30},{7,5},{8,0},{9,15},{... | collective-permute-start | bytes 3145736 | tf_op jit(solution)/shard_map/ppermute | solution.py:269
  16.1 1.6 collective-permute-start.3
  19.2 3.4 %collective-permute-start.4 = (bf16[2,16,1536]{2,1,0:T(8,128)(2,1)S(1)}, bf16[2,16,1536]{2,1,0:T(8,128)(2,1)S(1)}, u32[]{:S(2)}, u32[]{:S(2)}) collective-permute-start(bf16[2,16,1536]{2,1,0:T(8,128)(2,1)S(1)} %pad_maximum_fusion.3), channel_id=1, source_target_pairs={{0,64},{32,96},{64,0},{96,32},{128,192},{160,224},{192,128},{224,1... | collective-permute-start | bytes 294920 | tf_op jit(solution)/shard_map/ppermute | solution.py:42
  22.6 5.9 %collective-permute-done.6.rest_1_ = bf16[2048,256]{1,0:T(8,128)(2,1)S(1)} collective-permute-done((bf16[2048,256]{1,0:T(8,128)(2,1)S(1)}, bf16[2048,256]{1,0:T(8,128)(2,1)S(1)}, u32[]{:S(2)}, u32[]{:S(2)}) %collective-permute-start.6) | collective-permute-done | bytes 1048608 | tf_op jit(solution)/shard_map/ppermute | solution.py:268
  29.1 3.9 %collective-permute-start.11 = (bf16[2048,256]{1,0:T(8,128)(2,1)S(1)}, bf16[2048,256]{1,0:T(8,128)(2,1)S(1)}, u32[]{:S(2)}, u32[]{:S(2)}) collective-permute-start(bf16[2048,256]{1,0:T(8,128)(2,1)S(1)} %pad_maximum_fusion.rest_0_), channel_id=1, source_target_pairs={{0,1},{1,0},{2,3},{3,2},{4,5},{5,4},{6,7},{7,6},{8,9},{9,8},{10,11... | collective-permute-start | bytes 3145736 | tf_op jit(solution)/shard_map/ppermute | solution.py:71
  33.0 6.0 %collective-permute-start.5 = (bf16[4,16,1536]{2,1,0:T(8,128)(2,1)S(1)}, bf16[4,16,1536]{2,1,0:T(8,128)(2,1)S(1)}, u32[]{:S(2)}, u32[]{:S(2)}) collective-permute-start(bf16[4,16,1536]{2,1,0:T(8,128)(2,1)S(1)} %pad_maximum_fusion.2), channel_id=1, source_target_pairs={{0,128},{32,160},{64,192},{96,224},{128,0},{160,32},{192,64},{224,... | collective-permute-start | bytes 589832 | tf_op jit(solution)/shard_map/ppermute | solution.py:42
  40.1 1.8 %collective-permute-start.9 = (bf16[1024,256]{1,0:T(8,128)(2,1)S(1)}, bf16[1024,256]{1,0:T(8,128)(2,1)}, u32[]{:S(2)}, u32[]{:S(2)}) collective-permute-start(bf16[1024,256]{1,0:T(8,128)(2,1)S(1)} %slice.9), channel_id=1, source_target_pairs={{0,24},{1,7},{2,26},{3,1},{4,28},{5,3},{6,30},{7,5},{8,0},{9,15},{... | collective-permute-start | bytes 1572872 | tf_op jit(solution)/shard_map/ppermute | solution.py:272
  41.9 1.5 collective-permute-start.12
  44.1 1.5 fusion.24
  45.6 3.0 %collective-permute-done.9.rest_4_ = bf16[1024,256]{1,0:T(8,128)(2,1)} collective-permute-done((bf16[1024,256]{1,0:T(8,128)(2,1)S(1)}, bf16[1024,256]{1,0:T(8,128)(2,1)}, u32[]{:S(2)}, u32[]{:S(2)}) %collective-permute-start.9) | collective-permute-done | bytes 524320 | tf_op jit(solution)/shard_map/ppermute | solution.py:272
  48.7 1.5 collective-permute-start.14
  50.2 1.6 fusion.25
  51.9 2.1 %fusion.1.gram_a = f32[256,256]{1,0:T(8,128)S(1)} fusion(f32[256,256]{1,0:T(8,128)S(1)} %fusion.25, f32[256,256]{1,0:T(8,128)S(1)} %fusion.24, f32[256,256]{1,0:T(8,128)S(1)} %convolution_add_fusion.1, bf16[2048,256]{1,0:T(8,128)(2,1)} %collective-permute-done.7.rest_2_), kind=kOutput, calls=%fused_computation.2 | convolution fusion | flops 268632064 | bytes 2097152 | tf_op jit(solution)/shard_map/dot_general | solution.py:276
  56.8 1.2 copy-done.4
  58.0 13.9 %shard_map.69 = (f32[64,256]{1,0:T(8,128)S(1)}, f32[64,256]{1,0:T(8,128)S(1)}, bf16[16384,256]{1,0:T(8,128)(2,1)S(1)}) custom-call(s32[128]{0:T(128)S(1)} %reshape.104.code_ref, s32[128]{0:T(128)S(1)} %reshape.105.row_ref, s32[1]{0:T(128)} %bitcast.place_ref, f32[128,256]{1,0:T(8,128)S(1)} %get-tuple-element.21.start_ref, ...), custom_call_target="tpu_custom_call" | custom-call | tf_op jit(solution)/shard_map/pallas_call | solution.py:231
  71.9 1.9 %collective-permute-start.16 = (f32[64,256]{1,0:T(8,128)S(1)}, f32[64,256]{1,0:T(8,128)S(1)}, u32[]{:S(2)}, u32[]{:S(2)}) collective-permute-start(f32[64,256]{1,0:T(8,128)S(1)} %get-tuple-element.25), channel_id=1, source_target_pairs={{0,32},{32,0},{64,96},{96,64},{128,160},{160,128},{192,224},{224,1... | collective-permute-start | bytes 196616 | tf_op jit(solution)/shard_map/ppermute | solution.py:42
  73.7 1.7 collective-permute-done.16
  75.4 1.2 collective-permute-start.17
  76.5 2.6 %collective-permute-start.18 = (f32[64,256]{1,0:T(8,128)S(1)}, f32[64,256]{1,0:T(8,128)S(1)}, u32[]{:S(2)}, u32[]{:S(2)}) collective-permute-start(f32[64,256]{1,0:T(8,128)S(1)} %add.134), channel_id=1, source_target_pairs={{0,128},{32,160},{64,192},{96,224},{128,0},{160,32},{192,64},{224,... | collective-permute-start | bytes 196616 | tf_op jit(solution)/shard_map/ppermute | solution.py:42
  79.1 2.1 %collective-permute-start.19 = (f32[64,256]{1,0:T(8,128)S(1)}, f32[64,256]{1,0:T(8,128)S(1)}, u32[]{:S(2)}, u32[]{:S(2)}) collective-permute-start(f32[64,256]{1,0:T(8,128)S(1)} %add.134), channel_id=1, source_target_pairs={{0,192},{32,224},{64,0},{96,32},{128,64},{160,96},{192,128},{224,1... | collective-permute-start | bytes 196616 | tf_op jit(solution)/shard_map/ppermute | solution.py:42
  81.2 3.2 %collective-permute-done.18 = f32[64,256]{1,0:T(8,128)S(1)} collective-permute-done((f32[64,256]{1,0:T(8,128)S(1)}, f32[64,256]{1,0:T(8,128)S(1)}, u32[]{:S(2)}, u32[]{:S(2)}) %collective-permute-start.18) | collective-permute-done | bytes 65568 | tf_op jit(solution)/shard_map/ppermute | solution.py:42
  84.4 1.6 collective-permute-start.20
  86.0 2.7 %collective-permute-done.20.other_ref = f32[64,256]{1,0:T(8,128)S(1)} collective-permute-done((f32[64,256]{1,0:T(8,128)S(1)}, f32[64,256]{1,0:T(8,128)S(1)}, u32[]{:S(2)}, u32[]{:S(2)}) %collective-permute-start.20) | collective-permute-done | bytes 65568 | tf_op jit(solution)/shard_map/ppermute | solution.py:42
  88.7 4.7 %shard_map.70 = (f32[128,256]{1,0:T(8,128)S(1)}, f32[64,256]{1,0:T(8,128)S(1)}, f32[64,256]{1,0:T(8,128)S(1)}) custom-call(s32[1]{0:T(128)} %bitcast.place_ref, f32[64,256]{1,0:T(8,128)S(1)} %add_add_fusion.1.mine_ref, f32[64,256]{1,0:T(8,128)S(1)} %collective-permute-done.20.other_ref, f32[128,256]{1,0:T(8,128)S(1)} %get-tuple-element.21.start_ref, ...), custom_call_target="tpu_custom_call" | custom-call | tf_op jit(solution)/shard_map/pallas_call | solution.py:231
  94.0 2.5 %collective-permute-done.21 = f32[64,256]{1,0:T(8,128)S(1)} collective-permute-done((f32[64,256]{1,0:T(8,128)S(1)}, f32[64,256]{1,0:T(8,128)S(1)}, u32[]{:S(2)}, u32[]{:S(2)}) %collective-permute-start.21) | collective-permute-done | bytes 65568 | tf_op jit(solution)/shard_map/ppermute | solution.py:42
  96.5 2.4 %collective-permute-start.22 = (f32[64,256]{1,0:T(8,128)S(1)}, f32[64,256]{1,0:T(8,128)S(1)}, u32[]{:S(2)}, u32[]{:S(2)}) collective-permute-start(f32[64,256]{1,0:T(8,128)S(1)} %add.138), channel_id=1, source_target_pairs={{0,64},{32,96},{64,128},{96,160},{128,192},{160,224},{192,0},{224,... | collective-permute-start | bytes 196616 | tf_op jit(solution)/shard_map/ppermute | solution.py:42
  99.0 1.8 %collective-permute-start.23 = (f32[64,256]{1,0:T(8,128)S(1)}, f32[64,256]{1,0:T(8,128)S(1)}, u32[]{:S(2)}, u32[]{:S(2)}) collective-permute-start(f32[64,256]{1,0:T(8,128)S(1)} %add.138), channel_id=1, source_target_pairs={{0,128},{32,160},{64,192},{96,224},{128,0},{160,32},{192,64},{224,... | collective-permute-start | bytes 196616 | tf_op jit(solution)/shard_map/ppermute | solution.py:42
  100.8 2.6 %collective-permute-start.24 = (f32[64,256]{1,0:T(8,128)S(1)}, f32[64,256]{1,0:T(8,128)S(1)}, u32[]{:S(2)}, u32[]{:S(2)}) collective-permute-start(f32[64,256]{1,0:T(8,128)S(1)} %add.138), channel_id=1, source_target_pairs={{0,192},{32,224},{64,0},{96,32},{128,64},{160,96},{192,128},{224,1... | collective-permute-start | bytes 196616 | tf_op jit(solution)/shard_map/ppermute | solution.py:42
  103.4 2.6 %collective-permute-done.23 = f32[64,256]{1,0:T(8,128)S(1)} collective-permute-done((f32[64,256]{1,0:T(8,128)S(1)}, f32[64,256]{1,0:T(8,128)S(1)}, u32[]{:S(2)}, u32[]{:S(2)}) %collective-permute-start.23) | collective-permute-done | bytes 65568 | tf_op jit(solution)/shard_map/ppermute | solution.py:42
  106.0 2.0 %collective-permute-start.25 = (f32[64,256]{1,0:T(8,128)S(1)}, f32[64,256]{1,0:T(8,128)S(1)}, u32[]{:S(2)}, u32[]{:S(2)}) collective-permute-start(f32[64,256]{1,0:T(8,128)S(1)} %add_add_fusion.mine_ref), channel_id=1, source_target_pairs={{0,32},{32,0},{64,96},{96,64},{128,160},{160,128},{192,224},{224,1... | collective-permute-start | bytes 196616 | tf_op jit(solution)/shard_map/ppermute | solution.py:42
  108.0 1.7 collective-permute-done.25.other_ref
  109.7 3.7 %shard_map.71 = (f32[128,256]{1,0:T(8,128)S(1)}, f32[128,256]{1,0:T(8,128)S(1)}, f32[128,128]{1,0:T(8,128)S(1)}, f32[8,128]{1,0:T(8,128)S(1)}) custom-call(s32[1]{0:T(128)} %bitcast.place_ref, f32[64,256]{1,0:T(8,128)S(1)} %add_add_fusion.mine_ref, f32[64,256]{1,0:T(8,128)S(1)} %collective-permute-done.25.other_ref, ...), custom_call_target="tpu_custom_call" | custom-call | tf_op jit(solution)/shard_map/pallas_call | solution.py:231
  113.4 1.9 %collective-permute-start.26 = (f32[8,128]{1,0:T(8,128)S(1)}, f32[8,128]{1,0:T(8,128)S(1)}, u32[]{:S(2)}, u32[]{:S(2)}) collective-permute-start(f32[8,128]{1,0:T(8,128)S(1)} %get-tuple-element.30), channel_id=1, source_target_pairs={{0,32},{32,0},{64,96},{96,64},{128,160},{160,128},{192,224},{224,1... | collective-permute-start | bytes 12296 | tf_op jit(solution)/shard_map/ppermute | solution.py:42
  116.3 2.3 %collective-permute-start.27 = (f32[8,128]{1,0:T(8,128)S(1)}, f32[8,128]{1,0:T(8,128)S(1)}, u32[]{:S(2)}, u32[]{:S(2)}) collective-permute-start(f32[8,128]{1,0:T(8,128)S(1)} %add.142), channel_id=1, source_target_pairs={{0,64},{32,96},{64,0},{96,32},{128,192},{160,224},{192,128},{224,1... | collective-permute-start | bytes 12296 | tf_op jit(solution)/shard_map/ppermute | solution.py:42
  118.6 1.1 collective-permute-done.27
  119.7 2.8 %collective-permute-start.28 = (f32[8,128]{1,0:T(8,128)S(1)}, f32[8,128]{1,0:T(8,128)S(1)}, u32[]{:S(2)}, u32[]{:S(2)}) collective-permute-start(f32[8,128]{1,0:T(8,128)S(1)} %add.143), channel_id=1, source_target_pairs={{0,128},{32,160},{64,192},{96,224},{128,0},{160,32},{192,64},{224,... | collective-permute-start | bytes 12296 | tf_op jit(solution)/shard_map/ppermute | solution.py:42
  122.8 3.2 %collective-permute-done.28 = f32[8,128]{1,0:T(8,128)S(1)} collective-permute-done((f32[8,128]{1,0:T(8,128)S(1)}, f32[8,128]{1,0:T(8,128)S(1)}, u32[]{:S(2)}, u32[]{:S(2)}) %collective-permute-start.28) | collective-permute-done | bytes 4128 | tf_op jit(solution)/shard_map/ppermute | solution.py:42
  126.0 3.4 %copy-done.2 = bf16[16384,256]{1,0:T(8,128)(2,1)S(1)} copy-done((bf16[16384,256]{1,0:T(8,128)(2,1)S(1)}, bf16[16384,256]{1,0:T(8,128)(2,1)}, u32[]{:S(2)}) %copy-start.2) | copy-done | bytes 8388632
  129.4 2.5 %shard_map.72 = (f32[16,256]{1,0:T(8,128)}, bf16[16,144,384]{2,1,0:T(8,128)(2,1)S(1)}) custom-call(s32[1]{0:T(128)} %bitcast.place_ref, f32[8,128]{1,0:T(8,128)S(1)} %add.144.curve_ref, f32[128,256]{1,0:T(8,128)S(1)} %get-tuple-element.31.value_ref, f32[128,256]{1,0:T(8,128)S(1)} %get-tuple-element.32.direction_ref, ...), custom_call_target="tpu_custom_call" | custom-call | tf_op jit(solution)/shard_map/pallas_call | solution.py:231
  131.9 23.8 %all_to_all.5.got_ref = bf16[16,144,384]{2,1,0:T(8,128)(2,1)S(1)} all-to-all(bf16[16,144,384]{2,1,0:T(8,128)(2,1)S(1)} %get-tuple-element.35), channel_id=1, replica_groups=mesh['z'=8,'x'=4,'y'=4,'c'=2] {'x','y'}, dimensions={0} | all-to-all | bytes 3538944 | tf_op jit(solution)/shard_map/all_to_all | solution.py:347
  155.7 1.3 shard_map.73
  157.0 12.2 %collective-permute-start.29 = (f32[1024,256]{1,0:T(8,128)S(1)}, f32[1024,256]{1,0:T(8,128)S(1)}, u32[]{:S(2)}, u32[]{:S(2)}) collective-permute-start(f32[1024,256]{1,0:T(8,128)S(1)} %shard_map.73), channel_id=1, source_target_pairs={{0,1},{1,0},{2,3},{3,2},{4,5},{5,4},{6,7},{7,6},{8,9},{9,8},{10,11... | collective-permute-start | bytes 3145736 | tf_op jit(solution)/shard_map/ppermute | solution.py:71
  169.1 2.3 %collective-permute-done.29 = f32[1024,256]{1,0:T(8,128)S(1)} collective-permute-done((f32[1024,256]{1,0:T(8,128)S(1)}, f32[1024,256]{1,0:T(8,128)S(1)}, u32[]{:S(2)}, u32[]{:S(2)}) %collective-permute-start.29) | collective-permute-done | bytes 1048608 | tf_op jit(solution)/shard_map/ppermute | solution.py:71
  171.4 1.1 add.145
  (64 shorter events, 13.3 us)
Async XLA Ops:
  0.6 1.0 copy-start
  1.7 7.4 %collective-permute-start = (bf16[512,256]{1,0:T(8,128)(2,1)S(1)}, bf16[512,256]{1,0:T(8,128)(2,1)S(1)}, u32[]{:S(2)}, u32[]{:S(2)}) collective-permute-start(bf16[512,256]{1,0:T(8,128)(2,1)S(1)} %constant_dynamic-slice_fusion), channel_id=1, source_target_pairs={{0,2},{1,9},{2,4},{3,11},{4,6},{5,13},{6,0},{7,15},{8,10},{9,17},{... | collective-permute-start | bytes 786440 | tf_op jit(solution)/shard_map/ppermute | solution.py:264
  3.8 5.5 %collective-permute-start.1 = (bf16[512,256]{1,0:T(8,128)(2,1)S(1)}, bf16[512,256]{1,0:T(8,128)(2,1)S(1)}, u32[]{:S(2)}, u32[]{:S(2)}) collective-permute-start(bf16[512,256]{1,0:T(8,128)(2,1)S(1)} %constant_dynamic-slice_fusion), channel_id=1, source_target_pairs={{0,6},{1,25},{2,0},{3,27},{4,2},{5,29},{6,4},{7,31},{8,14},{9,1},{... | collective-permute-start | bytes 786440 | tf_op jit(solution)/shard_map/ppermute | solution.py:264
  5.2 8.0 %collective-permute-start.2 = (bf16[512,256]{1,0:T(8,128)(2,1)S(1)}, bf16[512,256]{1,0:T(8,128)(2,1)S(1)}, u32[]{:S(2)}, u32[]{:S(2)}) collective-permute-start(bf16[512,256]{1,0:T(8,128)(2,1)S(1)} %constant_dynamic-slice_fusion), channel_id=1, source_target_pairs={{0,4},{1,17},{2,6},{3,19},{4,0},{5,21},{6,2},{7,23},{8,12},{9,25},... | collective-permute-start | bytes 786440 | tf_op jit(solution)/shard_map/ppermute | solution.py:264
  13.2 15.3 %collective-permute-start.6 = (bf16[2048,256]{1,0:T(8,128)(2,1)S(1)}, bf16[2048,256]{1,0:T(8,128)(2,1)S(1)}, u32[]{:S(2)}, u32[]{:S(2)}) collective-permute-start(bf16[2048,256]{1,0:T(8,128)(2,1)S(1)} %pad_maximum_fusion.rest_0_), channel_id=1, source_target_pairs={{0,8},{1,3},{2,10},{3,5},{4,12},{5,7},{6,14},{7,1},{8,16},{9,11},{... | collective-permute-start | bytes 3145736 | tf_op jit(solution)/shard_map/ppermute | solution.py:268
  14.3 24.8 %collective-permute-start.7 = (bf16[2048,256]{1,0:T(8,128)(2,1)S(1)}, bf16[2048,256]{1,0:T(8,128)(2,1)}, u32[]{:S(2)}, u32[]{:S(2)}) collective-permute-start(bf16[2048,256]{1,0:T(8,128)(2,1)S(1)} %pad_maximum_fusion.rest_0_), channel_id=1, source_target_pairs={{0,24},{1,7},{2,26},{3,1},{4,28},{5,3},{6,30},{7,5},{8,0},{9,15},{... | collective-permute-start | bytes 3145736 | tf_op jit(solution)/shard_map/ppermute | solution.py:269
  16.1 3.1 %collective-permute-start.3 = (bf16[1,16,1536]{2,1,0:T(8,128)(2,1)S(1)}, bf16[1,16,1536]{2,1,0:T(8,128)(2,1)S(1)}, u32[]{:S(2)}, u32[]{:S(2)}) collective-permute-start(bf16[1,16,1536]{2,1,0:T(8,128)(2,1)S(1)} %bitcast.16), channel_id=1, source_target_pairs={{0,32},{32,0},{64,96},{96,64},{128,160},{160,128},{192,224},{224,1... | collective-permute-start | bytes 147464 | tf_op jit(solution)/shard_map/ppermute | solution.py:42
  19.2 13.8 %collective-permute-start.4 = (bf16[2,16,1536]{2,1,0:T(8,128)(2,1)S(1)}, bf16[2,16,1536]{2,1,0:T(8,128)(2,1)S(1)}, u32[]{:S(2)}, u32[]{:S(2)}) collective-permute-start(bf16[2,16,1536]{2,1,0:T(8,128)(2,1)S(1)} %pad_maximum_fusion.3), channel_id=1, source_target_pairs={{0,64},{32,96},{64,0},{96,32},{128,192},{160,224},{192,128},{224,1... | collective-permute-start | bytes 294920 | tf_op jit(solution)/shard_map/ppermute | solution.py:42
  28.5 15.4 %collective-permute-start.8 = (bf16[1024,256]{1,0:T(8,128)(2,1)S(1)}, bf16[1024,256]{1,0:T(8,128)(2,1)}, u32[]{:S(2)}, u32[]{:S(2)}) collective-permute-start(bf16[1024,256]{1,0:T(8,128)(2,1)S(1)} %slice.8), channel_id=1, source_target_pairs={{0,8},{1,3},{2,10},{3,5},{4,12},{5,7},{6,14},{7,1},{8,16},{9,11},{... | collective-permute-start | bytes 1572872 | tf_op jit(solution)/shard_map/ppermute | solution.py:271
  29.1 24.8 %collective-permute-start.11 = (bf16[2048,256]{1,0:T(8,128)(2,1)S(1)}, bf16[2048,256]{1,0:T(8,128)(2,1)S(1)}, u32[]{:S(2)}, u32[]{:S(2)}) collective-permute-start(bf16[2048,256]{1,0:T(8,128)(2,1)S(1)} %pad_maximum_fusion.rest_0_), channel_id=1, source_target_pairs={{0,1},{1,0},{2,3},{3,2},{4,5},{5,4},{6,7},{7,6},{8,9},{9,8},{10,11... | collective-permute-start | bytes 3145736 | tf_op jit(solution)/shard_map/ppermute | solution.py:71
  33.0 18.8 %collective-permute-start.5 = (bf16[4,16,1536]{2,1,0:T(8,128)(2,1)S(1)}, bf16[4,16,1536]{2,1,0:T(8,128)(2,1)S(1)}, u32[]{:S(2)}, u32[]{:S(2)}) collective-permute-start(bf16[4,16,1536]{2,1,0:T(8,128)(2,1)S(1)} %pad_maximum_fusion.2), channel_id=1, source_target_pairs={{0,128},{32,160},{64,192},{96,224},{128,0},{160,32},{192,64},{224,... | collective-permute-start | bytes 589832 | tf_op jit(solution)/shard_map/ppermute | solution.py:42
  40.1 8.5 %collective-permute-start.9 = (bf16[1024,256]{1,0:T(8,128)(2,1)S(1)}, bf16[1024,256]{1,0:T(8,128)(2,1)}, u32[]{:S(2)}, u32[]{:S(2)}) collective-permute-start(bf16[1024,256]{1,0:T(8,128)(2,1)S(1)} %slice.9), channel_id=1, source_target_pairs={{0,24},{1,7},{2,26},{3,1},{4,28},{5,3},{6,30},{7,5},{8,0},{9,15},{... | collective-permute-start | bytes 1572872 | tf_op jit(solution)/shard_map/ppermute | solution.py:272
  41.9 14.8 %collective-permute-start.12 = (bf16[2048,256]{1,0:T(8,128)(2,1)S(1)}, bf16[2048,256]{1,0:T(8,128)(2,1)}, u32[]{:S(2)}, u32[]{:S(2)}) collective-permute-start(bf16[2048,256]{1,0:T(8,128)(2,1)S(1)} %collective-permute-done.6.rest_1_), channel_id=1, source_target_pairs={{0,1},{1,0},{2,3},{3,2},{4,5},{5,4},{6,7},{7,6},{8,9},{9,8},{10,11... | collective-permute-start | bytes 3145736 | tf_op jit(solution)/shard_map/ppermute | solution.py:71
  44.0 12.8 %collective-permute-start.13 = (bf16[2048,256]{1,0:T(8,128)(2,1)}, bf16[2048,256]{1,0:T(8,128)(2,1)}, u32[]{:S(2)}, u32[]{:S(2)}) collective-permute-start(bf16[2048,256]{1,0:T(8,128)(2,1)} %collective-permute-done.7.rest_2_), channel_id=1, source_target_pairs={{0,1},{1,0},{2,3},{3,2},{4,5},{5,4},{6,7},{7,6},{8,9},{9,8},{10,11... | collective-permute-start | bytes 3145736 | tf_op jit(solution)/shard_map/ppermute | solution.py:71
  48.7 8.1 %collective-permute-start.14 = (bf16[1024,256]{1,0:T(8,128)(2,1)}, bf16[1024,256]{1,0:T(8,128)(2,1)}, u32[]{:S(2)}, u32[]{:S(2)}) collective-permute-start(bf16[1024,256]{1,0:T(8,128)(2,1)} %collective-permute-done.8.rest_3_), channel_id=1, source_target_pairs={{0,1},{1,0},{2,3},{3,2},{4,5},{5,4},{6,7},{7,6},{8,9},{9,8},{10,11... | collective-permute-start | bytes 1572872 | tf_op jit(solution)/shard_map/ppermute | solution.py:71
  51.8 4.4 %copy-start.5 = (s32[16]{0:T(128)S(1)}, s32[16]{0:T(128)}, u32[]{:S(2)}) copy-start(s32[16]{0:T(128)} %get-tuple-element.39) | copy-start | bytes 196
  51.8 5.0 %collective-permute-start.15 = (bf16[1024,256]{1,0:T(8,128)(2,1)}, bf16[1024,256]{1,0:T(8,128)(2,1)}, u32[]{:S(2)}, u32[]{:S(2)}) collective-permute-start(bf16[1024,256]{1,0:T(8,128)(2,1)} %collective-permute-done.9.rest_4_), channel_id=1, source_target_pairs={{0,1},{1,0},{2,3},{3,2},{4,5},{5,4},{6,7},{7,6},{8,9},{9,8},{10,11... | collective-permute-start | bytes 1572872 | tf_op jit(solution)/shard_map/ppermute | solution.py:71
  54.0 1.0 copy-start.3
  54.9 1.8 %collective-permute-start.10 = (f32[256,256]{1,0:T(8,128)S(1)}, f32[256,256]{1,0:T(8,128)}, u32[]{:S(2)}, u32[]{:S(2)}) collective-permute-start(f32[256,256]{1,0:T(8,128)S(1)} %fusion.1.gram_a), channel_id=1, source_target_pairs={{0,1},{1,0},{2,3},{3,2},{4,5},{5,4},{6,7},{7,6},{8,9},{9,8},{10,11... | collective-permute-start | bytes 786440 | tf_op jit(solution)/shard_map/ppermute | solution.py:71
  56.7 1.2 copy-start.4
  71.8 37.9 %copy-start.1 = (bf16[16384,256]{1,0:T(8,128)(2,1)}, bf16[16384,256]{1,0:T(8,128)(2,1)S(1)}, u32[]{:S(2)}) copy-start(bf16[16384,256]{1,0:T(8,128)(2,1)S(1)} %get-tuple-element.26.tiles) | copy-start | bytes 25165828
  71.9 3.5 %collective-permute-start.16 = (f32[64,256]{1,0:T(8,128)S(1)}, f32[64,256]{1,0:T(8,128)S(1)}, u32[]{:S(2)}, u32[]{:S(2)}) collective-permute-start(f32[64,256]{1,0:T(8,128)S(1)} %get-tuple-element.25), channel_id=1, source_target_pairs={{0,32},{32,0},{64,96},{96,64},{128,160},{160,128},{192,224},{224,1... | collective-permute-start | bytes 196616 | tf_op jit(solution)/shard_map/ppermute | solution.py:42
  75.4 5.8 %collective-permute-start.17 = (f32[64,256]{1,0:T(8,128)S(1)}, f32[64,256]{1,0:T(8,128)S(1)}, u32[]{:S(2)}, u32[]{:S(2)}) collective-permute-start(f32[64,256]{1,0:T(8,128)S(1)} %add.134), channel_id=1, source_target_pairs={{0,64},{32,96},{64,128},{96,160},{128,192},{160,224},{192,0},{224,... | collective-permute-start | bytes 196616 | tf_op jit(solution)/shard_map/ppermute | solution.py:42
  76.5 7.9 %collective-permute-start.18 = (f32[64,256]{1,0:T(8,128)S(1)}, f32[64,256]{1,0:T(8,128)S(1)}, u32[]{:S(2)}, u32[]{:S(2)}) collective-permute-start(f32[64,256]{1,0:T(8,128)S(1)} %add.134), channel_id=1, source_target_pairs={{0,128},{32,160},{64,192},{96,224},{128,0},{160,32},{192,64},{224,... | collective-permute-start | bytes 196616 | tf_op jit(solution)/shard_map/ppermute | solution.py:42
  79.1 5.3 %collective-permute-start.19 = (f32[64,256]{1,0:T(8,128)S(1)}, f32[64,256]{1,0:T(8,128)S(1)}, u32[]{:S(2)}, u32[]{:S(2)}) collective-permute-start(f32[64,256]{1,0:T(8,128)S(1)} %add.134), channel_id=1, source_target_pairs={{0,192},{32,224},{64,0},{96,32},{128,64},{160,96},{192,128},{224,1... | collective-permute-start | bytes 196616 | tf_op jit(solution)/shard_map/ppermute | solution.py:42
  84.4 4.3 %collective-permute-start.20 = (f32[64,256]{1,0:T(8,128)S(1)}, f32[64,256]{1,0:T(8,128)S(1)}, u32[]{:S(2)}, u32[]{:S(2)}) collective-permute-start(f32[64,256]{1,0:T(8,128)S(1)} %add_add_fusion.1.mine_ref), channel_id=1, source_target_pairs={{0,32},{32,0},{64,96},{96,64},{128,160},{160,128},{192,224},{224,1... | collective-permute-start | bytes 196616 | tf_op jit(solution)/shard_map/ppermute | solution.py:42
  93.4 3.1 %collective-permute-start.21 = (f32[64,256]{1,0:T(8,128)S(1)}, f32[64,256]{1,0:T(8,128)S(1)}, u32[]{:S(2)}, u32[]{:S(2)}) collective-permute-start(f32[64,256]{1,0:T(8,128)S(1)} %get-tuple-element.28), channel_id=1, source_target_pairs={{0,32},{32,0},{64,96},{96,64},{128,160},{160,128},{192,224},{224,1... | collective-permute-start | bytes 196616 | tf_op jit(solution)/shard_map/ppermute | solution.py:42
  96.5 6.9 %collective-permute-start.22 = (f32[64,256]{1,0:T(8,128)S(1)}, f32[64,256]{1,0:T(8,128)S(1)}, u32[]{:S(2)}, u32[]{:S(2)}) collective-permute-start(f32[64,256]{1,0:T(8,128)S(1)} %add.138), channel_id=1, source_target_pairs={{0,64},{32,96},{64,128},{96,160},{128,192},{160,224},{192,0},{224,... | collective-permute-start | bytes 196616 | tf_op jit(solution)/shard_map/ppermute | solution.py:42
  99.0 7.0 %collective-permute-start.23 = (f32[64,256]{1,0:T(8,128)S(1)}, f32[64,256]{1,0:T(8,128)S(1)}, u32[]{:S(2)}, u32[]{:S(2)}) collective-permute-start(f32[64,256]{1,0:T(8,128)S(1)} %add.138), channel_id=1, source_target_pairs={{0,128},{32,160},{64,192},{96,224},{128,0},{160,32},{192,64},{224,... | collective-permute-start | bytes 196616 | tf_op jit(solution)/shard_map/ppermute | solution.py:42
  100.8 5.2 %collective-permute-start.24 = (f32[64,256]{1,0:T(8,128)S(1)}, f32[64,256]{1,0:T(8,128)S(1)}, u32[]{:S(2)}, u32[]{:S(2)}) collective-permute-start(f32[64,256]{1,0:T(8,128)S(1)} %add.138), channel_id=1, source_target_pairs={{0,192},{32,224},{64,0},{96,32},{128,64},{160,96},{192,128},{224,1... | collective-permute-start | bytes 196616 | tf_op jit(solution)/shard_map/ppermute | solution.py:42
  106.0 3.7 %collective-permute-start.25 = (f32[64,256]{1,0:T(8,128)S(1)}, f32[64,256]{1,0:T(8,128)S(1)}, u32[]{:S(2)}, u32[]{:S(2)}) collective-permute-start(f32[64,256]{1,0:T(8,128)S(1)} %add_add_fusion.mine_ref), channel_id=1, source_target_pairs={{0,32},{32,0},{64,96},{96,64},{128,160},{160,128},{192,224},{224,1... | collective-permute-start | bytes 196616 | tf_op jit(solution)/shard_map/ppermute | solution.py:42
  113.4 2.9 %collective-permute-start.26 = (f32[8,128]{1,0:T(8,128)S(1)}, f32[8,128]{1,0:T(8,128)S(1)}, u32[]{:S(2)}, u32[]{:S(2)}) collective-permute-start(f32[8,128]{1,0:T(8,128)S(1)} %get-tuple-element.30), channel_id=1, source_target_pairs={{0,32},{32,0},{64,96},{96,64},{128,160},{160,128},{192,224},{224,1... | collective-permute-start | bytes 12296 | tf_op jit(solution)/shard_map/ppermute | solution.py:42
  116.3 3.4 %collective-permute-start.27 = (f32[8,128]{1,0:T(8,128)S(1)}, f32[8,128]{1,0:T(8,128)S(1)}, u32[]{:S(2)}, u32[]{:S(2)}) collective-permute-start(f32[8,128]{1,0:T(8,128)S(1)} %add.142), channel_id=1, source_target_pairs={{0,64},{32,96},{64,0},{96,32},{128,192},{160,224},{192,128},{224,1... | collective-permute-start | bytes 12296 | tf_op jit(solution)/shard_map/ppermute | solution.py:42
  119.7 6.4 %collective-permute-start.28 = (f32[8,128]{1,0:T(8,128)S(1)}, f32[8,128]{1,0:T(8,128)S(1)}, u32[]{:S(2)}, u32[]{:S(2)}) collective-permute-start(f32[8,128]{1,0:T(8,128)S(1)} %add.143), channel_id=1, source_target_pairs={{0,128},{32,160},{64,192},{96,224},{128,0},{160,32},{192,64},{224,... | collective-permute-start | bytes 12296 | tf_op jit(solution)/shard_map/ppermute | solution.py:42
  126.0 3.4 %copy-start.2 = (bf16[16384,256]{1,0:T(8,128)(2,1)S(1)}, bf16[16384,256]{1,0:T(8,128)(2,1)}, u32[]{:S(2)}) copy-start(bf16[16384,256]{1,0:T(8,128)(2,1)} %copy-done.1) | copy-start | bytes 25165828
  157.0 14.4 %collective-permute-start.29 = (f32[1024,256]{1,0:T(8,128)S(1)}, f32[1024,256]{1,0:T(8,128)S(1)}, u32[]{:S(2)}, u32[]{:S(2)}) collective-permute-start(f32[1024,256]{1,0:T(8,128)S(1)} %shard_map.73), channel_id=1, source_target_pairs={{0,1},{1,0},{2,3},{3,2},{4,5},{5,4},{6,7},{7,6},{8,9},{9,8},{10,11... | collective-permute-start | bytes 3145736 | tf_op jit(solution)/shard_map/ppermute | solution.py:71
where the time goes:
time: 173 us
  starting transfers between devices  66.5 us (38%)
  waiting for transfers between devices  36.2 us (21%)
  Pallas kernels  26.6 us (15%)
  blocking collectives  23.8 us (14%)
  local copies, waits for them, and re-layouts  8.3 us (5%)
  matrix products  6.11 us (4%)
  other arithmetic  4.07 us (2%)
    ppermute x16, starting transfers between devices, line_permute(): return lax.ppermute(value, 'z', [(s, partner(s)) for s in range(NZ)])  36.8 us
    pallas_call x6, Pallas kernels, call(): pl.pallas_call(kernel, out_shape=outs, grid_spec=pltpu.PrefetchScalarGrid...  26.6 us
    all_to_all x1, blocking collectives, shards(): lax.all_to_all(send, ('x', 'y'), split_axis=0, concat_axis=0, tiled=True)  23.8 us
    ppermute x16, waiting for transfers between devices, line_permute(): return lax.ppermute(value, 'z', [(s, partner(s)) for s in range(NZ)])  20.6 us
    ppermute x7, starting transfers between devices, swap_cores(): return lax.ppermute(value, 'c', [(0, 1), (1, 0)])  19.8 us
    unnamed x12, local copies, waits for them, and re-layouts  6.61 us
    dot_general x5, matrix products, shards(): lax.dot_general(v, v, (((0,), (0,)), ((), ())), preferred_element_type=F32)  6.11 us
    ppermute x1, waiting for transfers between devices, shards(): up = lax.ppermute(near, EVERY, ring_pairs(1, 1))  5.89 us
  transfers between devices with their start and end apart: 30, of which 16 were waited for; matrix products, arithmetic and copies ran while one was open for 6% of the time, Pallas kernels for 0%

commit v1 on v0

v1 whole, which is shorter than its diff:
```python
import functools

import jax
import jax.numpy as jnp
from jax import lax
from jax.experimental import pallas as pl
from jax.experimental.pallas import tpu as pltpu
from jax.sharding import Mesh, PartitionSpec as P

TILE = 128
RANK = 256
USERS = 16
SLOTS = 8
NZ, NX, NY = 8, 4, 4
PLANE = NX * NY
LINE_USERS = NZ * USERS
PLANE_ITEMS = PLANE * TILE
PENALTY = 1.0
EVERY = ("z", "x", "y", "c")
BF, F32 = jnp.bfloat16, jnp.float32
HIGH = lax.Precision.HIGHEST
WIDE = SLOTS * TILE + RANK + 2 * TILE
EXTRA = 16
VMEM_LIMIT = 16 * 2**20
HALF = LINE_USERS // 2
BLOCKS, BLOCK_ROWS = 6, 1024
SEND_ROWS = 3 * LINE_USERS + EXTRA


def ring_pairs(distance, phase):
    pairs = []
    for z in range(NZ):
        for x in range(NX):
            for y in range(NY):
                for c in range(2):
                    along_y = (c == 0) == (phase == 0)
                    x2 = x if along_y else (x + distance) % NX
                    y2 = (y + distance) % NY if along_y else y
                    pairs.append((((z * NX + x) * NY + y) * 2 + c, ((z * NX + x2) * NY + y2) * 2 + c))
    return pairs


def line_permute(value, partner):
    return lax.ppermute(value, "z", [(s, partner(s)) for s in range(NZ)])


def line_sum(keep, give):
    mine = keep + line_permute(give, lambda s: s ^ 1)
    others = [line_permute(mine, lambda s: (s + k) % NZ) for k in (2, 4, 6)]
    total = mine + others[0] + others[1] + others[2]
    return total, line_permute(total, lambda s: s ^ 1)


def split_halves(place_ref, part, keep_out, give_out):
    side = lax.rem(place_ref[0], 2)
    keep_out[...] = part[pl.ds(pl.multiple_of(side * HALF, HALF), HALF), :]
    give_out[...] = part[pl.ds(pl.multiple_of((1 - side) * HALF, HALF), HALF), :]


def join_halves(place_ref, mine_ref, other_ref, part):
    side = lax.rem(place_ref[0], 2)
    part[pl.ds(pl.multiple_of(side * HALF, HALF), HALF), :] = mine_ref[...]
    part[pl.ds(pl.multiple_of((1 - side) * HALF, HALF), HALF), :] = other_ref[...]


def swap_cores(value):
    return lax.ppermute(value, "c", [(0, 1), (1, 0)])


def against(vectors, block):
    return lax.dot_general(vectors, block, (((1,), (1,)), ((), ())), preferred_element_type=F32)


def tiles_of(row_ref, table, s):
    return jnp.concatenate(
        [
            table[pl.ds(pl.multiple_of(row_ref[s * PLANE + j] * TILE, TILE), TILE), :]
            for j in range(PLANE)
        ],
        axis=0,
    )


def weights_kernel(place_ref, held_ref, got_ref, weights_out, start_out, asked_out, lanes_out, wide):
    z = place_ref[0]
    for s in range(NZ):
        gap = lax.bitwise_xor(z, s)
        pair = lax.div(gap, 2)
        place = jnp.where(pair == 3, 1, jnp.where(pair == 0, 0, pair + 1))
        near = lax.bitwise_and(gap, 1) == 0

        def pay(start, stop):
            held = held_ref[place, :, start:stop].astype(F32)
            return jnp.where(near, held, got_ref[place, :, start:stop].astype(F32))

        rows = pl.ds(s * USERS, USERS)
        start_out[rows, :] = pay(SLOTS * TILE, SLOTS * TILE + RANK)
        slots = pay(SLOTS * TILE + RANK, SLOTS * TILE + RANK + TILE)
        asked = pay(WIDE - TILE, WIDE)
        asked_out[s : s + 1, :] = asked[:1]
        wide[rows, :] = asked
        owners = [jnp.broadcast_to(slots[:, k : k + 1], (USERS, TILE)) for k in range(SLOTS)]
        values = [pay(k * TILE, (k + 1) * TILE) for k in range(SLOTS)]
        for j in range(PLANE):
            owner = (z * PLANE + j).astype(F32)
            total = jnp.zeros((USERS, TILE), F32)
            for k in range(SLOTS):
                total = jnp.where(owners[k] == owner, values[k], total)
            weights_out[rows, j * TILE : (j + 1) * TILE] = total.astype(BF)
    wide[...] = wide[...].T
    lanes_out[...] = wide[pl.ds(pl.multiple_of(z * PLANE, PLANE), PLANE), :]


def gram_of(block):
    return lax.dot_general(block, block, (((0,), (0,)), ((), ())), preferred_element_type=F32)


def near_kernel(near_a, near_b, after_ref, later_a, later_b, gram_out):
    later_a[...] = near_a[...]
    later_b[...] = near_b[...]
    gram_out[...] = gram_of(near_a[...]) + gram_of(near_b[...])


def rest_kernel(*refs):
    sources, (after_ref, table, sems) = refs[:6], refs[6:]
    copies = [
        pltpu.make_async_copy(
            sources[i], table.at[pl.ds(i * BLOCK_ROWS, BLOCK_ROWS)], sems.at[i]
        )
        for i in range(6)
    ]
    for copy in copies:
        copy.start()
    for copy in copies:
        copy.wait()


def gram_kernel(gram_ref, table, gram_out):
    gram = gram_ref[...]
    for i in range(table.shape[0] // BLOCK_ROWS):
        gram = gram + gram_of(table[i * BLOCK_ROWS : (i + 1) * BLOCK_ROWS, :])
    gram_out[...] = gram


def first_kernel(row_ref, place_ref, start_ref, weights_ref, gram_a, gram_b, *rest):
    sources = rest[:BLOCKS]
    keep_out, give_out, gram_out, table, part, sems = rest[BLOCKS:]
    copies, row = [], 0
    for i, source in enumerate(sources):
        to = table.at[pl.ds(row, source.shape[0])]
        copies.append(pltpu.make_async_copy(source, to, sems.at[i]))
        row += source.shape[0]
    for copy in copies:
        copy.start()
    for copy in copies:
        copy.wait()
    gram = gram_a[...] + gram_b[...]
    gram_out[...] = gram
    part[...] = -jnp.dot(start_ref[...], gram, precision=HIGH, preferred_element_type=F32)
    for s in range(NZ):
        rows = pl.ds(s * USERS, USERS)
        block = tiles_of(row_ref, table, s)
        weights = weights_ref[rows, :].astype(F32)
        confidence = jnp.where(weights > 0.0, 1.0 + weights, 0.0).astype(BF)
        scaled = (weights * against(start_ref[rows, :].astype(BF), block)).astype(BF)
        both = jnp.dot(
            jnp.concatenate([confidence, scaled], axis=0), block, preferred_element_type=F32
        )
        part[rows, :] += both[:USERS] - both[USERS:]
    split_halves(place_ref, part, keep_out, give_out)


def second_kernel(
    row_ref, place_ref, mine_ref, other_ref, start_ref, gram_ref, weights_ref, table,
    residual_out, keep_out, give_out, part,
):
    join_halves(place_ref, mine_ref, other_ref, residual_out)
    residual = residual_out[...] - PENALTY * start_ref[...]
    residual_out[...] = residual
    part[...] = jnp.dot(residual, gram_ref[...], precision=HIGH, preferred_element_type=F32)
    for s in range(NZ):
        rows = pl.ds(s * USERS, USERS)
        block = tiles_of(row_ref, table, s)
        weights = weights_ref[rows, :].astype(F32)
        scaled = (weights * against(residual_out[rows, :].astype(BF), block)).astype(BF)
        part[rows, :] += jnp.dot(scaled, block, preferred_element_type=F32)
    split_halves(place_ref, part, keep_out, give_out)


def third_kernel(
    row_ref, place_ref, mine_ref, other_ref, start_ref, residual_ref, gram_ref, weights_ref, table,
    value_out, direction_out, norm_out, curve_out, part, column,
):
    join_halves(place_ref, mine_ref, other_ref, part)
    direction = residual_ref[...]
    image = part[...] + PENALTY * direction
    norm_now = jnp.sum(direction * direction, axis=1, keepdims=True)
    step = norm_now / jnp.sum(direction * image, axis=1, keepdims=True)
    value_out[...] = start_ref[...] + step * direction
    residual = direction - step * image
    norm_next = jnp.sum(residual * residual, axis=1, keepdims=True)
    direction = residual + (norm_next / norm_now) * direction
    direction_out[...] = direction
    norm_out[...] = jnp.broadcast_to(norm_next, (LINE_USERS, TILE))
    image = jnp.dot(direction, gram_ref[...], precision=HIGH, preferred_element_type=F32)
    column[...] = jnp.broadcast_to(
        jnp.sum(direction * image, axis=1, keepdims=True), (LINE_USERS, TILE)
    )
    for s in range(NZ):
        rows = pl.ds(s * USERS, USERS)
        block = tiles_of(row_ref, table, s)
        weights = weights_ref[rows, :].astype(F32)
        fitted = against(direction_out[rows, :].astype(BF), block)
        scaled = (weights * fitted).astype(BF).astype(F32)
        column[rows, :] += jnp.broadcast_to(
            jnp.sum(scaled * fitted, axis=1, keepdims=True), (USERS, TILE)
        )
    curve_out[...] = column[...].T[:8, :]


def fourth_kernel(
    row_ref, place_ref, curve_ref, value_ref, direction_ref, norm_ref, weights_ref, asked_ref, table,
    solved_out, send_out, solved,
):
    z = place_ref[0]
    curve = jnp.broadcast_to(curve_ref[:1, :], (TILE, LINE_USERS)).T[:, :1]
    direction = direction_ref[...]
    curve = curve + PENALTY * jnp.sum(direction * direction, axis=1, keepdims=True)
    step = norm_ref[:, :1] / curve
    solved[...] = value_ref[...] + step * direction
    solved_out[...] = solved[pl.ds(pl.multiple_of(z * USERS, USERS), USERS), :]
    for j in range(PLANE):
        send_out[j, 3 * LINE_USERS :, :] = jnp.broadcast_to(
            asked_ref[j : j + 1, :], (EXTRA, TILE)
        ).astype(BF)
    for s in range(NZ):
        rows = pl.ds(s * USERS, USERS)
        block = tiles_of(row_ref, table, s)
        weights = weights_ref[rows, :].astype(F32)
        confidence = (1.0 + weights).astype(BF).astype(F32)
        rounded = solved[rows, :].astype(BF)
        coeffs = confidence - weights * against(rounded, block)
        coeffs = jnp.where(weights > 0.0, coeffs, 0.0).astype(BF)
        for j in range(PLANE):
            send_out[j, rows, :] = coeffs[:, j * TILE : (j + 1) * TILE]
            for part in range(2):
                to = pl.ds((1 + part) * LINE_USERS + s * USERS, USERS)
                send_out[j, to, :] = rounded[:, part * TILE : (part + 1) * TILE]


def owner_kernel(got_ref, out_ref, coeffs, rounded):
    for p in range(PLANE):
        users = slice(p * LINE_USERS, (p + 1) * LINE_USERS)
        coeffs[:, users] = got_ref[p, :LINE_USERS, :].astype(F32).T
        rounded[users, :TILE] = got_ref[p, LINE_USERS : 2 * LINE_USERS, :]
        rounded[users, TILE:] = got_ref[p, 2 * LINE_USERS : 3 * LINE_USERS, :]
    asked = jnp.concatenate(
        [got_ref[p, 3 * LINE_USERS :, :].astype(F32)[:1] for p in range(PLANE)], axis=1
    )
    for t in range(out_ref.shape[0] // TILE):
        picked = jnp.where(asked == float(t), coeffs[...], 0.0).astype(BF)
        out_ref[t * TILE : (t + 1) * TILE, :] = jnp.dot(
            picked, rounded[...], preferred_element_type=F32
        )


def call(kernel, outs, operands, spaces, out_spaces, scratch, prefetch=0):
    memory = {"v": pltpu.VMEM, "a": pl.ANY}
    return pl.pallas_call(
        kernel,
        out_shape=outs,
        grid_spec=pltpu.PrefetchScalarGridSpec(
            num_scalar_prefetch=prefetch,
            grid=(1,),
            in_specs=[spec(memory[m]) for m in spaces],
            out_specs=[spec(memory[m]) for m in out_spaces],
            scratch_shapes=scratch,
        ),
        compiler_params=pltpu.CompilerParams(vmem_limit_bytes=VMEM_LIMIT),
    )(*operands)


def spec(space):
    return pl.BlockSpec(memory_space=space)


def shards(item_factors, user_factors, strengths, requests, user_slots):
    z, x, y, c = (lax.axis_index(name) for name in EVERY)
    shape = jax.ShapeDtypeStruct
    pay = jnp.concatenate(
        [
            strengths,
            user_factors,
            jnp.pad(user_slots, ((0, 0), (0, TILE - SLOTS))).astype(BF),
            jnp.broadcast_to(requests, (USERS, TILE)).astype(BF),
        ],
        axis=1,
    )
    half_rows = item_factors.shape[0] // 2
    half = lax.dynamic_slice_in_dim(item_factors, c * half_rows, half_rows, 0)
    half, pay = lax.optimization_barrier((half, pay))
    near = [half] + [lax.ppermute(half, EVERY, ring_pairs(d, 0)) for d in (1, -1, 2)]
    near_a, near_b = jnp.concatenate(near[:2], axis=0), jnp.concatenate(near[2:], axis=0)

    def grow(value, k):
        return jnp.concatenate([value, line_permute(value, lambda s: s ^ k)], axis=0)

    first_two = grow(pay[None], 6)
    held = grow(first_two, 2)
    got = line_permute(held, lambda s: s ^ 1)
    block = shape((BLOCK_ROWS, RANK), BF)
    square = shape((RANK, RANK), F32)
    up_a = lax.ppermute(near_a, EVERY, ring_pairs(1, 1))
    down_b = lax.ppermute(near_b, EVERY, ring_pairs(-1, 1))
    near_a, near_b, gram = call(
        near_kernel, [block, block, square], [near_a, near_b, first_two], "vva", "vvv", []
    )
    up_b = lax.ppermute(near_b, EVERY, ring_pairs(1, 1))
    down_a = lax.ppermute(near_a, EVERY, ring_pairs(-1, 1))
    far_a = lax.ppermute(up_a, EVERY, ring_pairs(1, 1))
    far_b = lax.ppermute(down_b, EVERY, ring_pairs(-1, 1))
    [rest] = call(
        rest_kernel,
        [shape((6 * BLOCK_ROWS, RANK), BF)],
        [up_a, up_b, down_a, down_b, far_a, far_b, got],
        "a" * 7,
        "v",
        [pltpu.SemaphoreType.DMA((6,))],
    )
    [gram_a] = call(gram_kernel, [square], [gram, rest], "vv", "v", [])
    own = [near_a, near_b, rest]
    other = [swap_cores(v) for v in own]
    gram_b = swap_cores(gram_a)
    place = z[None].astype(jnp.int32)
    vectors = shape((LINE_USERS, RANK), F32)
    halves = shape((HALF, RANK), F32)
    weights, start, asked, asked_rows = call(
        weights_kernel,
        [
            shape((LINE_USERS, PLANE_ITEMS), BF),
            vectors,
            shape((NZ, TILE), F32),
            shape((PLANE, LINE_USERS), F32),
        ],
        [place, held, got],
        "vv",
        "vvvv",
        [pltpu.VMEM((LINE_USERS, TILE), F32)],
        prefetch=1,
    )
    asked = lax.dynamic_slice(asked, (0, z * PLANE), (NZ, PLANE))
    tile = jnp.maximum(asked.astype(jnp.int32), 0)
    part_of = tile // 4
    j = jnp.arange(PLANE, dtype=jnp.int32)[None, :]
    along_x = (j // NY - x) % NX
    along_y = (j % NY - y) % NY
    first = jnp.where(part_of == 0, along_y, along_x)
    second = jnp.where(part_of == 0, along_x, along_y)

    def slot(delta):
        return jnp.where(delta == 3, 1, jnp.where(delta == 0, 0, delta + 1))

    first, second = slot(first), slot(second)
    row = jnp.where(part_of == c, 0, 64) + second * 16 + first * 4 + tile % 4
    row = row.reshape(-1)
    part = pltpu.VMEM(vectors.shape, F32)
    keep, give, gram, table = call(
        first_kernel,
        [halves, halves, shape((RANK, RANK), F32), shape((16 * BLOCK_ROWS, RANK), BF)],
        [row, place, start, weights, gram_a, gram_b, *own, *other],
        "vvvv" + "a" * BLOCKS,
        "vvvv",
        [part, pltpu.SemaphoreType.DMA((BLOCKS,))],
        prefetch=2,
    )
    residual, keep, give = call(
        second_kernel,
        [vectors, halves, halves],
        [row, place, *line_sum(keep, give), start, gram, weights, table],
        "v" * 6,
        "vvv",
        [part],
        prefetch=2,
    )
    value, direction, norm, curve = call(
        third_kernel,
        [vectors, vectors, shape((LINE_USERS, TILE), F32), shape((8, LINE_USERS), F32)],
        [row, place, *line_sum(keep, give), start, residual, gram, weights, table],
        "v" * 7,
        "vvvv",
        [part, pltpu.VMEM((LINE_USERS, TILE), F32)],
        prefetch=2,
    )
    for k in (1, 2, 6):
        curve = curve + line_permute(curve, lambda s: s ^ k)
    solved, send = call(
        fourth_kernel,
        [shape((USERS, RANK), F32), shape((PLANE, SEND_ROWS, TILE), BF)],
        [row, place, curve, value, direction, norm, weights, asked_rows, table],
        "v" * 7,
        "vv",
        [part],
        prefetch=2,
    )
    got = lax.all_to_all(send, ("x", "y"), split_axis=0, concat_axis=0, tiled=True)
    [sums] = call(
        owner_kernel,
        [shape(item_factors.shape, F32)],
        [got],
        "v",
        "v",
        [
            pltpu.VMEM((TILE, PLANE * LINE_USERS), F32),
            pltpu.VMEM((PLANE * LINE_USERS, RANK), BF),
        ],
    )
    return solved, sums + swap_cores(sums)


def solution(mesh):
    cut = Mesh(mesh.devices.reshape(NZ, NX, NY, 2), EVERY)
    every, owner = P(EVERY, None), P(("z", "x", "y"), None)
    return jax.shard_map(
        shards,
        mesh=cut,
        in_specs=(owner, every, every, every, every),
        out_specs=(every, owner),
        check_vma=False,
    )
```

time: 173 us -> 160 us (0.925)
  local copies, waits for them, and re-layouts: 8.3 us -> 1.24 us
  waiting for transfers between devices: 36.2 us -> 42.9 us
  matrix products: 6.11 us -> 0 us
  blocking collectives: 23.8 us -> 21.1 us
  starting transfers between devices: 66.5 us -> 63.9 us
    ppermute x16, waiting for transfers between devices: 20.6 us -> 29.5 us  [line_permute(): return lax.ppermute(value, 'z', [(s, partner(s)) for s in range(NZ)])]
    ppermute x16, starting transfers between devices: 36.8 us -> 30.5 us  [line_permute(): return lax.ppermute(value, 'z', [(s, partner(s)) for s in range(NZ)])]
    dot_general x5 -> x0, matrix products: 6.11 us -> none  [shards(): lax.dot_general(v, v, (((0,), (0,)), ((), ())), preferred_element_type=F32)]
    unnamed x12 -> x8, local copies, waits for them, and re-layouts: 6.61 us -> 1 us
    ppermute x4 -> x6, starting transfers between devices: 4.79 us -> 9.8 us  [the longest x1 2.81 us: shards(): down_b = lax.ppermute(near_b, EVERY, ring_pairs(-1, 1))]
    ppermute x4 -> x6, waiting for transfers between devices: 8.93 us -> 4.83 us  [the longest x1 4.82 us: shards(): far_a = lax.ppermute(up_a, EVERY, ring_pairs(1, 1))]
    all_to_all x1, blocking collectives: 23.8 us -> 21.1 us  [shards(): lax.all_to_all(send, ('x', 'y'), split_axis=0, concat_axis=0, tiled=True)]
    ppermute x7 -> x5, waiting for transfers between devices: 2.58 us -> 3.85 us  [swap_cores(): return lax.ppermute(value, 'c', [(0, 1), (1, 0)])]
  transfers between devices with their start and end apart: 30 -> 30, of which waited for: 16 -> 20; matrix products, arithmetic and copies ran while one was open for 6% -> 0% of each run, Pallas kernels for 0% -> 3%
where the time goes in v1:
time: 160 us
  starting transfers between devices  63.9 us (40%)
  waiting for transfers between devices  42.9 us (27%)
  Pallas kernels  26.5 us (17%)
  blocking collectives  21.1 us (13%)
  other arithmetic  3.5 us (2%)
    ppermute x16, starting transfers between devices, line_permute(): return lax.ppermute(value, 'z', [(s, partner(s)) for s in range(NZ)])  30.5 us
    ppermute x16, waiting for transfers between devices, line_permute(): return lax.ppermute(value, 'z', [(s, partner(s)) for s in range(NZ)])  29.5 us
    pallas_call x9, Pallas kernels, call(): pl.pallas_call(kernel, out_shape=outs, grid_spec=pltpu.PrefetchScalarGrid...  26.5 us
    all_to_all x1, blocking collectives, shards(): lax.all_to_all(send, ('x', 'y'), split_axis=0, concat_axis=0, tiled=True)  21.1 us
    ppermute x5, starting transfers between devices, swap_cores(): return lax.ppermute(value, 'c', [(0, 1), (1, 0)])  18.6 us
    ppermute x3, starting transfers between devices, shards(): lax.ppermute(half, EVERY, ring_pairs(d, 0))  5.12 us
    ppermute x1, waiting for transfers between devices, shards(): far_a = lax.ppermute(up_a, EVERY, ring_pairs(1, 1))  4.82 us
    ppermute x3, waiting for transfers between devices, shards(): lax.ppermute(half, EVERY, ring_pairs(d, 0))  4.68 us
  transfers between devices with their start and end apart: 30, of which 20 were waited for; matrix products, arithmetic and copies ran while one was open for 0% of the time, Pallas kernels for 3%

profile of v1, /device:TPU:1, one launch (start us, length us, event | category | flops | bytes accessed | tf_op | source)
XLA Modules:
  0.0 160.0 jit_solution(10659967591973910331)
XLA Ops:
  3.0 2.1 %collective-permute-start.3 = (bf16[512,256]{1,0:T(8,128)(2,1)S(1)}, bf16[512,256]{1,0:T(8,128)(2,1)S(1)}, u32[]{:S(2)}, u32[]{:S(2)}) collective-permute-start(bf16[512,256]{1,0:T(8,128)(2,1)S(1)} %constant_dynamic-slice_fusion), channel_id=1, source_target_pairs={{0,2},{1,9},{2,4},{3,11},{4,6},{5,13},{6,0},{7,15},{8,10},{9,17},{... | collective-permute-start | bytes 786440 | tf_op jit(solution)/shard_map/ppermute | solution.py:302
  5.1 1.4 collective-permute-start.4
  6.5 1.6 %collective-permute-start.5 = (bf16[512,256]{1,0:T(8,128)(2,1)S(1)}, bf16[512,256]{1,0:T(8,128)(2,1)S(1)}, u32[]{:S(2)}, u32[]{:S(2)}) collective-permute-start(bf16[512,256]{1,0:T(8,128)(2,1)S(1)} %constant_dynamic-slice_fusion), channel_id=1, source_target_pairs={{0,4},{1,17},{2,6},{3,19},{4,0},{5,21},{6,2},{7,23},{8,12},{9,25},... | collective-permute-start | bytes 786440 | tf_op jit(solution)/shard_map/ppermute | solution.py:302
  8.1 2.0 %collective-permute-done.3 = bf16[512,256]{1,0:T(8,128)(2,1)S(1)} collective-permute-done((bf16[512,256]{1,0:T(8,128)(2,1)S(1)}, bf16[512,256]{1,0:T(8,128)(2,1)S(1)}, u32[]{:S(2)}, u32[]{:S(2)}) %collective-permute-start.3) | collective-permute-done | bytes 262176 | tf_op jit(solution)/shard_map/ppermute | solution.py:302
  10.1 1.6 collective-permute-start.6
  11.7 2.7 %collective-permute-done.5 = bf16[512,256]{1,0:T(8,128)(2,1)S(1)} collective-permute-done((bf16[512,256]{1,0:T(8,128)(2,1)S(1)}, bf16[512,256]{1,0:T(8,128)(2,1)S(1)}, u32[]{:S(2)}, u32[]{:S(2)}) %collective-permute-start.5) | collective-permute-done | bytes 262176 | tf_op jit(solution)/shard_map/ppermute | solution.py:302
  14.4 2.8 %collective-permute-start.9 = (bf16[1024,256]{1,0:T(8,128)(2,1)S(1)}, bf16[1024,256]{1,0:T(8,128)(2,1)S(1)}, u32[]{:S(2)}, u32[]{:S(2)}) collective-permute-start(bf16[1024,256]{1,0:T(8,128)(2,1)S(1)} %constant_dynamic-update-slice_fusion.2.near_b), channel_id=1, source_target_pairs={{0,24},{1,7},{2,26},{3,1},{4,28},{5,3},{6,30},{7,5},{8,0},{9,15},{... | collective-permute-start | bytes 1572872 | tf_op jit(solution)/shard_map/ppermute | solution.py:314
  17.2 6.0 %collective-permute-start = (bf16[1,16,1536]{2,1,0:T(8,128)(2,1)S(1)}, bf16[1,16,1536]{2,1,0:T(8,128)(2,1)S(1)}, u32[]{:S(2)}, u32[]{:S(2)}) collective-permute-start(bf16[1,16,1536]{2,1,0:T(8,128)(2,1)S(1)} %bitcast.4), channel_id=1, source_target_pairs={{0,192},{32,224},{64,128},{96,160},{128,64},{160,96},{192,0},{224,... | collective-permute-start | bytes 147464 | tf_op jit(solution)/shard_map/ppermute | solution.py:44
  23.3 1.6 collective-permute-done
  24.8 1.2 collective-permute-start.1
  26.6 2.7 %collective-permute-start.8 = (bf16[1024,256]{1,0:T(8,128)(2,1)S(1)}, bf16[1024,256]{1,0:T(8,128)(2,1)S(1)}, u32[]{:S(2)}, u32[]{:S(2)}) collective-permute-start(bf16[1024,256]{1,0:T(8,128)(2,1)S(1)} %get-tuple-element.31.rest_0_), channel_id=1, source_target_pairs={{0,24},{1,7},{2,26},{3,1},{4,28},{5,3},{6,30},{7,5},{8,0},{9,15},{... | collective-permute-start | bytes 1572872 | tf_op jit(solution)/shard_map/ppermute | solution.py:319
  29.3 2.7 %collective-permute-start.11 = (bf16[1024,256]{1,0:T(8,128)(2,1)S(1)}, bf16[1024,256]{1,0:T(8,128)(2,1)S(1)}, u32[]{:S(2)}, u32[]{:S(2)}) collective-permute-start(bf16[1024,256]{1,0:T(8,128)(2,1)S(1)} %collective-permute-done.9.refs_3_), channel_id=1, source_target_pairs={{0,24},{1,7},{2,26},{3,1},{4,28},{5,3},{6,30},{7,5},{8,0},{9,15},{... | collective-permute-start | bytes 1572872 | tf_op jit(solution)/shard_map/ppermute | solution.py:321
  32.0 1.1 collective-permute-start.2
  33.1 3.8 %collective-permute-done.2.got_ref.refs_6_ = bf16[4,16,1536]{2,1,0:T(8,128)(2,1)S(1)} collective-permute-done((bf16[4,16,1536]{2,1,0:T(8,128)(2,1)S(1)}, bf16[4,16,1536]{2,1,0:T(8,128)(2,1)S(1)}, u32[]{:S(2)}, u32[]{:S(2)}) %collective-permute-start.2) | collective-permute-done | bytes 196640 | tf_op jit(solution)/shard_map/ppermute | solution.py:44
  37.0 4.8 %collective-permute-done.10.refs_4_ = bf16[1024,256]{1,0:T(8,128)(2,1)S(1)} collective-permute-done((bf16[1024,256]{1,0:T(8,128)(2,1)S(1)}, bf16[1024,256]{1,0:T(8,128)(2,1)S(1)}, u32[]{:S(2)}, u32[]{:S(2)}) %collective-permute-start.10) | collective-permute-done | bytes 524320 | tf_op jit(solution)/shard_map/ppermute | solution.py:320
  41.8 1.9 %shard_map.70.table.rest_2_ = bf16[6144,256]{1,0:T(8,128)(2,1)} custom-call(bf16[1024,256]{1,0:T(8,128)(2,1)S(1)} %collective-permute-done.6.refs_0_, bf16[1024,256]{1,0:T(8,128)(2,1)S(1)} %collective-permute-done.7.refs_1_, bf16[1024,256]{1,0:T(8,128)(2,1)S(1)} %collective-permute-done.8.refs_2_, bf16[1024,256]{1,0:T(8,128)(2,1)S(1)} %collective-permute-done.9.refs_3_, ...), custom_call_target="tpu_custom_call" | custom-call | tf_op jit(solution)/shard_map/pallas_call | solution.py:269
  43.7 5.0 %collective-permute-start.15 = (bf16[6144,256]{1,0:T(8,128)(2,1)}, bf16[6144,256]{1,0:T(8,128)(2,1)}, u32[]{:S(2)}, u32[]{:S(2)}) collective-permute-start(bf16[6144,256]{1,0:T(8,128)(2,1)} %shard_map.70.table.rest_2_), channel_id=1, source_target_pairs={{0,1},{1,0},{2,3},{3,2},{4,5},{5,4},{6,7},{7,6},{8,9},{9,8},{10,11... | collective-permute-start | bytes 9437192 | tf_op jit(solution)/shard_map/ppermute | solution.py:67
  49.2 0.9 copy-done.2
  50.1 2.9 %shard_map.71.gram_a = f32[256,256]{1,0:T(8,128)S(1)} custom-call(f32[256,256]{1,0:T(8,128)S(1)} %copy-done.2, bf16[6144,256]{1,0:T(8,128)(2,1)} %shard_map.70.table.rest_2_), custom_call_target="tpu_custom_call" | custom-call | tf_op jit(solution)/shard_map/pallas_call | solution.py:269
  54.4 0.9 collective-permute-done.14.rest_4_
  56.0 8.3 %shard_map.72 = (f32[64,256]{1,0:T(8,128)S(1)}, f32[64,256]{1,0:T(8,128)S(1)}, f32[256,256]{1,0:T(8,128)S(1)}, bf16[16384,256]{1,0:T(8,128)(2,1)S(1)}) custom-call(s32[128]{0:T(128)S(1)} %reshape.98.row_ref, s32[1]{0:T(128)} %bitcast.place_ref, f32[128,256]{1,0:T(8,128)S(1)} %get-tuple-element.26.start_ref, ...), custom_call_target="tpu_custom_call" | custom-call | tf_op jit(solution)/shard_map/pallas_call | solution.py:269
  64.3 1.4 collective-permute-start.16
  65.6 1.8 %collective-permute-done.16 = f32[64,256]{1,0:T(8,128)S(1)} collective-permute-done((f32[64,256]{1,0:T(8,128)S(1)}, f32[64,256]{1,0:T(8,128)S(1)}, u32[]{:S(2)}, u32[]{:S(2)}) %collective-permute-start.16) | collective-permute-done | bytes 65568 | tf_op jit(solution)/shard_map/ppermute | solution.py:44
  67.5 4.2 %collective-permute-start.19 = (f32[64,256]{1,0:T(8,128)S(1)}, f32[64,256]{1,0:T(8,128)S(1)}, u32[]{:S(2)}, u32[]{:S(2)}) collective-permute-start(f32[64,256]{1,0:T(8,128)S(1)} %add.112), channel_id=1, source_target_pairs={{0,192},{32,224},{64,0},{96,32},{128,64},{160,96},{192,128},{224,1... | collective-permute-start | bytes 196616 | tf_op jit(solution)/shard_map/ppermute | solution.py:44
  72.5 2.3 %collective-permute-start.17 = (f32[64,256]{1,0:T(8,128)S(1)}, f32[64,256]{1,0:T(8,128)S(1)}, u32[]{:S(2)}, u32[]{:S(2)}) collective-permute-start(f32[64,256]{1,0:T(8,128)S(1)} %add.112), channel_id=1, source_target_pairs={{0,64},{32,96},{64,128},{96,160},{128,192},{160,224},{192,0},{224,... | collective-permute-start | bytes 196616 | tf_op jit(solution)/shard_map/ppermute | solution.py:44
  74.7 4.1 %collective-permute-done.18 = f32[64,256]{1,0:T(8,128)S(1)} collective-permute-done((f32[64,256]{1,0:T(8,128)S(1)}, f32[64,256]{1,0:T(8,128)S(1)}, u32[]{:S(2)}, u32[]{:S(2)}) %collective-permute-start.18) | collective-permute-done | bytes 65568 | tf_op jit(solution)/shard_map/ppermute | solution.py:44
  79.5 2.9 %collective-permute-done.20.other_ref = f32[64,256]{1,0:T(8,128)S(1)} collective-permute-done((f32[64,256]{1,0:T(8,128)S(1)}, f32[64,256]{1,0:T(8,128)S(1)}, u32[]{:S(2)}, u32[]{:S(2)}) %collective-permute-start.20) | collective-permute-done | bytes 65568 | tf_op jit(solution)/shard_map/ppermute | solution.py:44
  82.5 4.2 %shard_map.73 = (f32[128,256]{1,0:T(8,128)S(1)}, f32[64,256]{1,0:T(8,128)S(1)}, f32[64,256]{1,0:T(8,128)S(1)}) custom-call(s32[128]{0:T(128)S(1)} %reshape.98.row_ref, s32[1]{0:T(128)} %bitcast.place_ref, f32[64,256]{1,0:T(8,128)S(1)} %add_add_fusion.1.mine_ref, f32[64,256]{1,0:T(8,128)S(1)} %collective-permute-done.20.other_ref, ...), custom_call_target="tpu_custom_call" | custom-call | tf_op jit(solution)/shard_map/pallas_call | solution.py:269
  87.2 2.6 %collective-permute-done.21 = f32[64,256]{1,0:T(8,128)S(1)} collective-permute-done((f32[64,256]{1,0:T(8,128)S(1)}, f32[64,256]{1,0:T(8,128)S(1)}, u32[]{:S(2)}, u32[]{:S(2)}) %collective-permute-start.21) | collective-permute-done | bytes 65568 | tf_op jit(solution)/shard_map/ppermute | solution.py:44
  89.8 1.6 collective-permute-start.24
  91.4 3.1 %collective-permute-start.23 = (f32[64,256]{1,0:T(8,128)S(1)}, f32[64,256]{1,0:T(8,128)S(1)}, u32[]{:S(2)}, u32[]{:S(2)}) collective-permute-start(f32[64,256]{1,0:T(8,128)S(1)} %add.116), channel_id=1, source_target_pairs={{0,128},{32,160},{64,192},{96,224},{128,0},{160,32},{192,64},{224,... | collective-permute-start | bytes 196616 | tf_op jit(solution)/shard_map/ppermute | solution.py:44
  94.5 2.2 %collective-permute-start.22 = (f32[64,256]{1,0:T(8,128)S(1)}, f32[64,256]{1,0:T(8,128)S(1)}, u32[]{:S(2)}, u32[]{:S(2)}) collective-permute-start(f32[64,256]{1,0:T(8,128)S(1)} %add.116), channel_id=1, source_target_pairs={{0,64},{32,96},{64,128},{96,160},{128,192},{160,224},{192,0},{224,... | collective-permute-start | bytes 196616 | tf_op jit(solution)/shard_map/ppermute | solution.py:44
  96.7 1.8 %collective-permute-done.23 = f32[64,256]{1,0:T(8,128)S(1)} collective-permute-done((f32[64,256]{1,0:T(8,128)S(1)}, f32[64,256]{1,0:T(8,128)S(1)}, u32[]{:S(2)}, u32[]{:S(2)}) %collective-permute-start.23) | collective-permute-done | bytes 65568 | tf_op jit(solution)/shard_map/ppermute | solution.py:44
  98.5 1.8 %collective-permute-done.22 = f32[64,256]{1,0:T(8,128)S(1)} collective-permute-done((f32[64,256]{1,0:T(8,128)S(1)}, f32[64,256]{1,0:T(8,128)S(1)}, u32[]{:S(2)}, u32[]{:S(2)}) %collective-permute-start.22) | collective-permute-done | bytes 65568 | tf_op jit(solution)/shard_map/ppermute | solution.py:44
  100.3 1.1 collective-permute-start.25
  101.4 2.5 %collective-permute-done.25.other_ref = f32[64,256]{1,0:T(8,128)S(1)} collective-permute-done((f32[64,256]{1,0:T(8,128)S(1)}, f32[64,256]{1,0:T(8,128)S(1)}, u32[]{:S(2)}, u32[]{:S(2)}) %collective-permute-start.25) | collective-permute-done | bytes 65568 | tf_op jit(solution)/shard_map/ppermute | solution.py:44
  103.8 3.2 %shard_map.74 = (f32[128,256]{1,0:T(8,128)S(1)}, f32[128,256]{1,0:T(8,128)S(1)}, f32[128,128]{1,0:T(8,128)S(1)}, f32[8,128]{1,0:T(8,128)S(1)}) custom-call(s32[128]{0:T(128)S(1)} %reshape.98.row_ref, s32[1]{0:T(128)} %bitcast.place_ref, f32[64,256]{1,0:T(8,128)S(1)} %add_add_fusion.mine_ref, f32[64,256]{1,0:T(8,128)S(1)} %collective-permute-done.25.other_ref, ...), custom_call_target="tpu_custom_call" | custom-call | tf_op jit(solution)/shard_map/pallas_call | solution.py:269
  107.1 2.1 %collective-permute-start.26 = (f32[8,128]{1,0:T(8,128)S(1)}, f32[8,128]{1,0:T(8,128)S(1)}, u32[]{:S(2)}, u32[]{:S(2)}) collective-permute-start(f32[8,128]{1,0:T(8,128)S(1)} %get-tuple-element.39), channel_id=1, source_target_pairs={{0,32},{32,0},{64,96},{96,64},{128,160},{160,128},{192,224},{224,1... | collective-permute-start | bytes 12296 | tf_op jit(solution)/shard_map/ppermute | solution.py:44
  109.2 1.0 collective-permute-done.26
  110.9 2.7 %collective-permute-done.27 = f32[8,128]{1,0:T(8,128)S(1)} collective-permute-done((f32[8,128]{1,0:T(8,128)S(1)}, f32[8,128]{1,0:T(8,128)S(1)}, u32[]{:S(2)}, u32[]{:S(2)}) %collective-permute-start.27) | collective-permute-done | bytes 4128 | tf_op jit(solution)/shard_map/ppermute | solution.py:44
  113.5 2.0 %collective-permute-start.28 = (f32[8,128]{1,0:T(8,128)S(1)}, f32[8,128]{1,0:T(8,128)S(1)}, u32[]{:S(2)}, u32[]{:S(2)}) collective-permute-start(f32[8,128]{1,0:T(8,128)S(1)} %add.121), channel_id=1, source_target_pairs={{0,192},{32,224},{64,128},{96,160},{128,64},{160,96},{192,0},{224,... | collective-permute-start | bytes 12296 | tf_op jit(solution)/shard_map/ppermute | solution.py:44
  115.6 2.5 %collective-permute-done.28 = f32[8,128]{1,0:T(8,128)S(1)} collective-permute-done((f32[8,128]{1,0:T(8,128)S(1)}, f32[8,128]{1,0:T(8,128)S(1)}, u32[]{:S(2)}, u32[]{:S(2)}) %collective-permute-start.28) | collective-permute-done | bytes 4128 | tf_op jit(solution)/shard_map/ppermute | solution.py:44
  118.1 3.3 %shard_map.75 = (f32[16,256]{1,0:T(8,128)}, bf16[16,400,128]{2,1,0:T(8,128)(2,1)S(1)}) custom-call(s32[128]{0:T(128)S(1)} %reshape.98.row_ref, s32[1]{0:T(128)} %bitcast.place_ref, f32[8,128]{1,0:T(8,128)S(1)} %add.122.curve_ref, f32[128,256]{1,0:T(8,128)S(1)} %get-tuple-element.40.value_ref, f32[128,256]{1,0:T(8,128)S(1)} %get-tuple-element.41.direction_ref, ...), custom_call_target="tpu_custom_call" | custom-call | tf_op jit(solution)/shard_map/pallas_call | solution.py:269
  121.4 21.1 %all_to_all.5.got_ref = bf16[16,400,128]{2,1,0:T(8,128)(2,1)S(1)} all-to-all(bf16[16,400,128]{2,1,0:T(8,128)(2,1)S(1)} %get-tuple-element.45), channel_id=1, replica_groups=mesh['z'=8,'x'=4,'y'=4,'c'=2] {'x','y'}, dimensions={0} | all-to-all | bytes 3276800 | tf_op jit(solution)/shard_map/all_to_all | solution.py:405
  142.6 1.3 shard_map.76
  143.9 12.7 %collective-permute-start.29 = (f32[1024,256]{1,0:T(8,128)S(1)}, f32[1024,256]{1,0:T(8,128)S(1)}, u32[]{:S(2)}, u32[]{:S(2)}) collective-permute-start(f32[1024,256]{1,0:T(8,128)S(1)} %shard_map.76), channel_id=1, source_target_pairs={{0,1},{1,0},{2,3},{3,2},{4,5},{5,4},{6,7},{7,6},{8,9},{9,8},{10,11... | collective-permute-start | bytes 3145736 | tf_op jit(solution)/shard_map/ppermute | solution.py:67
  156.6 2.3 %collective-permute-done.29 = f32[1024,256]{1,0:T(8,128)S(1)} collective-permute-done((f32[1024,256]{1,0:T(8,128)S(1)}, f32[1024,256]{1,0:T(8,128)S(1)}, u32[]{:S(2)}, u32[]{:S(2)}) %collective-permute-start.29) | collective-permute-done | bytes 1048608 | tf_op jit(solution)/shard_map/ppermute | solution.py:67
  158.9 1.1 add.123
  (51 shorter events, 8.3 us)
Async XLA Ops:
  0.6 1.5 copy-start
  3.0 7.1 %collective-permute-start.3 = (bf16[512,256]{1,0:T(8,128)(2,1)S(1)}, bf16[512,256]{1,0:T(8,128)(2,1)S(1)}, u32[]{:S(2)}, u32[]{:S(2)}) collective-permute-start(bf16[512,256]{1,0:T(8,128)(2,1)S(1)} %constant_dynamic-slice_fusion), channel_id=1, source_target_pairs={{0,2},{1,9},{2,4},{3,11},{4,6},{5,13},{6,0},{7,15},{8,10},{9,17},{... | collective-permute-start | bytes 786440 | tf_op jit(solution)/shard_map/ppermute | solution.py:302
  5.1 6.6 %collective-permute-start.4 = (bf16[512,256]{1,0:T(8,128)(2,1)S(1)}, bf16[512,256]{1,0:T(8,128)(2,1)S(1)}, u32[]{:S(2)}, u32[]{:S(2)}) collective-permute-start(bf16[512,256]{1,0:T(8,128)(2,1)S(1)} %constant_dynamic-slice_fusion), channel_id=1, source_target_pairs={{0,6},{1,25},{2,0},{3,27},{4,2},{5,29},{6,4},{7,31},{8,14},{9,1},{... | collective-permute-start | bytes 786440 | tf_op jit(solution)/shard_map/ppermute | solution.py:302
  6.5 8.0 %collective-permute-start.5 = (bf16[512,256]{1,0:T(8,128)(2,1)S(1)}, bf16[512,256]{1,0:T(8,128)(2,1)S(1)}, u32[]{:S(2)}, u32[]{:S(2)}) collective-permute-start(bf16[512,256]{1,0:T(8,128)(2,1)S(1)} %constant_dynamic-slice_fusion), channel_id=1, source_target_pairs={{0,4},{1,17},{2,6},{3,19},{4,0},{5,21},{6,2},{7,23},{8,12},{9,25},... | collective-permute-start | bytes 786440 | tf_op jit(solution)/shard_map/ppermute | solution.py:302
  10.1 19.2 %collective-permute-start.6 = (bf16[1024,256]{1,0:T(8,128)(2,1)S(1)}, bf16[1024,256]{1,0:T(8,128)(2,1)S(1)}, u32[]{:S(2)}, u32[]{:S(2)}) collective-permute-start(bf16[1024,256]{1,0:T(8,128)(2,1)S(1)} %constant_dynamic-update-slice_fusion.near_a), channel_id=1, source_target_pairs={{0,8},{1,3},{2,10},{3,5},{4,12},{5,7},{6,14},{7,1},{8,16},{9,11},{... | collective-permute-start | bytes 1572872 | tf_op jit(solution)/shard_map/ppermute | solution.py:313
  14.4 14.9 %collective-permute-start.9 = (bf16[1024,256]{1,0:T(8,128)(2,1)S(1)}, bf16[1024,256]{1,0:T(8,128)(2,1)S(1)}, u32[]{:S(2)}, u32[]{:S(2)}) collective-permute-start(bf16[1024,256]{1,0:T(8,128)(2,1)S(1)} %constant_dynamic-update-slice_fusion.2.near_b), channel_id=1, source_target_pairs={{0,24},{1,7},{2,26},{3,1},{4,28},{5,3},{6,30},{7,5},{8,0},{9,15},{... | collective-permute-start | bytes 1572872 | tf_op jit(solution)/shard_map/ppermute | solution.py:314
  17.2 7.6 %collective-permute-start = (bf16[1,16,1536]{2,1,0:T(8,128)(2,1)S(1)}, bf16[1,16,1536]{2,1,0:T(8,128)(2,1)S(1)}, u32[]{:S(2)}, u32[]{:S(2)}) collective-permute-start(bf16[1,16,1536]{2,1,0:T(8,128)(2,1)S(1)} %bitcast.4), channel_id=1, source_target_pairs={{0,192},{32,224},{64,128},{96,160},{128,64},{160,96},{192,0},{224,... | collective-permute-start | bytes 147464 | tf_op jit(solution)/shard_map/ppermute | solution.py:44
  24.8 7.2 %collective-permute-start.1 = (bf16[2,16,1536]{2,1,0:T(8,128)(2,1)S(1)}, bf16[2,16,1536]{2,1,0:T(8,128)(2,1)S(1)}, u32[]{:S(2)}, u32[]{:S(2)}) collective-permute-start(bf16[2,16,1536]{2,1,0:T(8,128)(2,1)S(1)} %pad_maximum_fusion.1.after_ref), channel_id=1, source_target_pairs={{0,64},{32,96},{64,0},{96,32},{128,192},{160,224},{192,128},{224,1... | collective-permute-start | bytes 294920 | tf_op jit(solution)/shard_map/ppermute | solution.py:44
  26.5 17.2 %copy-start.1 = (f32[256,256]{1,0:T(8,128)}, f32[256,256]{1,0:T(8,128)S(1)}, u32[]{:S(2)}) copy-start(f32[256,256]{1,0:T(8,128)S(1)} %get-tuple-element.29.gram_ref) | copy-start | bytes 786436
  26.5 10.4 %collective-permute-start.7 = (bf16[1024,256]{1,0:T(8,128)(2,1)S(1)}, bf16[1024,256]{1,0:T(8,128)(2,1)S(1)}, u32[]{:S(2)}, u32[]{:S(2)}) collective-permute-start(bf16[1024,256]{1,0:T(8,128)(2,1)S(1)} %get-tuple-element.30.rest_1_), channel_id=1, source_target_pairs={{0,8},{1,3},{2,10},{3,5},{4,12},{5,7},{6,14},{7,1},{8,16},{9,11},{... | collective-permute-start | bytes 1572872 | tf_op jit(solution)/shard_map/ppermute | solution.py:318
  26.6 10.3 %collective-permute-start.8 = (bf16[1024,256]{1,0:T(8,128)(2,1)S(1)}, bf16[1024,256]{1,0:T(8,128)(2,1)S(1)}, u32[]{:S(2)}, u32[]{:S(2)}) collective-permute-start(bf16[1024,256]{1,0:T(8,128)(2,1)S(1)} %get-tuple-element.31.rest_0_), channel_id=1, source_target_pairs={{0,24},{1,7},{2,26},{3,1},{4,28},{5,3},{6,30},{7,5},{8,0},{9,15},{... | collective-permute-start | bytes 1572872 | tf_op jit(solution)/shard_map/ppermute | solution.py:319
  29.3 12.5 %collective-permute-start.10 = (bf16[1024,256]{1,0:T(8,128)(2,1)S(1)}, bf16[1024,256]{1,0:T(8,128)(2,1)S(1)}, u32[]{:S(2)}, u32[]{:S(2)}) collective-permute-start(bf16[1024,256]{1,0:T(8,128)(2,1)S(1)} %collective-permute-done.6.refs_0_), channel_id=1, source_target_pairs={{0,8},{1,3},{2,10},{3,5},{4,12},{5,7},{6,14},{7,1},{8,16},{9,11},{... | collective-permute-start | bytes 1572872 | tf_op jit(solution)/shard_map/ppermute | solution.py:320
  29.3 12.5 %collective-permute-start.11 = (bf16[1024,256]{1,0:T(8,128)(2,1)S(1)}, bf16[1024,256]{1,0:T(8,128)(2,1)S(1)}, u32[]{:S(2)}, u32[]{:S(2)}) collective-permute-start(bf16[1024,256]{1,0:T(8,128)(2,1)S(1)} %collective-permute-done.9.refs_3_), channel_id=1, source_target_pairs={{0,24},{1,7},{2,26},{3,1},{4,28},{5,3},{6,30},{7,5},{8,0},{9,15},{... | collective-permute-start | bytes 1572872 | tf_op jit(solution)/shard_map/ppermute | solution.py:321
  32.0 4.9 %collective-permute-start.2 = (bf16[4,16,1536]{2,1,0:T(8,128)(2,1)S(1)}, bf16[4,16,1536]{2,1,0:T(8,128)(2,1)S(1)}, u32[]{:S(2)}, u32[]{:S(2)}) collective-permute-start(bf16[4,16,1536]{2,1,0:T(8,128)(2,1)S(1)} %pad_maximum_fusion.held_ref), channel_id=1, source_target_pairs={{0,32},{32,0},{64,96},{96,64},{128,160},{160,128},{192,224},{224,1... | collective-permute-start | bytes 589832 | tf_op jit(solution)/shard_map/ppermute | solution.py:44
  43.7 12.3 %collective-permute-start.15 = (bf16[6144,256]{1,0:T(8,128)(2,1)}, bf16[6144,256]{1,0:T(8,128)(2,1)}, u32[]{:S(2)}, u32[]{:S(2)}) collective-permute-start(bf16[6144,256]{1,0:T(8,128)(2,1)} %shard_map.70.table.rest_2_), channel_id=1, source_target_pairs={{0,1},{1,0},{2,3},{3,2},{4,5},{5,4},{6,7},{7,6},{8,9},{9,8},{10,11... | collective-permute-start | bytes 9437192 | tf_op jit(solution)/shard_map/ppermute | solution.py:67
  48.7 6.7 %collective-permute-start.14 = (bf16[1024,256]{1,0:T(8,128)(2,1)S(1)}, bf16[1024,256]{1,0:T(8,128)(2,1)S(1)}, u32[]{:S(2)}, u32[]{:S(2)}) collective-permute-start(bf16[1024,256]{1,0:T(8,128)(2,1)S(1)} %get-tuple-element.30.rest_1_), channel_id=1, source_target_pairs={{0,1},{1,0},{2,3},{3,2},{4,5},{5,4},{6,7},{7,6},{8,9},{9,8},{10,11... | collective-permute-start | bytes 1572872 | tf_op jit(solution)/shard_map/ppermute | solution.py:67
  48.8 6.7 %collective-permute-start.13 = (bf16[1024,256]{1,0:T(8,128)(2,1)S(1)}, bf16[1024,256]{1,0:T(8,128)(2,1)}, u32[]{:S(2)}, u32[]{:S(2)}) collective-permute-start(bf16[1024,256]{1,0:T(8,128)(2,1)S(1)} %get-tuple-element.31.rest_0_), channel_id=1, source_target_pairs={{0,1},{1,0},{2,3},{3,2},{4,5},{5,4},{6,7},{7,6},{8,9},{9,8},{10,11... | collective-permute-start | bytes 1572872 | tf_op jit(solution)/shard_map/ppermute | solution.py:67
  49.2 0.9 copy-start.2
  53.0 2.9 %collective-permute-start.12 = (f32[256,256]{1,0:T(8,128)S(1)}, f32[256,256]{1,0:T(8,128)}, u32[]{:S(2)}, u32[]{:S(2)}) collective-permute-start(f32[256,256]{1,0:T(8,128)S(1)} %shard_map.71.gram_a), channel_id=1, source_target_pairs={{0,1},{1,0},{2,3},{3,2},{4,5},{5,4},{6,7},{7,6},{8,9},{9,8},{10,11... | collective-permute-start | bytes 786440 | tf_op jit(solution)/shard_map/ppermute | solution.py:67
  64.3 3.2 %collective-permute-start.16 = (f32[64,256]{1,0:T(8,128)S(1)}, f32[64,256]{1,0:T(8,128)S(1)}, u32[]{:S(2)}, u32[]{:S(2)}) collective-permute-start(f32[64,256]{1,0:T(8,128)S(1)} %get-tuple-element.33), channel_id=1, source_target_pairs={{0,32},{32,0},{64,96},{96,64},{128,160},{160,128},{192,224},{224,1... | collective-permute-start | bytes 196616 | tf_op jit(solution)/shard_map/ppermute | solution.py:44
  67.5 7.2 %collective-permute-start.19 = (f32[64,256]{1,0:T(8,128)S(1)}, f32[64,256]{1,0:T(8,128)S(1)}, u32[]{:S(2)}, u32[]{:S(2)}) collective-permute-start(f32[64,256]{1,0:T(8,128)S(1)} %add.112), channel_id=1, source_target_pairs={{0,192},{32,224},{64,0},{96,32},{128,64},{160,96},{192,128},{224,1... | collective-permute-start | bytes 196616 | tf_op jit(solution)/shard_map/ppermute | solution.py:44
  71.7 7.1 %collective-permute-start.18 = (f32[64,256]{1,0:T(8,128)S(1)}, f32[64,256]{1,0:T(8,128)S(1)}, u32[]{:S(2)}, u32[]{:S(2)}) collective-permute-start(f32[64,256]{1,0:T(8,128)S(1)} %add.112), channel_id=1, source_target_pairs={{0,128},{32,160},{64,192},{96,224},{128,0},{160,32},{192,64},{224,... | collective-permute-start | bytes 196616 | tf_op jit(solution)/shard_map/ppermute | solution.py:44
  72.5 6.8 %collective-permute-start.17 = (f32[64,256]{1,0:T(8,128)S(1)}, f32[64,256]{1,0:T(8,128)S(1)}, u32[]{:S(2)}, u32[]{:S(2)}) collective-permute-start(f32[64,256]{1,0:T(8,128)S(1)} %add.112), channel_id=1, source_target_pairs={{0,64},{32,96},{64,128},{96,160},{128,192},{160,224},{192,0},{224,... | collective-permute-start | bytes 196616 | tf_op jit(solution)/shard_map/ppermute | solution.py:44
  79.3 3.2 %collective-permute-start.20 = (f32[64,256]{1,0:T(8,128)S(1)}, f32[64,256]{1,0:T(8,128)S(1)}, u32[]{:S(2)}, u32[]{:S(2)}) collective-permute-start(f32[64,256]{1,0:T(8,128)S(1)} %add_add_fusion.1.mine_ref), channel_id=1, source_target_pairs={{0,32},{32,0},{64,96},{96,64},{128,160},{160,128},{192,224},{224,1... | collective-permute-start | bytes 196616 | tf_op jit(solution)/shard_map/ppermute | solution.py:44
  86.7 3.1 %collective-permute-start.21 = (f32[64,256]{1,0:T(8,128)S(1)}, f32[64,256]{1,0:T(8,128)S(1)}, u32[]{:S(2)}, u32[]{:S(2)}) collective-permute-start(f32[64,256]{1,0:T(8,128)S(1)} %get-tuple-element.37), channel_id=1, source_target_pairs={{0,32},{32,0},{64,96},{96,64},{128,160},{160,128},{192,224},{224,1... | collective-permute-start | bytes 196616 | tf_op jit(solution)/shard_map/ppermute | solution.py:44
  89.8 6.9 %collective-permute-start.24 = (f32[64,256]{1,0:T(8,128)S(1)}, f32[64,256]{1,0:T(8,128)S(1)}, u32[]{:S(2)}, u32[]{:S(2)}) collective-permute-start(f32[64,256]{1,0:T(8,128)S(1)} %add.116), channel_id=1, source_target_pairs={{0,192},{32,224},{64,0},{96,32},{128,64},{160,96},{192,128},{224,1... | collective-permute-start | bytes 196616 | tf_op jit(solution)/shard_map/ppermute | solution.py:44
  91.4 7.1 %collective-permute-start.23 = (f32[64,256]{1,0:T(8,128)S(1)}, f32[64,256]{1,0:T(8,128)S(1)}, u32[]{:S(2)}, u32[]{:S(2)}) collective-permute-start(f32[64,256]{1,0:T(8,128)S(1)} %add.116), channel_id=1, source_target_pairs={{0,128},{32,160},{64,192},{96,224},{128,0},{160,32},{192,64},{224,... | collective-permute-start | bytes 196616 | tf_op jit(solution)/shard_map/ppermute | solution.py:44
  94.5 5.7 %collective-permute-start.22 = (f32[64,256]{1,0:T(8,128)S(1)}, f32[64,256]{1,0:T(8,128)S(1)}, u32[]{:S(2)}, u32[]{:S(2)}) collective-permute-start(f32[64,256]{1,0:T(8,128)S(1)} %add.116), channel_id=1, source_target_pairs={{0,64},{32,96},{64,128},{96,160},{128,192},{160,224},{192,0},{224,... | collective-permute-start | bytes 196616 | tf_op jit(solution)/shard_map/ppermute | solution.py:44
  100.3 3.5 %collective-permute-start.25 = (f32[64,256]{1,0:T(8,128)S(1)}, f32[64,256]{1,0:T(8,128)S(1)}, u32[]{:S(2)}, u32[]{:S(2)}) collective-permute-start(f32[64,256]{1,0:T(8,128)S(1)} %add_add_fusion.mine_ref), channel_id=1, source_target_pairs={{0,32},{32,0},{64,96},{96,64},{128,160},{160,128},{192,224},{224,1... | collective-permute-start | bytes 196616 | tf_op jit(solution)/shard_map/ppermute | solution.py:44
  107.1 3.1 %collective-permute-start.26 = (f32[8,128]{1,0:T(8,128)S(1)}, f32[8,128]{1,0:T(8,128)S(1)}, u32[]{:S(2)}, u32[]{:S(2)}) collective-permute-start(f32[8,128]{1,0:T(8,128)S(1)} %get-tuple-element.39), channel_id=1, source_target_pairs={{0,32},{32,0},{64,96},{96,64},{128,160},{160,128},{192,224},{224,1... | collective-permute-start | bytes 12296 | tf_op jit(solution)/shard_map/ppermute | solution.py:44
  110.2 3.4 %collective-permute-start.27 = (f32[8,128]{1,0:T(8,128)S(1)}, f32[8,128]{1,0:T(8,128)S(1)}, u32[]{:S(2)}, u32[]{:S(2)}) collective-permute-start(f32[8,128]{1,0:T(8,128)S(1)} %add.120), channel_id=1, source_target_pairs={{0,64},{32,96},{64,0},{96,32},{128,192},{160,224},{192,128},{224,1... | collective-permute-start | bytes 12296 | tf_op jit(solution)/shard_map/ppermute | solution.py:44
  113.5 4.6 %collective-permute-start.28 = (f32[8,128]{1,0:T(8,128)S(1)}, f32[8,128]{1,0:T(8,128)S(1)}, u32[]{:S(2)}, u32[]{:S(2)}) collective-permute-start(f32[8,128]{1,0:T(8,128)S(1)} %add.121), channel_id=1, source_target_pairs={{0,192},{32,224},{64,128},{96,160},{128,64},{160,96},{192,0},{224,... | collective-permute-start | bytes 12296 | tf_op jit(solution)/shard_map/ppermute | solution.py:44
  143.9 15.0 %collective-permute-start.29 = (f32[1024,256]{1,0:T(8,128)S(1)}, f32[1024,256]{1,0:T(8,128)S(1)}, u32[]{:S(2)}, u32[]{:S(2)}) collective-permute-start(f32[1024,256]{1,0:T(8,128)S(1)} %shard_map.76), channel_id=1, source_target_pairs={{0,1},{1,0},{2,3},{3,2},{4,5},{5,4},{6,7},{7,6},{8,9},{9,8},{10,11... | collective-permute-start | bytes 3145736 | tf_op jit(solution)/shard_map/ppermute | solution.py:67

commit v2 on v1

--- a/solution.py
+++ b/solution.py
@@ -152,11 +152,11 @@
         row += source.shape[0]
     for copy in copies:
         copy.start()
-    for copy in copies:
-        copy.wait()
     gram = gram_a[...] + gram_b[...]
     gram_out[...] = gram
     part[...] = -jnp.dot(start_ref[...], gram, precision=HIGH, preferred_element_type=F32)
+    for copy in copies:
+        copy.wait()
     for s in range(NZ):
         rows = pl.ds(s * USERS, USERS)
         block = tiles_of(row_ref, table, s)
@@ -298,7 +298,6 @@
     )
     half_rows = item_factors.shape[0] // 2
     half = lax.dynamic_slice_in_dim(item_factors, c * half_rows, half_rows, 0)
-    half, pay = lax.optimization_barrier((half, pay))
     near = [half] + [lax.ppermute(half, EVERY, ring_pairs(d, 0)) for d in (1, -1, 2)]
     near_a, near_b = jnp.concatenate(near[:2], axis=0), jnp.concatenate(near[2:], axis=0)
 

time: 160 us -> 160 us (level)
  waiting for transfers between devices: 42.9 us -> 40.3 us
  local copies, waits for them, and re-layouts: 1.24 us -> 2.91 us
    ppermute x3, waiting for transfers between devices: 4.68 us -> 2.66 us  [shards(): lax.ppermute(half, EVERY, ring_pairs(d, 0))]
    unnamed x8 -> x7, local copies, waits for them, and re-layouts: 1 us -> 2.7 us
  transfers between devices with their start and end apart: 30 -> 30, of which waited for: 20 -> 20; matrix products, arithmetic and copies ran while one was open for 0% -> 2% of each run, Pallas kernels for 3% -> 3%
where the time goes in v2:
time: 160 us
  starting transfers between devices  64.9 us (41%)
  waiting for transfers between devices  40.3 us (25%)
  Pallas kernels  26.4 us (16%)
  blocking collectives  21.1 us (13%)
  other arithmetic  3.47 us (2%)
  local copies, waits for them, and re-layouts  2.91 us (2%)
    ppermute x16, starting transfers between devices, line_permute(): return lax.ppermute(value, 'z', [(s, partner(s)) for s in range(NZ)])  31.1 us
    ppermute x16, waiting for transfers between devices, line_permute(): return lax.ppermute(value, 'z', [(s, partner(s)) for s in range(NZ)])  28.9 us
    pallas_call x9, Pallas kernels, call(): pl.pallas_call(kernel, out_shape=outs, grid_spec=pltpu.PrefetchScalarGrid...  26.4 us
    all_to_all x1, blocking collectives, shards(): lax.all_to_all(send, ('x', 'y'), split_axis=0, concat_axis=0, tiled=True)  21.1 us
    ppermute x5, starting transfers between devices, swap_cores(): return lax.ppermute(value, 'c', [(0, 1), (1, 0)])  18.7 us
    ppermute x3, starting transfers between devices, shards(): lax.ppermute(half, EVERY, ring_pairs(d, 0))  5.72 us
    ppermute x1, waiting for transfers between devices, shards(): far_a = lax.ppermute(up_a, EVERY, ring_pairs(1, 1))  4.85 us
    ppermute x5, waiting for transfers between devices, swap_cores(): return lax.ppermute(value, 'c', [(0, 1), (1, 0)])  3.85 us
  transfers between devices with their start and end apart: 30, of which 20 were waited for; matrix products, arithmetic and copies ran while one was open for 2% of the time, Pallas kernels for 3%

profile of v2, /device:TPU:1, one launch (start us, length us, event | category | flops | bytes accessed | tf_op | source)
XLA Modules:
  0.0 159.9 jit_solution(939493137020829027)
XLA Ops:
  0.6 1.0 copy-done
  1.7 2.1 %collective-permute-start.3 = (bf16[512,256]{1,0:T(8,128)(2,1)S(1)}, bf16[512,256]{1,0:T(8,128)(2,1)S(1)}, u32[]{:S(2)}, u32[]{:S(2)}) collective-permute-start(bf16[512,256]{1,0:T(8,128)(2,1)S(1)} %constant_dynamic-slice_fusion), channel_id=1, source_target_pairs={{0,2},{1,9},{2,4},{3,11},{4,6},{5,13},{6,0},{7,15},{8,10},{9,17},{... | collective-permute-start | bytes 786440 | tf_op jit(solution)/shard_map/ppermute | solution.py:301
  3.8 2.5 %collective-permute-start.5 = (bf16[512,256]{1,0:T(8,128)(2,1)S(1)}, bf16[512,256]{1,0:T(8,128)(2,1)S(1)}, u32[]{:S(2)}, u32[]{:S(2)}) collective-permute-start(bf16[512,256]{1,0:T(8,128)(2,1)S(1)} %constant_dynamic-slice_fusion), channel_id=1, source_target_pairs={{0,4},{1,17},{2,6},{3,19},{4,0},{5,21},{6,2},{7,23},{8,12},{9,25},... | collective-permute-start | bytes 786440 | tf_op jit(solution)/shard_map/ppermute | solution.py:301
  6.3 1.2 collective-permute-start.4
  8.9 1.5 collective-permute-start.6
  10.5 2.2 %collective-permute-done.4 = bf16[512,256]{1,0:T(8,128)(2,1)S(1)} collective-permute-done((bf16[512,256]{1,0:T(8,128)(2,1)S(1)}, bf16[512,256]{1,0:T(8,128)(2,1)S(1)}, u32[]{:S(2)}, u32[]{:S(2)}) %collective-permute-start.4) | collective-permute-done | bytes 262176 | tf_op jit(solution)/shard_map/ppermute | solution.py:301
  13.1 2.5 %collective-permute-start.9 = (bf16[1024,256]{1,0:T(8,128)(2,1)S(1)}, bf16[1024,256]{1,0:T(8,128)(2,1)S(1)}, u32[]{:S(2)}, u32[]{:S(2)}) collective-permute-start(bf16[1024,256]{1,0:T(8,128)(2,1)S(1)} %constant_dynamic-update-slice_fusion.near_b), channel_id=1, source_target_pairs={{0,24},{1,7},{2,26},{3,1},{4,28},{5,3},{6,30},{7,5},{8,0},{9,15},{... | collective-permute-start | bytes 1572872 | tf_op jit(solution)/shard_map/ppermute | solution.py:313
  16.5 6.1 %collective-permute-start = (bf16[1,16,1536]{2,1,0:T(8,128)(2,1)S(1)}, bf16[1,16,1536]{2,1,0:T(8,128)(2,1)S(1)}, u32[]{:S(2)}, u32[]{:S(2)}) collective-permute-start(bf16[1,16,1536]{2,1,0:T(8,128)(2,1)S(1)} %fusion.4), channel_id=1, source_target_pairs={{0,192},{32,224},{64,128},{96,160},{128,64},{160,96},{192,0},{224,... | collective-permute-start | bytes 147464 | tf_op jit(solution)/shard_map/ppermute | solution.py:44
  22.6 1.6 collective-permute-done
  24.1 1.2 collective-permute-start.1
  26.6 2.7 %collective-permute-start.8 = (bf16[1024,256]{1,0:T(8,128)(2,1)S(1)}, bf16[1024,256]{1,0:T(8,128)(2,1)S(1)}, u32[]{:S(2)}, u32[]{:S(2)}) collective-permute-start(bf16[1024,256]{1,0:T(8,128)(2,1)S(1)} %get-tuple-element.27.rest_0_), channel_id=1, source_target_pairs={{0,24},{1,7},{2,26},{3,1},{4,28},{5,3},{6,30},{7,5},{8,0},{9,15},{... | collective-permute-start | bytes 1572872 | tf_op jit(solution)/shard_map/ppermute | solution.py:318
  29.2 2.7 %collective-permute-start.11 = (bf16[1024,256]{1,0:T(8,128)(2,1)S(1)}, bf16[1024,256]{1,0:T(8,128)(2,1)S(1)}, u32[]{:S(2)}, u32[]{:S(2)}) collective-permute-start(bf16[1024,256]{1,0:T(8,128)(2,1)S(1)} %collective-permute-done.9.refs_3_), channel_id=1, source_target_pairs={{0,24},{1,7},{2,26},{3,1},{4,28},{5,3},{6,30},{7,5},{8,0},{9,15},{... | collective-permute-start | bytes 1572872 | tf_op jit(solution)/shard_map/ppermute | solution.py:320
  31.9 1.1 collective-permute-start.2
  33.0 3.8 %collective-permute-done.2.got_ref.refs_6_ = bf16[4,16,1536]{2,1,0:T(8,128)(2,1)S(1)} collective-permute-done((bf16[4,16,1536]{2,1,0:T(8,128)(2,1)S(1)}, bf16[4,16,1536]{2,1,0:T(8,128)(2,1)S(1)}, u32[]{:S(2)}, u32[]{:S(2)}) %collective-permute-start.2) | collective-permute-done | bytes 196640 | tf_op jit(solution)/shard_map/ppermute | solution.py:44
  36.8 4.9 %collective-permute-done.10.refs_4_ = bf16[1024,256]{1,0:T(8,128)(2,1)S(1)} collective-permute-done((bf16[1024,256]{1,0:T(8,128)(2,1)S(1)}, bf16[1024,256]{1,0:T(8,128)(2,1)S(1)}, u32[]{:S(2)}, u32[]{:S(2)}) %collective-permute-start.10) | collective-permute-done | bytes 524320 | tf_op jit(solution)/shard_map/ppermute | solution.py:319
  41.7 1.9 %shard_map.70.table.rest_2_ = bf16[6144,256]{1,0:T(8,128)(2,1)} custom-call(bf16[1024,256]{1,0:T(8,128)(2,1)S(1)} %collective-permute-done.6.refs_0_, bf16[1024,256]{1,0:T(8,128)(2,1)S(1)} %collective-permute-done.7.refs_1_, bf16[1024,256]{1,0:T(8,128)(2,1)S(1)} %collective-permute-done.8.refs_2_, bf16[1024,256]{1,0:T(8,128)(2,1)S(1)} %collective-permute-done.9.refs_3_, ...), custom_call_target="tpu_custom_call" | custom-call | tf_op jit(solution)/shard_map/pallas_call | solution.py:269
  43.6 5.4 %collective-permute-start.15 = (bf16[6144,256]{1,0:T(8,128)(2,1)}, bf16[6144,256]{1,0:T(8,128)(2,1)}, u32[]{:S(2)}, u32[]{:S(2)}) collective-permute-start(bf16[6144,256]{1,0:T(8,128)(2,1)} %shard_map.70.table.rest_2_), channel_id=1, source_target_pairs={{0,1},{1,0},{2,3},{3,2},{4,5},{5,4},{6,7},{7,6},{8,9},{9,8},{10,11... | collective-permute-start | bytes 9437192 | tf_op jit(solution)/shard_map/ppermute | solution.py:67
  49.5 0.9 copy-done.2
  50.4 2.9 %shard_map.71.gram_a = f32[256,256]{1,0:T(8,128)S(1)} custom-call(f32[256,256]{1,0:T(8,128)S(1)} %copy-done.2, bf16[6144,256]{1,0:T(8,128)(2,1)} %shard_map.70.table.rest_2_), custom_call_target="tpu_custom_call" | custom-call | tf_op jit(solution)/shard_map/pallas_call | solution.py:269
  56.3 8.2 %shard_map.72 = (f32[64,256]{1,0:T(8,128)S(1)}, f32[64,256]{1,0:T(8,128)S(1)}, f32[256,256]{1,0:T(8,128)S(1)}, bf16[16384,256]{1,0:T(8,128)(2,1)S(1)}) custom-call(s32[128]{0:T(128)S(1)} %reshape.98.row_ref, s32[1]{0:T(128)} %bitcast.place_ref, f32[128,256]{1,0:T(8,128)S(1)} %get-tuple-element.23.start_ref, ...), custom_call_target="tpu_custom_call" | custom-call | tf_op jit(solution)/shard_map/pallas_call | solution.py:269
  64.4 1.3 collective-permute-start.16
  65.7 1.9 %collective-permute-done.16 = f32[64,256]{1,0:T(8,128)S(1)} collective-permute-done((f32[64,256]{1,0:T(8,128)S(1)}, f32[64,256]{1,0:T(8,128)S(1)}, u32[]{:S(2)}, u32[]{:S(2)}) %collective-permute-start.16) | collective-permute-done | bytes 65568 | tf_op jit(solution)/shard_map/ppermute | solution.py:44
  67.7 4.4 %collective-permute-start.19 = (f32[64,256]{1,0:T(8,128)S(1)}, f32[64,256]{1,0:T(8,128)S(1)}, u32[]{:S(2)}, u32[]{:S(2)}) collective-permute-start(f32[64,256]{1,0:T(8,128)S(1)} %add.112), channel_id=1, source_target_pairs={{0,192},{32,224},{64,0},{96,32},{128,64},{160,96},{192,128},{224,1... | collective-permute-start | bytes 196616 | tf_op jit(solution)/shard_map/ppermute | solution.py:44
  72.6 2.3 %collective-permute-start.17 = (f32[64,256]{1,0:T(8,128)S(1)}, f32[64,256]{1,0:T(8,128)S(1)}, u32[]{:S(2)}, u32[]{:S(2)}) collective-permute-start(f32[64,256]{1,0:T(8,128)S(1)} %add.112), channel_id=1, source_target_pairs={{0,64},{32,96},{64,128},{96,160},{128,192},{160,224},{192,0},{224,... | collective-permute-start | bytes 196616 | tf_op jit(solution)/shard_map/ppermute | solution.py:44
  74.9 4.2 %collective-permute-done.18 = f32[64,256]{1,0:T(8,128)S(1)} collective-permute-done((f32[64,256]{1,0:T(8,128)S(1)}, f32[64,256]{1,0:T(8,128)S(1)}, u32[]{:S(2)}, u32[]{:S(2)}) %collective-permute-start.18) | collective-permute-done | bytes 65568 | tf_op jit(solution)/shard_map/ppermute | solution.py:44
  79.6 3.0 %collective-permute-done.20.other_ref = f32[64,256]{1,0:T(8,128)S(1)} collective-permute-done((f32[64,256]{1,0:T(8,128)S(1)}, f32[64,256]{1,0:T(8,128)S(1)}, u32[]{:S(2)}, u32[]{:S(2)}) %collective-permute-start.20) | collective-permute-done | bytes 65568 | tf_op jit(solution)/shard_map/ppermute | solution.py:44
  82.6 4.2 %shard_map.73 = (f32[128,256]{1,0:T(8,128)S(1)}, f32[64,256]{1,0:T(8,128)S(1)}, f32[64,256]{1,0:T(8,128)S(1)}) custom-call(s32[128]{0:T(128)S(1)} %reshape.98.row_ref, s32[1]{0:T(128)} %bitcast.place_ref, f32[64,256]{1,0:T(8,128)S(1)} %add_add_fusion.1.mine_ref, f32[64,256]{1,0:T(8,128)S(1)} %collective-permute-done.20.other_ref, ...), custom_call_target="tpu_custom_call" | custom-call | tf_op jit(solution)/shard_map/pallas_call | solution.py:269
  87.2 2.8 %collective-permute-done.21 = f32[64,256]{1,0:T(8,128)S(1)} collective-permute-done((f32[64,256]{1,0:T(8,128)S(1)}, f32[64,256]{1,0:T(8,128)S(1)}, u32[]{:S(2)}, u32[]{:S(2)}) %collective-permute-start.21) | collective-permute-done | bytes 65568 | tf_op jit(solution)/shard_map/ppermute | solution.py:44
  90.0 1.7 %collective-permute-start.24 = (f32[64,256]{1,0:T(8,128)S(1)}, f32[64,256]{1,0:T(8,128)S(1)}, u32[]{:S(2)}, u32[]{:S(2)}) collective-permute-start(f32[64,256]{1,0:T(8,128)S(1)} %add.116), channel_id=1, source_target_pairs={{0,192},{32,224},{64,0},{96,32},{128,64},{160,96},{192,128},{224,1... | collective-permute-start | bytes 196616 | tf_op jit(solution)/shard_map/ppermute | solution.py:44
  91.7 3.0 %collective-permute-start.23 = (f32[64,256]{1,0:T(8,128)S(1)}, f32[64,256]{1,0:T(8,128)S(1)}, u32[]{:S(2)}, u32[]{:S(2)}) collective-permute-start(f32[64,256]{1,0:T(8,128)S(1)} %add.116), channel_id=1, source_target_pairs={{0,128},{32,160},{64,192},{96,224},{128,0},{160,32},{192,64},{224,... | collective-permute-start | bytes 196616 | tf_op jit(solution)/shard_map/ppermute | solution.py:44
  94.7 2.2 %collective-permute-start.22 = (f32[64,256]{1,0:T(8,128)S(1)}, f32[64,256]{1,0:T(8,128)S(1)}, u32[]{:S(2)}, u32[]{:S(2)}) collective-permute-start(f32[64,256]{1,0:T(8,128)S(1)} %add.116), channel_id=1, source_target_pairs={{0,64},{32,96},{64,128},{96,160},{128,192},{160,224},{192,0},{224,... | collective-permute-start | bytes 196616 | tf_op jit(solution)/shard_map/ppermute | solution.py:44
  96.8 2.0 %collective-permute-done.23 = f32[64,256]{1,0:T(8,128)S(1)} collective-permute-done((f32[64,256]{1,0:T(8,128)S(1)}, f32[64,256]{1,0:T(8,128)S(1)}, u32[]{:S(2)}, u32[]{:S(2)}) %collective-permute-start.23) | collective-permute-done | bytes 65568 | tf_op jit(solution)/shard_map/ppermute | solution.py:44
  98.8 1.6 collective-permute-done.22
  100.4 1.6 collective-permute-start.25
  102.0 2.1 %collective-permute-done.25.other_ref = f32[64,256]{1,0:T(8,128)S(1)} collective-permute-done((f32[64,256]{1,0:T(8,128)S(1)}, f32[64,256]{1,0:T(8,128)S(1)}, u32[]{:S(2)}, u32[]{:S(2)}) %collective-permute-start.25) | collective-permute-done | bytes 65568 | tf_op jit(solution)/shard_map/ppermute | solution.py:44
  104.1 3.2 %shard_map.74 = (f32[128,256]{1,0:T(8,128)S(1)}, f32[128,256]{1,0:T(8,128)S(1)}, f32[128,128]{1,0:T(8,128)S(1)}, f32[8,128]{1,0:T(8,128)S(1)}) custom-call(s32[128]{0:T(128)S(1)} %reshape.98.row_ref, s32[1]{0:T(128)} %bitcast.place_ref, f32[64,256]{1,0:T(8,128)S(1)} %add_add_fusion.mine_ref, f32[64,256]{1,0:T(8,128)S(1)} %collective-permute-done.25.other_ref, ...), custom_call_target="tpu_custom_call" | custom-call | tf_op jit(solution)/shard_map/pallas_call | solution.py:269
  107.3 2.0 %collective-permute-start.26 = (f32[8,128]{1,0:T(8,128)S(1)}, f32[8,128]{1,0:T(8,128)S(1)}, u32[]{:S(2)}, u32[]{:S(2)}) collective-permute-start(f32[8,128]{1,0:T(8,128)S(1)} %get-tuple-element.35), channel_id=1, source_target_pairs={{0,32},{32,0},{64,96},{96,64},{128,160},{160,128},{192,224},{224,1... | collective-permute-start | bytes 12296 | tf_op jit(solution)/shard_map/ppermute | solution.py:44
  109.3 1.0 collective-permute-done.26
  110.3 1.0 collective-permute-start.27
  111.4 2.3 %collective-permute-done.27 = f32[8,128]{1,0:T(8,128)S(1)} collective-permute-done((f32[8,128]{1,0:T(8,128)S(1)}, f32[8,128]{1,0:T(8,128)S(1)}, u32[]{:S(2)}, u32[]{:S(2)}) %collective-permute-start.27) | collective-permute-done | bytes 4128 | tf_op jit(solution)/shard_map/ppermute | solution.py:44
  113.7 2.3 %collective-permute-start.28 = (f32[8,128]{1,0:T(8,128)S(1)}, f32[8,128]{1,0:T(8,128)S(1)}, u32[]{:S(2)}, u32[]{:S(2)}) collective-permute-start(f32[8,128]{1,0:T(8,128)S(1)} %add.121), channel_id=1, source_target_pairs={{0,192},{32,224},{64,128},{96,160},{128,64},{160,96},{192,0},{224,... | collective-permute-start | bytes 12296 | tf_op jit(solution)/shard_map/ppermute | solution.py:44
  116.0 2.3 %collective-permute-done.28 = f32[8,128]{1,0:T(8,128)S(1)} collective-permute-done((f32[8,128]{1,0:T(8,128)S(1)}, f32[8,128]{1,0:T(8,128)S(1)}, u32[]{:S(2)}, u32[]{:S(2)}) %collective-permute-start.28) | collective-permute-done | bytes 4128 | tf_op jit(solution)/shard_map/ppermute | solution.py:44
  118.3 3.3 %shard_map.75 = (f32[16,256]{1,0:T(8,128)}, bf16[16,400,128]{2,1,0:T(8,128)(2,1)S(1)}) custom-call(s32[128]{0:T(128)S(1)} %reshape.98.row_ref, s32[1]{0:T(128)} %bitcast.place_ref, f32[8,128]{1,0:T(8,128)S(1)} %add.122.curve_ref, f32[128,256]{1,0:T(8,128)S(1)} %get-tuple-element.36.value_ref, f32[128,256]{1,0:T(8,128)S(1)} %get-tuple-element.37.direction_ref, ...), custom_call_target="tpu_custom_call" | custom-call | tf_op jit(solution)/shard_map/pallas_call | solution.py:269
  121.6 21.1 %all_to_all.5.got_ref = bf16[16,400,128]{2,1,0:T(8,128)(2,1)S(1)} all-to-all(bf16[16,400,128]{2,1,0:T(8,128)(2,1)S(1)} %get-tuple-element.41), channel_id=1, replica_groups=mesh['z'=8,'x'=4,'y'=4,'c'=2] {'x','y'}, dimensions={0} | all-to-all | bytes 3276800 | tf_op jit(solution)/shard_map/all_to_all | solution.py:404
  142.7 1.3 shard_map.76
  144.0 12.5 %collective-permute-start.29 = (f32[1024,256]{1,0:T(8,128)S(1)}, f32[1024,256]{1,0:T(8,128)S(1)}, u32[]{:S(2)}, u32[]{:S(2)}) collective-permute-start(f32[1024,256]{1,0:T(8,128)S(1)} %shard_map.76), channel_id=1, source_target_pairs={{0,1},{1,0},{2,3},{3,2},{4,5},{5,4},{6,7},{7,6},{8,9},{9,8},{10,11... | collective-permute-start | bytes 3145736 | tf_op jit(solution)/shard_map/ppermute | solution.py:67
  156.5 2.3 %collective-permute-done.29 = f32[1024,256]{1,0:T(8,128)S(1)} collective-permute-done((f32[1024,256]{1,0:T(8,128)S(1)}, f32[1024,256]{1,0:T(8,128)S(1)}, u32[]{:S(2)}, u32[]{:S(2)}) %collective-permute-start.29) | collective-permute-done | bytes 1048608 | tf_op jit(solution)/shard_map/ppermute | solution.py:67
  158.8 1.1 add.123
  (50 shorter events, 9.0 us)
Async XLA Ops:
  0.6 1.0 copy-start
  1.7 7.2 %collective-permute-start.3 = (bf16[512,256]{1,0:T(8,128)(2,1)S(1)}, bf16[512,256]{1,0:T(8,128)(2,1)S(1)}, u32[]{:S(2)}, u32[]{:S(2)}) collective-permute-start(bf16[512,256]{1,0:T(8,128)(2,1)S(1)} %constant_dynamic-slice_fusion), channel_id=1, source_target_pairs={{0,2},{1,9},{2,4},{3,11},{4,6},{5,13},{6,0},{7,15},{8,10},{9,17},{... | collective-permute-start | bytes 786440 | tf_op jit(solution)/shard_map/ppermute | solution.py:301
  3.8 9.3 %collective-permute-start.5 = (bf16[512,256]{1,0:T(8,128)(2,1)S(1)}, bf16[512,256]{1,0:T(8,128)(2,1)S(1)}, u32[]{:S(2)}, u32[]{:S(2)}) collective-permute-start(bf16[512,256]{1,0:T(8,128)(2,1)S(1)} %constant_dynamic-slice_fusion), channel_id=1, source_target_pairs={{0,4},{1,17},{2,6},{3,19},{4,0},{5,21},{6,2},{7,23},{8,12},{9,25},... | collective-permute-start | bytes 786440 | tf_op jit(solution)/shard_map/ppermute | solution.py:301
  6.3 6.4 %collective-permute-start.4 = (bf16[512,256]{1,0:T(8,128)(2,1)S(1)}, bf16[512,256]{1,0:T(8,128)(2,1)S(1)}, u32[]{:S(2)}, u32[]{:S(2)}) collective-permute-start(bf16[512,256]{1,0:T(8,128)(2,1)S(1)} %constant_dynamic-slice_fusion), channel_id=1, source_target_pairs={{0,6},{1,25},{2,0},{3,27},{4,2},{5,29},{6,4},{7,31},{8,14},{9,1},{... | collective-permute-start | bytes 786440 | tf_op jit(solution)/shard_map/ppermute | solution.py:301
  8.9 20.3 %collective-permute-start.6 = (bf16[1024,256]{1,0:T(8,128)(2,1)S(1)}, bf16[1024,256]{1,0:T(8,128)(2,1)S(1)}, u32[]{:S(2)}, u32[]{:S(2)}) collective-permute-start(bf16[1024,256]{1,0:T(8,128)(2,1)S(1)} %pad_maximum_fusion.near_a), channel_id=1, source_target_pairs={{0,8},{1,3},{2,10},{3,5},{4,12},{5,7},{6,14},{7,1},{8,16},{9,11},{... | collective-permute-start | bytes 1572872 | tf_op jit(solution)/shard_map/ppermute | solution.py:312
  13.1 16.1 %collective-permute-start.9 = (bf16[1024,256]{1,0:T(8,128)(2,1)S(1)}, bf16[1024,256]{1,0:T(8,128)(2,1)S(1)}, u32[]{:S(2)}, u32[]{:S(2)}) collective-permute-start(bf16[1024,256]{1,0:T(8,128)(2,1)S(1)} %constant_dynamic-update-slice_fusion.near_b), channel_id=1, source_target_pairs={{0,24},{1,7},{2,26},{3,1},{4,28},{5,3},{6,30},{7,5},{8,0},{9,15},{... | collective-permute-start | bytes 1572872 | tf_op jit(solution)/shard_map/ppermute | solution.py:313
  16.5 7.7 %collective-permute-start = (bf16[1,16,1536]{2,1,0:T(8,128)(2,1)S(1)}, bf16[1,16,1536]{2,1,0:T(8,128)(2,1)S(1)}, u32[]{:S(2)}, u32[]{:S(2)}) collective-permute-start(bf16[1,16,1536]{2,1,0:T(8,128)(2,1)S(1)} %fusion.4), channel_id=1, source_target_pairs={{0,192},{32,224},{64,128},{96,160},{128,64},{160,96},{192,0},{224,... | collective-permute-start | bytes 147464 | tf_op jit(solution)/shard_map/ppermute | solution.py:44
  24.1 7.8 %collective-permute-start.1 = (bf16[2,16,1536]{2,1,0:T(8,128)(2,1)S(1)}, bf16[2,16,1536]{2,1,0:T(8,128)(2,1)S(1)}, u32[]{:S(2)}, u32[]{:S(2)}) collective-permute-start(bf16[2,16,1536]{2,1,0:T(8,128)(2,1)S(1)} %pad_maximum_fusion.2.after_ref), channel_id=1, source_target_pairs={{0,64},{32,96},{64,0},{96,32},{128,192},{160,224},{192,128},{224,1... | collective-permute-start | bytes 294920 | tf_op jit(solution)/shard_map/ppermute | solution.py:44
  25.8 0.7 copy-start.1
  26.5 10.3 %collective-permute-start.7 = (bf16[1024,256]{1,0:T(8,128)(2,1)S(1)}, bf16[1024,256]{1,0:T(8,128)(2,1)S(1)}, u32[]{:S(2)}, u32[]{:S(2)}) collective-permute-start(bf16[1024,256]{1,0:T(8,128)(2,1)S(1)} %get-tuple-element.26.rest_1_), channel_id=1, source_target_pairs={{0,8},{1,3},{2,10},{3,5},{4,12},{5,7},{6,14},{7,1},{8,16},{9,11},{... | collective-permute-start | bytes 1572872 | tf_op jit(solution)/shard_map/ppermute | solution.py:317
  26.6 10.3 %collective-permute-start.8 = (bf16[1024,256]{1,0:T(8,128)(2,1)S(1)}, bf16[1024,256]{1,0:T(8,128)(2,1)S(1)}, u32[]{:S(2)}, u32[]{:S(2)}) collective-permute-start(bf16[1024,256]{1,0:T(8,128)(2,1)S(1)} %get-tuple-element.27.rest_0_), channel_id=1, source_target_pairs={{0,24},{1,7},{2,26},{3,1},{4,28},{5,3},{6,30},{7,5},{8,0},{9,15},{... | collective-permute-start | bytes 1572872 | tf_op jit(solution)/shard_map/ppermute | solution.py:318
  29.2 12.5 %collective-permute-start.10 = (bf16[1024,256]{1,0:T(8,128)(2,1)S(1)}, bf16[1024,256]{1,0:T(8,128)(2,1)S(1)}, u32[]{:S(2)}, u32[]{:S(2)}) collective-permute-start(bf16[1024,256]{1,0:T(8,128)(2,1)S(1)} %collective-permute-done.6.refs_0_), channel_id=1, source_target_pairs={{0,8},{1,3},{2,10},{3,5},{4,12},{5,7},{6,14},{7,1},{8,16},{9,11},{... | collective-permute-start | bytes 1572872 | tf_op jit(solution)/shard_map/ppermute | solution.py:319
  29.2 12.5 %collective-permute-start.11 = (bf16[1024,256]{1,0:T(8,128)(2,1)S(1)}, bf16[1024,256]{1,0:T(8,128)(2,1)S(1)}, u32[]{:S(2)}, u32[]{:S(2)}) collective-permute-start(bf16[1024,256]{1,0:T(8,128)(2,1)S(1)} %collective-permute-done.9.refs_3_), channel_id=1, source_target_pairs={{0,24},{1,7},{2,26},{3,1},{4,28},{5,3},{6,30},{7,5},{8,0},{9,15},{... | collective-permute-start | bytes 1572872 | tf_op jit(solution)/shard_map/ppermute | solution.py:320
  31.9 4.9 %collective-permute-start.2 = (bf16[4,16,1536]{2,1,0:T(8,128)(2,1)S(1)}, bf16[4,16,1536]{2,1,0:T(8,128)(2,1)S(1)}, u32[]{:S(2)}, u32[]{:S(2)}) collective-permute-start(bf16[4,16,1536]{2,1,0:T(8,128)(2,1)S(1)} %pad_maximum_fusion.1.held_ref), channel_id=1, source_target_pairs={{0,32},{32,0},{64,96},{96,64},{128,160},{160,128},{192,224},{224,1... | collective-permute-start | bytes 589832 | tf_op jit(solution)/shard_map/ppermute | solution.py:44
  43.6 12.7 %collective-permute-start.15 = (bf16[6144,256]{1,0:T(8,128)(2,1)}, bf16[6144,256]{1,0:T(8,128)(2,1)}, u32[]{:S(2)}, u32[]{:S(2)}) collective-permute-start(bf16[6144,256]{1,0:T(8,128)(2,1)} %shard_map.70.table.rest_2_), channel_id=1, source_target_pairs={{0,1},{1,0},{2,3},{3,2},{4,5},{5,4},{6,7},{7,6},{8,9},{9,8},{10,11... | collective-permute-start | bytes 9437192 | tf_op jit(solution)/shard_map/ppermute | solution.py:67
  49.0 6.7 %collective-permute-start.14 = (bf16[1024,256]{1,0:T(8,128)(2,1)S(1)}, bf16[1024,256]{1,0:T(8,128)(2,1)S(1)}, u32[]{:S(2)}, u32[]{:S(2)}) collective-permute-start(bf16[1024,256]{1,0:T(8,128)(2,1)S(1)} %get-tuple-element.26.rest_1_), channel_id=1, source_target_pairs={{0,1},{1,0},{2,3},{3,2},{4,5},{5,4},{6,7},{7,6},{8,9},{9,8},{10,11... | collective-permute-start | bytes 1572872 | tf_op jit(solution)/shard_map/ppermute | solution.py:67
  49.1 6.7 %collective-permute-start.13 = (bf16[1024,256]{1,0:T(8,128)(2,1)S(1)}, bf16[1024,256]{1,0:T(8,128)(2,1)}, u32[]{:S(2)}, u32[]{:S(2)}) collective-permute-start(bf16[1024,256]{1,0:T(8,128)(2,1)S(1)} %get-tuple-element.27.rest_0_), channel_id=1, source_target_pairs={{0,1},{1,0},{2,3},{3,2},{4,5},{5,4},{6,7},{7,6},{8,9},{9,8},{10,11... | collective-permute-start | bytes 1572872 | tf_op jit(solution)/shard_map/ppermute | solution.py:67
  49.5 0.9 copy-start.2
  53.3 2.9 %collective-permute-start.12 = (f32[256,256]{1,0:T(8,128)S(1)}, f32[256,256]{1,0:T(8,128)}, u32[]{:S(2)}, u32[]{:S(2)}) collective-permute-start(f32[256,256]{1,0:T(8,128)S(1)} %shard_map.71.gram_a), channel_id=1, source_target_pairs={{0,1},{1,0},{2,3},{3,2},{4,5},{5,4},{6,7},{7,6},{8,9},{9,8},{10,11... | collective-permute-start | bytes 786440 | tf_op jit(solution)/shard_map/ppermute | solution.py:67
  64.4 3.2 %collective-permute-start.16 = (f32[64,256]{1,0:T(8,128)S(1)}, f32[64,256]{1,0:T(8,128)S(1)}, u32[]{:S(2)}, u32[]{:S(2)}) collective-permute-start(f32[64,256]{1,0:T(8,128)S(1)} %get-tuple-element.29), channel_id=1, source_target_pairs={{0,32},{32,0},{64,96},{96,64},{128,160},{160,128},{192,224},{224,1... | collective-permute-start | bytes 196616 | tf_op jit(solution)/shard_map/ppermute | solution.py:44
  67.7 7.2 %collective-permute-start.19 = (f32[64,256]{1,0:T(8,128)S(1)}, f32[64,256]{1,0:T(8,128)S(1)}, u32[]{:S(2)}, u32[]{:S(2)}) collective-permute-start(f32[64,256]{1,0:T(8,128)S(1)} %add.112), channel_id=1, source_target_pairs={{0,192},{32,224},{64,0},{96,32},{128,64},{160,96},{192,128},{224,1... | collective-permute-start | bytes 196616 | tf_op jit(solution)/shard_map/ppermute | solution.py:44
  72.0 7.0 %collective-permute-start.18 = (f32[64,256]{1,0:T(8,128)S(1)}, f32[64,256]{1,0:T(8,128)S(1)}, u32[]{:S(2)}, u32[]{:S(2)}) collective-permute-start(f32[64,256]{1,0:T(8,128)S(1)} %add.112), channel_id=1, source_target_pairs={{0,128},{32,160},{64,192},{96,224},{128,0},{160,32},{192,64},{224,... | collective-permute-start | bytes 196616 | tf_op jit(solution)/shard_map/ppermute | solution.py:44
  72.6 6.8 %collective-permute-start.17 = (f32[64,256]{1,0:T(8,128)S(1)}, f32[64,256]{1,0:T(8,128)S(1)}, u32[]{:S(2)}, u32[]{:S(2)}) collective-permute-start(f32[64,256]{1,0:T(8,128)S(1)} %add.112), channel_id=1, source_target_pairs={{0,64},{32,96},{64,128},{96,160},{128,192},{160,224},{192,0},{224,... | collective-permute-start | bytes 196616 | tf_op jit(solution)/shard_map/ppermute | solution.py:44
  79.4 3.2 %collective-permute-start.20 = (f32[64,256]{1,0:T(8,128)S(1)}, f32[64,256]{1,0:T(8,128)S(1)}, u32[]{:S(2)}, u32[]{:S(2)}) collective-permute-start(f32[64,256]{1,0:T(8,128)S(1)} %add_add_fusion.1.mine_ref), channel_id=1, source_target_pairs={{0,32},{32,0},{64,96},{96,64},{128,160},{160,128},{192,224},{224,1... | collective-permute-start | bytes 196616 | tf_op jit(solution)/shard_map/ppermute | solution.py:44
  86.9 3.1 %collective-permute-start.21 = (f32[64,256]{1,0:T(8,128)S(1)}, f32[64,256]{1,0:T(8,128)S(1)}, u32[]{:S(2)}, u32[]{:S(2)}) collective-permute-start(f32[64,256]{1,0:T(8,128)S(1)} %get-tuple-element.33), channel_id=1, source_target_pairs={{0,32},{32,0},{64,96},{96,64},{128,160},{160,128},{192,224},{224,1... | collective-permute-start | bytes 196616 | tf_op jit(solution)/shard_map/ppermute | solution.py:44
  90.0 6.8 %collective-permute-start.24 = (f32[64,256]{1,0:T(8,128)S(1)}, f32[64,256]{1,0:T(8,128)S(1)}, u32[]{:S(2)}, u32[]{:S(2)}) collective-permute-start(f32[64,256]{1,0:T(8,128)S(1)} %add.116), channel_id=1, source_target_pairs={{0,192},{32,224},{64,0},{96,32},{128,64},{160,96},{192,128},{224,1... | collective-permute-start | bytes 196616 | tf_op jit(solution)/shard_map/ppermute | solution.py:44
  91.7 7.1 %collective-permute-start.23 = (f32[64,256]{1,0:T(8,128)S(1)}, f32[64,256]{1,0:T(8,128)S(1)}, u32[]{:S(2)}, u32[]{:S(2)}) collective-permute-start(f32[64,256]{1,0:T(8,128)S(1)} %add.116), channel_id=1, source_target_pairs={{0,128},{32,160},{64,192},{96,224},{128,0},{160,32},{192,64},{224,... | collective-permute-start | bytes 196616 | tf_op jit(solution)/shard_map/ppermute | solution.py:44
  94.7 5.7 %collective-permute-start.22 = (f32[64,256]{1,0:T(8,128)S(1)}, f32[64,256]{1,0:T(8,128)S(1)}, u32[]{:S(2)}, u32[]{:S(2)}) collective-permute-start(f32[64,256]{1,0:T(8,128)S(1)} %add.116), channel_id=1, source_target_pairs={{0,64},{32,96},{64,128},{96,160},{128,192},{160,224},{192,0},{224,... | collective-permute-start | bytes 196616 | tf_op jit(solution)/shard_map/ppermute | solution.py:44
  100.4 3.7 %collective-permute-start.25 = (f32[64,256]{1,0:T(8,128)S(1)}, f32[64,256]{1,0:T(8,128)S(1)}, u32[]{:S(2)}, u32[]{:S(2)}) collective-permute-start(f32[64,256]{1,0:T(8,128)S(1)} %add_add_fusion.mine_ref), channel_id=1, source_target_pairs={{0,32},{32,0},{64,96},{96,64},{128,160},{160,128},{192,224},{224,1... | collective-permute-start | bytes 196616 | tf_op jit(solution)/shard_map/ppermute | solution.py:44
  107.3 3.0 %collective-permute-start.26 = (f32[8,128]{1,0:T(8,128)S(1)}, f32[8,128]{1,0:T(8,128)S(1)}, u32[]{:S(2)}, u32[]{:S(2)}) collective-permute-start(f32[8,128]{1,0:T(8,128)S(1)} %get-tuple-element.35), channel_id=1, source_target_pairs={{0,32},{32,0},{64,96},{96,64},{128,160},{160,128},{192,224},{224,1... | collective-permute-start | bytes 12296 | tf_op jit(solution)/shard_map/ppermute | solution.py:44
  110.3 3.4 %collective-permute-start.27 = (f32[8,128]{1,0:T(8,128)S(1)}, f32[8,128]{1,0:T(8,128)S(1)}, u32[]{:S(2)}, u32[]{:S(2)}) collective-permute-start(f32[8,128]{1,0:T(8,128)S(1)} %add.120), channel_id=1, source_target_pairs={{0,64},{32,96},{64,0},{96,32},{128,192},{160,224},{192,128},{224,1... | collective-permute-start | bytes 12296 | tf_op jit(solution)/shard_map/ppermute | solution.py:44
  113.7 4.6 %collective-permute-start.28 = (f32[8,128]{1,0:T(8,128)S(1)}, f32[8,128]{1,0:T(8,128)S(1)}, u32[]{:S(2)}, u32[]{:S(2)}) collective-permute-start(f32[8,128]{1,0:T(8,128)S(1)} %add.121), channel_id=1, source_target_pairs={{0,192},{32,224},{64,128},{96,160},{128,64},{160,96},{192,0},{224,... | collective-permute-start | bytes 12296 | tf_op jit(solution)/shard_map/ppermute | solution.py:44
  144.0 14.8 %collective-permute-start.29 = (f32[1024,256]{1,0:T(8,128)S(1)}, f32[1024,256]{1,0:T(8,128)S(1)}, u32[]{:S(2)}, u32[]{:S(2)}) collective-permute-start(f32[1024,256]{1,0:T(8,128)S(1)} %shard_map.76), channel_id=1, source_target_pairs={{0,1},{1,0},{2,3},{3,2},{4,5},{5,4},{6,7},{7,6},{8,9},{9,8},{10,11... | collective-permute-start | bytes 3145736 | tf_op jit(solution)/shard_map/ppermute | solution.py:67

commit v3 on v2

--- a/solution.py
+++ b/solution.py
@@ -115,10 +115,16 @@
     return lax.dot_general(block, block, (((0,), (0,)), ((), ())), preferred_element_type=F32)
 
 
-def near_kernel(near_a, near_b, after_ref, later_a, later_b, gram_out):
-    later_a[...] = near_a[...]
-    later_b[...] = near_b[...]
-    gram_out[...] = gram_of(near_a[...]) + gram_of(near_b[...])
+def join_kernel(one, two, three, four, after_ref, near_a, near_b, gram_out):
+    rows = one.shape[0]
+    near_a[:rows, :] = one[...]
+    near_a[rows:, :] = two[...]
+    near_b[:rows, :] = three[...]
+    near_b[rows:, :] = four[...]
+    gram = gram_of(one[...])
+    for block in (two, three, four):
+        gram = gram + gram_of(block[...])
+    gram_out[...] = gram
 
 
 def rest_kernel(*refs):
@@ -299,7 +305,6 @@
     half_rows = item_factors.shape[0] // 2
     half = lax.dynamic_slice_in_dim(item_factors, c * half_rows, half_rows, 0)
     near = [half] + [lax.ppermute(half, EVERY, ring_pairs(d, 0)) for d in (1, -1, 2)]
-    near_a, near_b = jnp.concatenate(near[:2], axis=0), jnp.concatenate(near[2:], axis=0)
 
     def grow(value, k):
         return jnp.concatenate([value, line_permute(value, lambda s: s ^ k)], axis=0)
@@ -309,11 +314,11 @@
     got = line_permute(held, lambda s: s ^ 1)
     block = shape((BLOCK_ROWS, RANK), BF)
     square = shape((RANK, RANK), F32)
+    near_a, near_b, gram = call(
+        join_kernel, [block, block, square], [*near, first_two], "vvvva", "vvv", []
+    )
     up_a = lax.ppermute(near_a, EVERY, ring_pairs(1, 1))
     down_b = lax.ppermute(near_b, EVERY, ring_pairs(-1, 1))
-    near_a, near_b, gram = call(
-        near_kernel, [block, block, square], [near_a, near_b, first_two], "vva", "vvv", []
-    )
     up_b = lax.ppermute(near_b, EVERY, ring_pairs(1, 1))
     down_a = lax.ppermute(near_a, EVERY, ring_pairs(-1, 1))
     far_a = lax.ppermute(up_a, EVERY, ring_pairs(1, 1))

time: 160 us -> 157 us (0.981)
  starting transfers between devices: 64.9 us -> 53.6 us
  waiting for transfers between devices: 40.3 us -> 50.7 us
    ppermute x16, starting transfers between devices: 31.1 us -> 26.3 us  [line_permute(): return lax.ppermute(value, 'z', [(s, partner(s)) for s in range(NZ)])]
    ppermute x1, waiting for transfers between devices: 0.01 us -> 4.22 us  [shards(): up_a = lax.ppermute(near_a, EVERY, ring_pairs(1, 1))]
    ppermute x16, waiting for transfers between devices: 28.9 us -> 32.9 us  [line_permute(): return lax.ppermute(value, 'z', [(s, partner(s)) for s in range(NZ)])]
    ppermute x3, waiting for transfers between devices: 2.66 us -> 6.1 us  [shards(): lax.ppermute(half, EVERY, ring_pairs(d, 0))]
    ppermute x5, starting transfers between devices: 18.7 us -> 16.1 us  [swap_cores(): return lax.ppermute(value, 'c', [(0, 1), (1, 0)])]
  transfers between devices with their start and end apart: 30 -> 30, of which waited for: 20 -> 22; matrix products, arithmetic and copies ran while one was open for 2% -> 0% of each run, Pallas kernels for 3% -> 2%
where the time goes in v3:
time: 157 us
  starting transfers between devices  53.6 us (34%)
  waiting for transfers between devices  50.7 us (32%)
  Pallas kernels  26.4 us (17%)
  blocking collectives  20 us (13%)
  other arithmetic  3.5 us (2%)
  local copies, waits for them, and re-layouts  1.85 us (1%)
    ppermute x16, waiting for transfers between devices, line_permute(): return lax.ppermute(value, 'z', [(s, partner(s)) for s in range(NZ)])  32.9 us
    pallas_call x9, Pallas kernels, call(): pl.pallas_call(kernel, out_shape=outs, grid_spec=pltpu.PrefetchScalarGrid...  26.4 us
    ppermute x16, starting transfers between devices, line_permute(): return lax.ppermute(value, 'z', [(s, partner(s)) for s in range(NZ)])  26.3 us
    all_to_all x1, blocking collectives, shards(): lax.all_to_all(send, ('x', 'y'), split_axis=0, concat_axis=0, tiled=True)  20 us
    ppermute x5, starting transfers between devices, swap_cores(): return lax.ppermute(value, 'c', [(0, 1), (1, 0)])  16.1 us
    ppermute x3, waiting for transfers between devices, shards(): lax.ppermute(half, EVERY, ring_pairs(d, 0))  6.1 us
    ppermute x3, starting transfers between devices, shards(): lax.ppermute(half, EVERY, ring_pairs(d, 0))  4.3 us
    ppermute x1, waiting for transfers between devices, shards(): up_a = lax.ppermute(near_a, EVERY, ring_pairs(1, 1))  4.22 us
  transfers between devices with their start and end apart: 30, of which 22 were waited for; matrix products, arithmetic and copies ran while one was open for 0% of the time, Pallas kernels for 2%

profile of v3, /device:TPU:1, one launch (start us, length us, event | category | flops | bytes accessed | tf_op | source)
XLA Modules:
  0.0 156.9 jit_solution(13638891398316861087)
XLA Ops:
  2.9 6.9 %collective-permute-start = (bf16[1,16,1536]{2,1,0:T(8,128)(2,1)S(1)}, bf16[1,16,1536]{2,1,0:T(8,128)(2,1)S(1)}, u32[]{:S(2)}, u32[]{:S(2)}) collective-permute-start(bf16[1,16,1536]{2,1,0:T(8,128)(2,1)S(1)} %fusion.4), channel_id=1, source_target_pairs={{0,192},{32,224},{64,128},{96,160},{128,64},{160,96},{192,0},{224,... | collective-permute-start | bytes 147464 | tf_op jit(solution)/shard_map/ppermute | solution.py:44
  9.9 2.8 %collective-permute-start.5 = (bf16[512,256]{1,0:T(8,128)(2,1)S(1)}, bf16[512,256]{1,0:T(8,128)(2,1)S(1)}, u32[]{:S(2)}, u32[]{:S(2)}) collective-permute-start(bf16[512,256]{1,0:T(8,128)(2,1)S(1)} %constant_dynamic-slice_fusion.one), channel_id=1, source_target_pairs={{0,4},{1,17},{2,6},{3,19},{4,0},{5,21},{6,2},{7,23},{8,12},{9,25},... | collective-permute-start | bytes 786440 | tf_op jit(solution)/shard_map/ppermute | solution.py:307
  12.7 0.9 collective-permute-start.4
  14.2 2.8 %collective-permute-done.5.four = bf16[512,256]{1,0:T(8,128)(2,1)S(1)} collective-permute-done((bf16[512,256]{1,0:T(8,128)(2,1)S(1)}, bf16[512,256]{1,0:T(8,128)(2,1)S(1)}, u32[]{:S(2)}, u32[]{:S(2)}) %collective-permute-start.5) | collective-permute-done | bytes 262176 | tf_op jit(solution)/shard_map/ppermute | solution.py:307
  17.0 2.9 %collective-permute-done.4.three = bf16[512,256]{1,0:T(8,128)(2,1)S(1)} collective-permute-done((bf16[512,256]{1,0:T(8,128)(2,1)S(1)}, bf16[512,256]{1,0:T(8,128)(2,1)S(1)}, u32[]{:S(2)}, u32[]{:S(2)}) %collective-permute-start.4) | collective-permute-done | bytes 262176 | tf_op jit(solution)/shard_map/ppermute | solution.py:307
  21.6 1.0 collective-permute-start.6
  22.6 1.7 %collective-permute-start.9 = (bf16[1024,256]{1,0:T(8,128)(2,1)S(1)}, bf16[1024,256]{1,0:T(8,128)(2,1)S(1)}, u32[]{:S(2)}, u32[]{:S(2)}) collective-permute-start(bf16[1024,256]{1,0:T(8,128)(2,1)S(1)} %get-tuple-element.27.rest_1_), channel_id=1, source_target_pairs={{0,24},{1,7},{2,26},{3,1},{4,28},{5,3},{6,30},{7,5},{8,0},{9,15},{... | collective-permute-start | bytes 1572872 | tf_op jit(solution)/shard_map/ppermute | solution.py:321
  24.3 1.2 collective-permute-start.1
  25.5 1.5 collective-permute-start.8
  26.9 4.2 %collective-permute-done.6.refs_0_ = bf16[1024,256]{1,0:T(8,128)(2,1)S(1)} collective-permute-done((bf16[1024,256]{1,0:T(8,128)(2,1)S(1)}, bf16[1024,256]{1,0:T(8,128)(2,1)S(1)}, u32[]{:S(2)}, u32[]{:S(2)}) %collective-permute-start.6) | collective-permute-done | bytes 524320 | tf_op jit(solution)/shard_map/ppermute | solution.py:320
  31.2 2.7 %collective-permute-start.11 = (bf16[1024,256]{1,0:T(8,128)(2,1)S(1)}, bf16[1024,256]{1,0:T(8,128)(2,1)S(1)}, u32[]{:S(2)}, u32[]{:S(2)}) collective-permute-start(bf16[1024,256]{1,0:T(8,128)(2,1)S(1)} %collective-permute-done.9.refs_3_), channel_id=1, source_target_pairs={{0,24},{1,7},{2,26},{3,1},{4,28},{5,3},{6,30},{7,5},{8,0},{9,15},{... | collective-permute-start | bytes 1572872 | tf_op jit(solution)/shard_map/ppermute | solution.py:325
  33.9 0.8 collective-permute-start.2
  34.7 4.1 %collective-permute-done.2.got_ref.refs_6_ = bf16[4,16,1536]{2,1,0:T(8,128)(2,1)S(1)} collective-permute-done((bf16[4,16,1536]{2,1,0:T(8,128)(2,1)S(1)}, bf16[4,16,1536]{2,1,0:T(8,128)(2,1)S(1)}, u32[]{:S(2)}, u32[]{:S(2)}) %collective-permute-start.2) | collective-permute-done | bytes 196640 | tf_op jit(solution)/shard_map/ppermute | solution.py:44
  38.8 3.6 %collective-permute-done.10.refs_4_ = bf16[1024,256]{1,0:T(8,128)(2,1)S(1)} collective-permute-done((bf16[1024,256]{1,0:T(8,128)(2,1)S(1)}, bf16[1024,256]{1,0:T(8,128)(2,1)S(1)}, u32[]{:S(2)}, u32[]{:S(2)}) %collective-permute-start.10) | collective-permute-done | bytes 524320 | tf_op jit(solution)/shard_map/ppermute | solution.py:324
  42.4 1.9 %shard_map.70.table.rest_2_ = bf16[6144,256]{1,0:T(8,128)(2,1)} custom-call(bf16[1024,256]{1,0:T(8,128)(2,1)S(1)} %collective-permute-done.6.refs_0_, bf16[1024,256]{1,0:T(8,128)(2,1)S(1)} %collective-permute-done.7.refs_1_, bf16[1024,256]{1,0:T(8,128)(2,1)S(1)} %collective-permute-done.8.refs_2_, bf16[1024,256]{1,0:T(8,128)(2,1)S(1)} %collective-permute-done.9.refs_3_, ...), custom_call_target="tpu_custom_call" | custom-call | tf_op jit(solution)/shard_map/pallas_call | solution.py:275
  44.3 4.0 %collective-permute-start.15 = (bf16[6144,256]{1,0:T(8,128)(2,1)}, bf16[6144,256]{1,0:T(8,128)(2,1)}, u32[]{:S(2)}, u32[]{:S(2)}) collective-permute-start(bf16[6144,256]{1,0:T(8,128)(2,1)} %shard_map.70.table.rest_2_), channel_id=1, source_target_pairs={{0,1},{1,0},{2,3},{3,2},{4,5},{5,4},{6,7},{7,6},{8,9},{9,8},{10,11... | collective-permute-start | bytes 9437192 | tf_op jit(solution)/shard_map/ppermute | solution.py:67
  48.8 0.9 copy-done.2
  49.7 2.9 %shard_map.71.gram_a = f32[256,256]{1,0:T(8,128)S(1)} custom-call(f32[256,256]{1,0:T(8,128)S(1)} %copy-done.2, bf16[6144,256]{1,0:T(8,128)(2,1)} %shard_map.70.table.rest_2_), custom_call_target="tpu_custom_call" | custom-call | tf_op jit(solution)/shard_map/pallas_call | solution.py:275
  53.0 0.8 shard_map.68
  54.0 0.9 collective-permute-done.13.rest_3_
  55.5 8.2 %shard_map.72 = (f32[64,256]{1,0:T(8,128)S(1)}, f32[64,256]{1,0:T(8,128)S(1)}, f32[256,256]{1,0:T(8,128)S(1)}, bf16[16384,256]{1,0:T(8,128)(2,1)S(1)}) custom-call(s32[128]{0:T(128)S(1)} %reshape.98.row_ref, s32[1]{0:T(128)} %bitcast.place_ref, f32[128,256]{1,0:T(8,128)S(1)} %get-tuple-element.23.start_ref, ...), custom_call_target="tpu_custom_call" | custom-call | tf_op jit(solution)/shard_map/pallas_call | solution.py:275
  63.7 0.8 collective-permute-start.16
  64.6 2.4 %collective-permute-done.16 = f32[64,256]{1,0:T(8,128)S(1)} collective-permute-done((f32[64,256]{1,0:T(8,128)S(1)}, f32[64,256]{1,0:T(8,128)S(1)}, u32[]{:S(2)}, u32[]{:S(2)}) %collective-permute-start.16) | collective-permute-done | bytes 65568 | tf_op jit(solution)/shard_map/ppermute | solution.py:44
  67.0 4.5 %collective-permute-start.18 = (f32[64,256]{1,0:T(8,128)S(1)}, f32[64,256]{1,0:T(8,128)S(1)}, u32[]{:S(2)}, u32[]{:S(2)}) collective-permute-start(f32[64,256]{1,0:T(8,128)S(1)} %add.112), channel_id=1, source_target_pairs={{0,128},{32,160},{64,192},{96,224},{128,0},{160,32},{192,64},{224,... | collective-permute-start | bytes 196616 | tf_op jit(solution)/shard_map/ppermute | solution.py:44
  71.5 1.3 collective-permute-done.19
  72.8 2.1 %collective-permute-done.18 = f32[64,256]{1,0:T(8,128)S(1)} collective-permute-done((f32[64,256]{1,0:T(8,128)S(1)}, f32[64,256]{1,0:T(8,128)S(1)}, u32[]{:S(2)}, u32[]{:S(2)}) %collective-permute-start.18) | collective-permute-done | bytes 65568 | tf_op jit(solution)/shard_map/ppermute | solution.py:44
  74.9 3.5 %collective-permute-done.17 = f32[64,256]{1,0:T(8,128)S(1)} collective-permute-done((f32[64,256]{1,0:T(8,128)S(1)}, f32[64,256]{1,0:T(8,128)S(1)}, u32[]{:S(2)}, u32[]{:S(2)}) %collective-permute-start.17) | collective-permute-done | bytes 65568 | tf_op jit(solution)/shard_map/ppermute | solution.py:44
  78.4 1.6 %collective-permute-start.20 = (f32[64,256]{1,0:T(8,128)S(1)}, f32[64,256]{1,0:T(8,128)S(1)}, u32[]{:S(2)}, u32[]{:S(2)}) collective-permute-start(f32[64,256]{1,0:T(8,128)S(1)} %add_add_fusion.1.mine_ref), channel_id=1, source_target_pairs={{0,32},{32,0},{64,96},{96,64},{128,160},{160,128},{192,224},{224,1... | collective-permute-start | bytes 196616 | tf_op jit(solution)/shard_map/ppermute | solution.py:44
  80.0 1.7 %collective-permute-done.20.other_ref = f32[64,256]{1,0:T(8,128)S(1)} collective-permute-done((f32[64,256]{1,0:T(8,128)S(1)}, f32[64,256]{1,0:T(8,128)S(1)}, u32[]{:S(2)}, u32[]{:S(2)}) %collective-permute-start.20) | collective-permute-done | bytes 65568 | tf_op jit(solution)/shard_map/ppermute | solution.py:44
  81.6 4.2 %shard_map.73 = (f32[128,256]{1,0:T(8,128)S(1)}, f32[64,256]{1,0:T(8,128)S(1)}, f32[64,256]{1,0:T(8,128)S(1)}) custom-call(s32[128]{0:T(128)S(1)} %reshape.98.row_ref, s32[1]{0:T(128)} %bitcast.place_ref, f32[64,256]{1,0:T(8,128)S(1)} %add_add_fusion.1.mine_ref, f32[64,256]{1,0:T(8,128)S(1)} %collective-permute-done.20.other_ref, ...), custom_call_target="tpu_custom_call" | custom-call | tf_op jit(solution)/shard_map/pallas_call | solution.py:275
  85.9 1.5 collective-permute-start.21
  87.3 1.7 %collective-permute-done.21 = f32[64,256]{1,0:T(8,128)S(1)} collective-permute-done((f32[64,256]{1,0:T(8,128)S(1)}, f32[64,256]{1,0:T(8,128)S(1)}, u32[]{:S(2)}, u32[]{:S(2)}) %collective-permute-start.21) | collective-permute-done | bytes 65568 | tf_op jit(solution)/shard_map/ppermute | solution.py:44
  89.3 3.9 %collective-permute-start.23 = (f32[64,256]{1,0:T(8,128)S(1)}, f32[64,256]{1,0:T(8,128)S(1)}, u32[]{:S(2)}, u32[]{:S(2)}) collective-permute-start(f32[64,256]{1,0:T(8,128)S(1)} %add.116), channel_id=1, source_target_pairs={{0,128},{32,160},{64,192},{96,224},{128,0},{160,32},{192,64},{224,... | collective-permute-start | bytes 196616 | tf_op jit(solution)/shard_map/ppermute | solution.py:44
  93.2 3.2 %collective-permute-done.23 = f32[64,256]{1,0:T(8,128)S(1)} collective-permute-done((f32[64,256]{1,0:T(8,128)S(1)}, f32[64,256]{1,0:T(8,128)S(1)}, u32[]{:S(2)}, u32[]{:S(2)}) %collective-permute-start.23) | collective-permute-done | bytes 65568 | tf_op jit(solution)/shard_map/ppermute | solution.py:44
  96.4 2.1 %collective-permute-done.22 = f32[64,256]{1,0:T(8,128)S(1)} collective-permute-done((f32[64,256]{1,0:T(8,128)S(1)}, f32[64,256]{1,0:T(8,128)S(1)}, u32[]{:S(2)}, u32[]{:S(2)}) %collective-permute-start.22) | collective-permute-done | bytes 65568 | tf_op jit(solution)/shard_map/ppermute | solution.py:44
  98.5 2.1 %collective-permute-start.25 = (f32[64,256]{1,0:T(8,128)S(1)}, f32[64,256]{1,0:T(8,128)S(1)}, u32[]{:S(2)}, u32[]{:S(2)}) collective-permute-start(f32[64,256]{1,0:T(8,128)S(1)} %add_add_fusion.mine_ref), channel_id=1, source_target_pairs={{0,32},{32,0},{64,96},{96,64},{128,160},{160,128},{192,224},{224,1... | collective-permute-start | bytes 196616 | tf_op jit(solution)/shard_map/ppermute | solution.py:44
  100.6 2.4 %collective-permute-done.25.other_ref = f32[64,256]{1,0:T(8,128)S(1)} collective-permute-done((f32[64,256]{1,0:T(8,128)S(1)}, f32[64,256]{1,0:T(8,128)S(1)}, u32[]{:S(2)}, u32[]{:S(2)}) %collective-permute-start.25) | collective-permute-done | bytes 65568 | tf_op jit(solution)/shard_map/ppermute | solution.py:44
  103.0 3.2 %shard_map.74 = (f32[128,256]{1,0:T(8,128)S(1)}, f32[128,256]{1,0:T(8,128)S(1)}, f32[128,128]{1,0:T(8,128)S(1)}, f32[8,128]{1,0:T(8,128)S(1)}) custom-call(s32[128]{0:T(128)S(1)} %reshape.98.row_ref, s32[1]{0:T(128)} %bitcast.place_ref, f32[64,256]{1,0:T(8,128)S(1)} %add_add_fusion.mine_ref, f32[64,256]{1,0:T(8,128)S(1)} %collective-permute-done.25.other_ref, ...), custom_call_target="tpu_custom_call" | custom-call | tf_op jit(solution)/shard_map/pallas_call | solution.py:275
  106.3 2.0 %collective-permute-start.26 = (f32[8,128]{1,0:T(8,128)S(1)}, f32[8,128]{1,0:T(8,128)S(1)}, u32[]{:S(2)}, u32[]{:S(2)}) collective-permute-start(f32[8,128]{1,0:T(8,128)S(1)} %get-tuple-element.35), channel_id=1, source_target_pairs={{0,32},{32,0},{64,96},{96,64},{128,160},{160,128},{192,224},{224,1... | collective-permute-start | bytes 12296 | tf_op jit(solution)/shard_map/ppermute | solution.py:44
  108.3 1.3 collective-permute-done.26
  109.6 3.3 %collective-permute-done.27 = f32[8,128]{1,0:T(8,128)S(1)} collective-permute-done((f32[8,128]{1,0:T(8,128)S(1)}, f32[8,128]{1,0:T(8,128)S(1)}, u32[]{:S(2)}, u32[]{:S(2)}) %collective-permute-start.27) | collective-permute-done | bytes 4128 | tf_op jit(solution)/shard_map/ppermute | solution.py:44
  113.5 4.1 %collective-permute-done.28 = f32[8,128]{1,0:T(8,128)S(1)} collective-permute-done((f32[8,128]{1,0:T(8,128)S(1)}, f32[8,128]{1,0:T(8,128)S(1)}, u32[]{:S(2)}, u32[]{:S(2)}) %collective-permute-start.28) | collective-permute-done | bytes 4128 | tf_op jit(solution)/shard_map/ppermute | solution.py:44
  117.5 3.3 %shard_map.75 = (f32[16,256]{1,0:T(8,128)}, bf16[16,400,128]{2,1,0:T(8,128)(2,1)S(1)}) custom-call(s32[128]{0:T(128)S(1)} %reshape.98.row_ref, s32[1]{0:T(128)} %bitcast.place_ref, f32[8,128]{1,0:T(8,128)S(1)} %add.122.curve_ref, f32[128,256]{1,0:T(8,128)S(1)} %get-tuple-element.36.value_ref, f32[128,256]{1,0:T(8,128)S(1)} %get-tuple-element.37.direction_ref, ...), custom_call_target="tpu_custom_call" | custom-call | tf_op jit(solution)/shard_map/pallas_call | solution.py:275
  120.9 20.0 %all_to_all.5.got_ref = bf16[16,400,128]{2,1,0:T(8,128)(2,1)S(1)} all-to-all(bf16[16,400,128]{2,1,0:T(8,128)(2,1)S(1)} %get-tuple-element.41), channel_id=1, replica_groups=mesh['z'=8,'x'=4,'y'=4,'c'=2] {'x','y'}, dimensions={0} | all-to-all | bytes 3276800 | tf_op jit(solution)/shard_map/all_to_all | solution.py:409
  140.9 1.3 shard_map.76
  142.2 11.3 %collective-permute-start.29 = (f32[1024,256]{1,0:T(8,128)S(1)}, f32[1024,256]{1,0:T(8,128)S(1)}, u32[]{:S(2)}, u32[]{:S(2)}) collective-permute-start(f32[1024,256]{1,0:T(8,128)S(1)} %shard_map.76), channel_id=1, source_target_pairs={{0,1},{1,0},{2,3},{3,2},{4,5},{5,4},{6,7},{7,6},{8,9},{9,8},{10,11... | collective-permute-start | bytes 3145736 | tf_op jit(solution)/shard_map/ppermute | solution.py:67
  153.5 2.3 %collective-permute-done.29 = f32[1024,256]{1,0:T(8,128)S(1)} collective-permute-done((f32[1024,256]{1,0:T(8,128)S(1)}, f32[1024,256]{1,0:T(8,128)S(1)}, u32[]{:S(2)}, u32[]{:S(2)}) %collective-permute-start.29) | collective-permute-done | bytes 1048608 | tf_op jit(solution)/shard_map/ppermute | solution.py:67
  155.8 1.1 add.123
  (47 shorter events, 7.3 us)
Async XLA Ops:
  0.6 9.2 %copy-start = (bf16[1024,256]{1,0:T(8,128)(2,1)S(1)}, bf16[1024,256]{1,0:T(8,128)(2,1)}, u32[]{:S(2)}) copy-start(bf16[1024,256]{1,0:T(8,128)(2,1)} %param.5) | copy-start | bytes 1572868
  2.9 11.3 %collective-permute-start = (bf16[1,16,1536]{2,1,0:T(8,128)(2,1)S(1)}, bf16[1,16,1536]{2,1,0:T(8,128)(2,1)S(1)}, u32[]{:S(2)}, u32[]{:S(2)}) collective-permute-start(bf16[1,16,1536]{2,1,0:T(8,128)(2,1)S(1)} %fusion.4), channel_id=1, source_target_pairs={{0,192},{32,224},{64,128},{96,160},{128,64},{160,96},{192,0},{224,... | collective-permute-start | bytes 147464 | tf_op jit(solution)/shard_map/ppermute | solution.py:44
  9.9 7.1 %collective-permute-start.5 = (bf16[512,256]{1,0:T(8,128)(2,1)S(1)}, bf16[512,256]{1,0:T(8,128)(2,1)S(1)}, u32[]{:S(2)}, u32[]{:S(2)}) collective-permute-start(bf16[512,256]{1,0:T(8,128)(2,1)S(1)} %constant_dynamic-slice_fusion.one), channel_id=1, source_target_pairs={{0,4},{1,17},{2,6},{3,19},{4,0},{5,21},{6,2},{7,23},{8,12},{9,25},... | collective-permute-start | bytes 786440 | tf_op jit(solution)/shard_map/ppermute | solution.py:307
  12.7 7.2 %collective-permute-start.4 = (bf16[512,256]{1,0:T(8,128)(2,1)S(1)}, bf16[512,256]{1,0:T(8,128)(2,1)S(1)}, u32[]{:S(2)}, u32[]{:S(2)}) collective-permute-start(bf16[512,256]{1,0:T(8,128)(2,1)S(1)} %constant_dynamic-slice_fusion.one), channel_id=1, source_target_pairs={{0,6},{1,25},{2,0},{3,27},{4,2},{5,29},{6,4},{7,31},{8,14},{9,1},{... | collective-permute-start | bytes 786440 | tf_op jit(solution)/shard_map/ppermute | solution.py:307
  13.6 6.7 %collective-permute-start.3 = (bf16[512,256]{1,0:T(8,128)(2,1)S(1)}, bf16[512,256]{1,0:T(8,128)(2,1)S(1)}, u32[]{:S(2)}, u32[]{:S(2)}) collective-permute-start(bf16[512,256]{1,0:T(8,128)(2,1)S(1)} %constant_dynamic-slice_fusion.one), channel_id=1, source_target_pairs={{0,2},{1,9},{2,4},{3,11},{4,6},{5,13},{6,0},{7,15},{8,10},{9,17},{... | collective-permute-start | bytes 786440 | tf_op jit(solution)/shard_map/ppermute | solution.py:307
  20.8 0.7 copy-start.1
  21.6 9.6 %collective-permute-start.6 = (bf16[1024,256]{1,0:T(8,128)(2,1)S(1)}, bf16[1024,256]{1,0:T(8,128)(2,1)S(1)}, u32[]{:S(2)}, u32[]{:S(2)}) collective-permute-start(bf16[1024,256]{1,0:T(8,128)(2,1)S(1)} %get-tuple-element.26.rest_0_), channel_id=1, source_target_pairs={{0,8},{1,3},{2,10},{3,5},{4,12},{5,7},{6,14},{7,1},{8,16},{9,11},{... | collective-permute-start | bytes 1572872 | tf_op jit(solution)/shard_map/ppermute | solution.py:320
  22.6 8.6 %collective-permute-start.9 = (bf16[1024,256]{1,0:T(8,128)(2,1)S(1)}, bf16[1024,256]{1,0:T(8,128)(2,1)S(1)}, u32[]{:S(2)}, u32[]{:S(2)}) collective-permute-start(bf16[1024,256]{1,0:T(8,128)(2,1)S(1)} %get-tuple-element.27.rest_1_), channel_id=1, source_target_pairs={{0,24},{1,7},{2,26},{3,1},{4,28},{5,3},{6,30},{7,5},{8,0},{9,15},{... | collective-permute-start | bytes 1572872 | tf_op jit(solution)/shard_map/ppermute | solution.py:321
  24.3 9.5 %collective-permute-start.1 = (bf16[2,16,1536]{2,1,0:T(8,128)(2,1)S(1)}, bf16[2,16,1536]{2,1,0:T(8,128)(2,1)S(1)}, u32[]{:S(2)}, u32[]{:S(2)}) collective-permute-start(bf16[2,16,1536]{2,1,0:T(8,128)(2,1)S(1)} %pad_maximum_fusion.1.after_ref), channel_id=1, source_target_pairs={{0,64},{32,96},{64,0},{96,32},{128,192},{160,224},{192,128},{224,1... | collective-permute-start | bytes 294920 | tf_op jit(solution)/shard_map/ppermute | solution.py:44
  25.5 13.3 %collective-permute-start.8 = (bf16[1024,256]{1,0:T(8,128)(2,1)S(1)}, bf16[1024,256]{1,0:T(8,128)(2,1)S(1)}, u32[]{:S(2)}, u32[]{:S(2)}) collective-permute-start(bf16[1024,256]{1,0:T(8,128)(2,1)S(1)} %get-tuple-element.26.rest_0_), channel_id=1, source_target_pairs={{0,24},{1,7},{2,26},{3,1},{4,28},{5,3},{6,30},{7,5},{8,0},{9,15},{... | collective-permute-start | bytes 1572872 | tf_op jit(solution)/shard_map/ppermute | solution.py:323
  26.9 11.8 %collective-permute-start.7 = (bf16[1024,256]{1,0:T(8,128)(2,1)S(1)}, bf16[1024,256]{1,0:T(8,128)(2,1)S(1)}, u32[]{:S(2)}, u32[]{:S(2)}) collective-permute-start(bf16[1024,256]{1,0:T(8,128)(2,1)S(1)} %get-tuple-element.27.rest_1_), channel_id=1, source_target_pairs={{0,8},{1,3},{2,10},{3,5},{4,12},{5,7},{6,14},{7,1},{8,16},{9,11},{... | collective-permute-start | bytes 1572872 | tf_op jit(solution)/shard_map/ppermute | solution.py:322
  31.2 11.2 %collective-permute-start.10 = (bf16[1024,256]{1,0:T(8,128)(2,1)S(1)}, bf16[1024,256]{1,0:T(8,128)(2,1)S(1)}, u32[]{:S(2)}, u32[]{:S(2)}) collective-permute-start(bf16[1024,256]{1,0:T(8,128)(2,1)S(1)} %collective-permute-done.6.refs_0_), channel_id=1, source_target_pairs={{0,8},{1,3},{2,10},{3,5},{4,12},{5,7},{6,14},{7,1},{8,16},{9,11},{... | collective-permute-start | bytes 1572872 | tf_op jit(solution)/shard_map/ppermute | solution.py:324
  31.2 11.2 %collective-permute-start.11 = (bf16[1024,256]{1,0:T(8,128)(2,1)S(1)}, bf16[1024,256]{1,0:T(8,128)(2,1)S(1)}, u32[]{:S(2)}, u32[]{:S(2)}) collective-permute-start(bf16[1024,256]{1,0:T(8,128)(2,1)S(1)} %collective-permute-done.9.refs_3_), channel_id=1, source_target_pairs={{0,24},{1,7},{2,26},{3,1},{4,28},{5,3},{6,30},{7,5},{8,0},{9,15},{... | collective-permute-start | bytes 1572872 | tf_op jit(solution)/shard_map/ppermute | solution.py:325
  33.9 4.9 %collective-permute-start.2 = (bf16[4,16,1536]{2,1,0:T(8,128)(2,1)S(1)}, bf16[4,16,1536]{2,1,0:T(8,128)(2,1)S(1)}, u32[]{:S(2)}, u32[]{:S(2)}) collective-permute-start(bf16[4,16,1536]{2,1,0:T(8,128)(2,1)S(1)} %pad_maximum_fusion.held_ref), channel_id=1, source_target_pairs={{0,32},{32,0},{64,96},{96,64},{128,160},{160,128},{192,224},{224,1... | collective-permute-start | bytes 589832 | tf_op jit(solution)/shard_map/ppermute | solution.py:44
  44.3 11.2 %collective-permute-start.15 = (bf16[6144,256]{1,0:T(8,128)(2,1)}, bf16[6144,256]{1,0:T(8,128)(2,1)}, u32[]{:S(2)}, u32[]{:S(2)}) collective-permute-start(bf16[6144,256]{1,0:T(8,128)(2,1)} %shard_map.70.table.rest_2_), channel_id=1, source_target_pairs={{0,1},{1,0},{2,3},{3,2},{4,5},{5,4},{6,7},{7,6},{8,9},{9,8},{10,11... | collective-permute-start | bytes 9437192 | tf_op jit(solution)/shard_map/ppermute | solution.py:67
  48.3 6.7 %collective-permute-start.13 = (bf16[1024,256]{1,0:T(8,128)(2,1)S(1)}, bf16[1024,256]{1,0:T(8,128)(2,1)S(1)}, u32[]{:S(2)}, u32[]{:S(2)}) collective-permute-start(bf16[1024,256]{1,0:T(8,128)(2,1)S(1)} %get-tuple-element.26.rest_0_), channel_id=1, source_target_pairs={{0,1},{1,0},{2,3},{3,2},{4,5},{5,4},{6,7},{7,6},{8,9},{9,8},{10,11... | collective-permute-start | bytes 1572872 | tf_op jit(solution)/shard_map/ppermute | solution.py:67
  48.4 6.7 %collective-permute-start.14 = (bf16[1024,256]{1,0:T(8,128)(2,1)S(1)}, bf16[1024,256]{1,0:T(8,128)(2,1)}, u32[]{:S(2)}, u32[]{:S(2)}) collective-permute-start(bf16[1024,256]{1,0:T(8,128)(2,1)S(1)} %get-tuple-element.27.rest_1_), channel_id=1, source_target_pairs={{0,1},{1,0},{2,3},{3,2},{4,5},{5,4},{6,7},{7,6},{8,9},{9,8},{10,11... | collective-permute-start | bytes 1572872 | tf_op jit(solution)/shard_map/ppermute | solution.py:67
  48.8 0.9 copy-start.2
  52.6 2.9 %collective-permute-start.12 = (f32[256,256]{1,0:T(8,128)S(1)}, f32[256,256]{1,0:T(8,128)}, u32[]{:S(2)}, u32[]{:S(2)}) collective-permute-start(f32[256,256]{1,0:T(8,128)S(1)} %shard_map.71.gram_a), channel_id=1, source_target_pairs={{0,1},{1,0},{2,3},{3,2},{4,5},{5,4},{6,7},{7,6},{8,9},{9,8},{10,11... | collective-permute-start | bytes 786440 | tf_op jit(solution)/shard_map/ppermute | solution.py:67
  63.7 3.2 %collective-permute-start.16 = (f32[64,256]{1,0:T(8,128)S(1)}, f32[64,256]{1,0:T(8,128)S(1)}, u32[]{:S(2)}, u32[]{:S(2)}) collective-permute-start(f32[64,256]{1,0:T(8,128)S(1)} %get-tuple-element.29), channel_id=1, source_target_pairs={{0,32},{32,0},{64,96},{96,64},{128,160},{160,128},{192,224},{224,1... | collective-permute-start | bytes 196616 | tf_op jit(solution)/shard_map/ppermute | solution.py:44
  66.9 5.8 %collective-permute-start.19 = (f32[64,256]{1,0:T(8,128)S(1)}, f32[64,256]{1,0:T(8,128)S(1)}, u32[]{:S(2)}, u32[]{:S(2)}) collective-permute-start(f32[64,256]{1,0:T(8,128)S(1)} %add.112), channel_id=1, source_target_pairs={{0,192},{32,224},{64,0},{96,32},{128,64},{160,96},{192,128},{224,1... | collective-permute-start | bytes 196616 | tf_op jit(solution)/shard_map/ppermute | solution.py:44
  67.0 7.8 %collective-permute-start.18 = (f32[64,256]{1,0:T(8,128)S(1)}, f32[64,256]{1,0:T(8,128)S(1)}, u32[]{:S(2)}, u32[]{:S(2)}) collective-permute-start(f32[64,256]{1,0:T(8,128)S(1)} %add.112), channel_id=1, source_target_pairs={{0,128},{32,160},{64,192},{96,224},{128,0},{160,32},{192,64},{224,... | collective-permute-start | bytes 196616 | tf_op jit(solution)/shard_map/ppermute | solution.py:44
  71.5 6.8 %collective-permute-start.17 = (f32[64,256]{1,0:T(8,128)S(1)}, f32[64,256]{1,0:T(8,128)S(1)}, u32[]{:S(2)}, u32[]{:S(2)}) collective-permute-start(f32[64,256]{1,0:T(8,128)S(1)} %add.112), channel_id=1, source_target_pairs={{0,64},{32,96},{64,128},{96,160},{128,192},{160,224},{192,0},{224,... | collective-permute-start | bytes 196616 | tf_op jit(solution)/shard_map/ppermute | solution.py:44
  78.4 3.3 %collective-permute-start.20 = (f32[64,256]{1,0:T(8,128)S(1)}, f32[64,256]{1,0:T(8,128)S(1)}, u32[]{:S(2)}, u32[]{:S(2)}) collective-permute-start(f32[64,256]{1,0:T(8,128)S(1)} %add_add_fusion.1.mine_ref), channel_id=1, source_target_pairs={{0,32},{32,0},{64,96},{96,64},{128,160},{160,128},{192,224},{224,1... | collective-permute-start | bytes 196616 | tf_op jit(solution)/shard_map/ppermute | solution.py:44
  85.9 3.1 %collective-permute-start.21 = (f32[64,256]{1,0:T(8,128)S(1)}, f32[64,256]{1,0:T(8,128)S(1)}, u32[]{:S(2)}, u32[]{:S(2)}) collective-permute-start(f32[64,256]{1,0:T(8,128)S(1)} %get-tuple-element.33), channel_id=1, source_target_pairs={{0,32},{32,0},{64,96},{96,64},{128,160},{160,128},{192,224},{224,1... | collective-permute-start | bytes 196616 | tf_op jit(solution)/shard_map/ppermute | solution.py:44
  89.0 4.2 %collective-permute-start.24 = (f32[64,256]{1,0:T(8,128)S(1)}, f32[64,256]{1,0:T(8,128)S(1)}, u32[]{:S(2)}, u32[]{:S(2)}) collective-permute-start(f32[64,256]{1,0:T(8,128)S(1)} %add.116), channel_id=1, source_target_pairs={{0,192},{32,224},{64,0},{96,32},{128,64},{160,96},{192,128},{224,1... | collective-permute-start | bytes 196616 | tf_op jit(solution)/shard_map/ppermute | solution.py:44
  89.3 7.1 %collective-permute-start.23 = (f32[64,256]{1,0:T(8,128)S(1)}, f32[64,256]{1,0:T(8,128)S(1)}, u32[]{:S(2)}, u32[]{:S(2)}) collective-permute-start(f32[64,256]{1,0:T(8,128)S(1)} %add.116), channel_id=1, source_target_pairs={{0,128},{32,160},{64,192},{96,224},{128,0},{160,32},{192,64},{224,... | collective-permute-start | bytes 196616 | tf_op jit(solution)/shard_map/ppermute | solution.py:44
  93.2 5.3 %collective-permute-start.22 = (f32[64,256]{1,0:T(8,128)S(1)}, f32[64,256]{1,0:T(8,128)S(1)}, u32[]{:S(2)}, u32[]{:S(2)}) collective-permute-start(f32[64,256]{1,0:T(8,128)S(1)} %add.116), channel_id=1, source_target_pairs={{0,64},{32,96},{64,128},{96,160},{128,192},{160,224},{192,0},{224,... | collective-permute-start | bytes 196616 | tf_op jit(solution)/shard_map/ppermute | solution.py:44
  98.5 4.6 %collective-permute-start.25 = (f32[64,256]{1,0:T(8,128)S(1)}, f32[64,256]{1,0:T(8,128)S(1)}, u32[]{:S(2)}, u32[]{:S(2)}) collective-permute-start(f32[64,256]{1,0:T(8,128)S(1)} %add_add_fusion.mine_ref), channel_id=1, source_target_pairs={{0,32},{32,0},{64,96},{96,64},{128,160},{160,128},{192,224},{224,1... | collective-permute-start | bytes 196616 | tf_op jit(solution)/shard_map/ppermute | solution.py:44
  106.3 3.3 %collective-permute-start.26 = (f32[8,128]{1,0:T(8,128)S(1)}, f32[8,128]{1,0:T(8,128)S(1)}, u32[]{:S(2)}, u32[]{:S(2)}) collective-permute-start(f32[8,128]{1,0:T(8,128)S(1)} %get-tuple-element.35), channel_id=1, source_target_pairs={{0,32},{32,0},{64,96},{96,64},{128,160},{160,128},{192,224},{224,1... | collective-permute-start | bytes 12296 | tf_op jit(solution)/shard_map/ppermute | solution.py:44
  109.6 3.4 %collective-permute-start.27 = (f32[8,128]{1,0:T(8,128)S(1)}, f32[8,128]{1,0:T(8,128)S(1)}, u32[]{:S(2)}, u32[]{:S(2)}) collective-permute-start(f32[8,128]{1,0:T(8,128)S(1)} %add.120), channel_id=1, source_target_pairs={{0,64},{32,96},{64,0},{96,32},{128,192},{160,224},{192,128},{224,1... | collective-permute-start | bytes 12296 | tf_op jit(solution)/shard_map/ppermute | solution.py:44
  112.9 4.6 %collective-permute-start.28 = (f32[8,128]{1,0:T(8,128)S(1)}, f32[8,128]{1,0:T(8,128)S(1)}, u32[]{:S(2)}, u32[]{:S(2)}) collective-permute-start(f32[8,128]{1,0:T(8,128)S(1)} %add.121), channel_id=1, source_target_pairs={{0,192},{32,224},{64,128},{96,160},{128,64},{160,96},{192,0},{224,... | collective-permute-start | bytes 12296 | tf_op jit(solution)/shard_map/ppermute | solution.py:44
  142.2 13.6 %collective-permute-start.29 = (f32[1024,256]{1,0:T(8,128)S(1)}, f32[1024,256]{1,0:T(8,128)S(1)}, u32[]{:S(2)}, u32[]{:S(2)}) collective-permute-start(f32[1024,256]{1,0:T(8,128)S(1)} %shard_map.76), channel_id=1, source_target_pairs={{0,1},{1,0},{2,3},{3,2},{4,5},{5,4},{6,7},{7,6},{8,9},{9,8},{10,11... | collective-permute-start | bytes 3145736 | tf_op jit(solution)/shard_map/ppermute | solution.py:67

commit v4 on v3

--- a/solution.py
+++ b/solution.py
@@ -85,9 +85,8 @@
     z = place_ref[0]
     for s in range(NZ):
         gap = lax.bitwise_xor(z, s)
-        pair = lax.div(gap, 2)
-        place = jnp.where(pair == 3, 1, jnp.where(pair == 0, 0, pair + 1))
-        near = lax.bitwise_and(gap, 1) == 0
+        near = gap < 4
+        place = jnp.where(near, gap, lax.bitwise_xor(gap, 6))
 
         def pay(start, stop):
             held = held_ref[place, :, start:stop].astype(F32)
@@ -309,9 +308,9 @@
     def grow(value, k):
         return jnp.concatenate([value, line_permute(value, lambda s: s ^ k)], axis=0)
 
-    first_two = grow(pay[None], 6)
+    first_two = grow(pay[None], 1)
     held = grow(first_two, 2)
-    got = line_permute(held, lambda s: s ^ 1)
+    got = line_permute(held, lambda s: s ^ 6)
     block = shape((BLOCK_ROWS, RANK), BF)
     square = shape((RANK, RANK), F32)
     near_a, near_b, gram = call(

time: 157 us -> 156 us (level)
  waiting for transfers between devices: 50.7 us -> 41.1 us
  starting transfers between devices: 53.6 us -> 62.6 us
    ppermute x16, starting transfers between devices: 26.3 us -> 32.9 us  [line_permute(): return lax.ppermute(value, 'z', [(s, partner(s)) for s in range(NZ)])]
    ppermute x16, waiting for transfers between devices: 32.9 us -> 28.6 us  [line_permute(): return lax.ppermute(value, 'z', [(s, partner(s)) for s in range(NZ)])]
    ppermute x1, waiting for transfers between devices: 3.62 us -> 0.11 us  [shards(): far_a = lax.ppermute(up_a, EVERY, ring_pairs(1, 1))]
    ppermute x5, starting transfers between devices: 16.1 us -> 18.5 us  [swap_cores(): return lax.ppermute(value, 'c', [(0, 1), (1, 0)])]
    ppermute x1, waiting for transfers between devices: 4.22 us -> 2.4 us  [shards(): up_a = lax.ppermute(near_a, EVERY, ring_pairs(1, 1))]
  transfers between devices with their start and end apart: 30 -> 30, of which waited for: 22 -> 21; matrix products, arithmetic and copies ran while one was open for 0% -> 0% of each run, Pallas kernels for 2% -> 2%
where the time goes in v4:
time: 156 us; the launch traced here: 155 us
  starting transfers between devices  62.6 us (40%)
  waiting for transfers between devices  41.1 us (26%)
  Pallas kernels  26.4 us (17%)
  blocking collectives  19 us (12%)
  other arithmetic  3.5 us (2%)
  local copies, waits for them, and re-layouts  1.85 us (1%)
    ppermute x16, starting transfers between devices, line_permute(): return lax.ppermute(value, 'z', [(s, partner(s)) for s in range(NZ)])  32.9 us
    ppermute x16, waiting for transfers between devices, line_permute(): return lax.ppermute(value, 'z', [(s, partner(s)) for s in range(NZ)])  28.6 us
    pallas_call x9, Pallas kernels, call(): pl.pallas_call(kernel, out_shape=outs, grid_spec=pltpu.PrefetchScalarGrid...  26.4 us
    all_to_all x1, blocking collectives, shards(): lax.all_to_all(send, ('x', 'y'), split_axis=0, concat_axis=0, tiled=True)  19 us
    ppermute x5, starting transfers between devices, swap_cores(): return lax.ppermute(value, 'c', [(0, 1), (1, 0)])  18.5 us
    ppermute x3, waiting for transfers between devices, shards(): lax.ppermute(half, EVERY, ring_pairs(d, 0))  6.1 us
    ppermute x3, starting transfers between devices, shards(): lax.ppermute(half, EVERY, ring_pairs(d, 0))  4.3 us
    ppermute x5, waiting for transfers between devices, swap_cores(): return lax.ppermute(value, 'c', [(0, 1), (1, 0)])  3.87 us
  transfers between devices with their start and end apart: 30, of which 21 were waited for; matrix products, arithmetic and copies ran while one was open for 0% of the time, Pallas kernels for 2%

profile of v4, /device:TPU:1, one launch (start us, length us, event | category | flops | bytes accessed | tf_op | source)
XLA Modules:
  0.0 155.2 jit_solution(6089699542269428185)
XLA Ops:
  2.1 0.8 fusion.4
  2.9 2.6 %collective-permute-start = (bf16[1,16,1536]{2,1,0:T(8,128)(2,1)S(1)}, bf16[1,16,1536]{2,1,0:T(8,128)(2,1)S(1)}, u32[]{:S(2)}, u32[]{:S(2)}) collective-permute-start(bf16[1,16,1536]{2,1,0:T(8,128)(2,1)S(1)} %fusion.4), channel_id=1, source_target_pairs={{0,32},{32,0},{64,96},{96,64},{128,160},{160,128},{192,224},{224,1... | collective-permute-start | bytes 147464 | tf_op jit(solution)/shard_map/ppermute | solution.py:44
  5.5 2.8 %collective-permute-start.5 = (bf16[512,256]{1,0:T(8,128)(2,1)S(1)}, bf16[512,256]{1,0:T(8,128)(2,1)S(1)}, u32[]{:S(2)}, u32[]{:S(2)}) collective-permute-start(bf16[512,256]{1,0:T(8,128)(2,1)S(1)} %constant_dynamic-slice_fusion.one), channel_id=1, source_target_pairs={{0,4},{1,17},{2,6},{3,19},{4,0},{5,21},{6,2},{7,23},{8,12},{9,25},... | collective-permute-start | bytes 786440 | tf_op jit(solution)/shard_map/ppermute | solution.py:306
  8.3 0.9 collective-permute-start.4
  9.8 2.8 %collective-permute-done.5.four = bf16[512,256]{1,0:T(8,128)(2,1)S(1)} collective-permute-done((bf16[512,256]{1,0:T(8,128)(2,1)S(1)}, bf16[512,256]{1,0:T(8,128)(2,1)S(1)}, u32[]{:S(2)}, u32[]{:S(2)}) %collective-permute-start.5) | collective-permute-done | bytes 262176 | tf_op jit(solution)/shard_map/ppermute | solution.py:306
  12.6 2.9 %collective-permute-done.4.three = bf16[512,256]{1,0:T(8,128)(2,1)S(1)} collective-permute-done((bf16[512,256]{1,0:T(8,128)(2,1)S(1)}, bf16[512,256]{1,0:T(8,128)(2,1)S(1)}, u32[]{:S(2)}, u32[]{:S(2)}) %collective-permute-start.4) | collective-permute-done | bytes 262176 | tf_op jit(solution)/shard_map/ppermute | solution.py:306
  17.2 1.0 collective-permute-start.6
  18.2 1.7 %collective-permute-start.9 = (bf16[1024,256]{1,0:T(8,128)(2,1)S(1)}, bf16[1024,256]{1,0:T(8,128)(2,1)S(1)}, u32[]{:S(2)}, u32[]{:S(2)}) collective-permute-start(bf16[1024,256]{1,0:T(8,128)(2,1)S(1)} %get-tuple-element.27.rest_1_), channel_id=1, source_target_pairs={{0,24},{1,7},{2,26},{3,1},{4,28},{5,3},{6,30},{7,5},{8,0},{9,15},{... | collective-permute-start | bytes 1572872 | tf_op jit(solution)/shard_map/ppermute | solution.py:320
  19.9 3.0 %collective-permute-start.1 = (bf16[2,16,1536]{2,1,0:T(8,128)(2,1)S(1)}, bf16[2,16,1536]{2,1,0:T(8,128)(2,1)S(1)}, u32[]{:S(2)}, u32[]{:S(2)}) collective-permute-start(bf16[2,16,1536]{2,1,0:T(8,128)(2,1)S(1)} %pad_maximum_fusion.1.after_ref), channel_id=1, source_target_pairs={{0,64},{32,96},{64,0},{96,32},{128,192},{160,224},{192,128},{224,1... | collective-permute-start | bytes 294920 | tf_op jit(solution)/shard_map/ppermute | solution.py:44
  22.9 1.5 collective-permute-start.8
  24.4 2.4 %collective-permute-done.6.refs_0_ = bf16[1024,256]{1,0:T(8,128)(2,1)S(1)} collective-permute-done((bf16[1024,256]{1,0:T(8,128)(2,1)S(1)}, bf16[1024,256]{1,0:T(8,128)(2,1)S(1)}, u32[]{:S(2)}, u32[]{:S(2)}) %collective-permute-start.6) | collective-permute-done | bytes 524320 | tf_op jit(solution)/shard_map/ppermute | solution.py:319
  26.8 2.7 %collective-permute-start.11 = (bf16[1024,256]{1,0:T(8,128)(2,1)S(1)}, bf16[1024,256]{1,0:T(8,128)(2,1)S(1)}, u32[]{:S(2)}, u32[]{:S(2)}) collective-permute-start(bf16[1024,256]{1,0:T(8,128)(2,1)S(1)} %collective-permute-done.9.refs_3_), channel_id=1, source_target_pairs={{0,24},{1,7},{2,26},{3,1},{4,28},{5,3},{6,30},{7,5},{8,0},{9,15},{... | collective-permute-start | bytes 1572872 | tf_op jit(solution)/shard_map/ppermute | solution.py:324
  29.5 5.2 %collective-permute-start.2 = (bf16[4,16,1536]{2,1,0:T(8,128)(2,1)S(1)}, bf16[4,16,1536]{2,1,0:T(8,128)(2,1)S(1)}, u32[]{:S(2)}, u32[]{:S(2)}) collective-permute-start(bf16[4,16,1536]{2,1,0:T(8,128)(2,1)S(1)} %pad_maximum_fusion.held_ref), channel_id=1, source_target_pairs={{0,192},{32,224},{64,128},{96,160},{128,64},{160,96},{192,0},{224,... | collective-permute-start | bytes 589832 | tf_op jit(solution)/shard_map/ppermute | solution.py:44
  34.7 4.7 %collective-permute-done.2.got_ref.refs_6_ = bf16[4,16,1536]{2,1,0:T(8,128)(2,1)S(1)} collective-permute-done((bf16[4,16,1536]{2,1,0:T(8,128)(2,1)S(1)}, bf16[4,16,1536]{2,1,0:T(8,128)(2,1)S(1)}, u32[]{:S(2)}, u32[]{:S(2)}) %collective-permute-start.2) | collective-permute-done | bytes 196640 | tf_op jit(solution)/shard_map/ppermute | solution.py:44
  39.5 1.9 %shard_map.70.table.rest_2_ = bf16[6144,256]{1,0:T(8,128)(2,1)} custom-call(bf16[1024,256]{1,0:T(8,128)(2,1)S(1)} %collective-permute-done.6.refs_0_, bf16[1024,256]{1,0:T(8,128)(2,1)S(1)} %collective-permute-done.7.refs_1_, bf16[1024,256]{1,0:T(8,128)(2,1)S(1)} %collective-permute-done.8.refs_2_, bf16[1024,256]{1,0:T(8,128)(2,1)S(1)} %collective-permute-done.9.refs_3_, ...), custom_call_target="tpu_custom_call" | custom-call | tf_op jit(solution)/shard_map/pallas_call | solution.py:274
  41.4 4.7 %collective-permute-start.15 = (bf16[6144,256]{1,0:T(8,128)(2,1)}, bf16[6144,256]{1,0:T(8,128)(2,1)}, u32[]{:S(2)}, u32[]{:S(2)}) collective-permute-start(bf16[6144,256]{1,0:T(8,128)(2,1)} %shard_map.70.table.rest_2_), channel_id=1, source_target_pairs={{0,1},{1,0},{2,3},{3,2},{4,5},{5,4},{6,7},{7,6},{8,9},{9,8},{10,11... | collective-permute-start | bytes 9437192 | tf_op jit(solution)/shard_map/ppermute | solution.py:67
  46.6 0.9 copy-done.2
  47.6 2.9 %shard_map.71.gram_a = f32[256,256]{1,0:T(8,128)S(1)} custom-call(f32[256,256]{1,0:T(8,128)S(1)} %copy-done.2, bf16[6144,256]{1,0:T(8,128)(2,1)} %shard_map.70.table.rest_2_), custom_call_target="tpu_custom_call" | custom-call | tf_op jit(solution)/shard_map/pallas_call | solution.py:274
  51.8 0.9 collective-permute-done.13.rest_3_
  53.4 8.2 %shard_map.72 = (f32[64,256]{1,0:T(8,128)S(1)}, f32[64,256]{1,0:T(8,128)S(1)}, f32[256,256]{1,0:T(8,128)S(1)}, bf16[16384,256]{1,0:T(8,128)(2,1)S(1)}) custom-call(s32[128]{0:T(128)S(1)} %reshape.98.row_ref, s32[1]{0:T(128)} %bitcast.place_ref, f32[128,256]{1,0:T(8,128)S(1)} %get-tuple-element.23.start_ref, ...), custom_call_target="tpu_custom_call" | custom-call | tf_op jit(solution)/shard_map/pallas_call | solution.py:274
  61.6 1.5 collective-permute-start.16
  63.1 1.7 %collective-permute-done.16 = f32[64,256]{1,0:T(8,128)S(1)} collective-permute-done((f32[64,256]{1,0:T(8,128)S(1)}, f32[64,256]{1,0:T(8,128)S(1)}, u32[]{:S(2)}, u32[]{:S(2)}) %collective-permute-start.16) | collective-permute-done | bytes 65568 | tf_op jit(solution)/shard_map/ppermute | solution.py:44
  64.8 4.4 %collective-permute-start.19 = (f32[64,256]{1,0:T(8,128)S(1)}, f32[64,256]{1,0:T(8,128)S(1)}, u32[]{:S(2)}, u32[]{:S(2)}) collective-permute-start(f32[64,256]{1,0:T(8,128)S(1)} %add.112), channel_id=1, source_target_pairs={{0,192},{32,224},{64,0},{96,32},{128,64},{160,96},{192,128},{224,1... | collective-permute-start | bytes 196616 | tf_op jit(solution)/shard_map/ppermute | solution.py:44
  69.2 1.1 collective-permute-start.18
  70.3 1.9 %collective-permute-start.17 = (f32[64,256]{1,0:T(8,128)S(1)}, f32[64,256]{1,0:T(8,128)S(1)}, u32[]{:S(2)}, u32[]{:S(2)}) collective-permute-start(f32[64,256]{1,0:T(8,128)S(1)} %add.112), channel_id=1, source_target_pairs={{0,64},{32,96},{64,128},{96,160},{128,192},{160,224},{192,0},{224,... | collective-permute-start | bytes 196616 | tf_op jit(solution)/shard_map/ppermute | solution.py:44
  72.2 4.1 %collective-permute-done.18 = f32[64,256]{1,0:T(8,128)S(1)} collective-permute-done((f32[64,256]{1,0:T(8,128)S(1)}, f32[64,256]{1,0:T(8,128)S(1)}, u32[]{:S(2)}, u32[]{:S(2)}) %collective-permute-start.18) | collective-permute-done | bytes 65568 | tf_op jit(solution)/shard_map/ppermute | solution.py:44
  77.1 3.1 %collective-permute-done.20.other_ref = f32[64,256]{1,0:T(8,128)S(1)} collective-permute-done((f32[64,256]{1,0:T(8,128)S(1)}, f32[64,256]{1,0:T(8,128)S(1)}, u32[]{:S(2)}, u32[]{:S(2)}) %collective-permute-start.20) | collective-permute-done | bytes 65568 | tf_op jit(solution)/shard_map/ppermute | solution.py:44
  80.2 4.2 %shard_map.73 = (f32[128,256]{1,0:T(8,128)S(1)}, f32[64,256]{1,0:T(8,128)S(1)}, f32[64,256]{1,0:T(8,128)S(1)}) custom-call(s32[128]{0:T(128)S(1)} %reshape.98.row_ref, s32[1]{0:T(128)} %bitcast.place_ref, f32[64,256]{1,0:T(8,128)S(1)} %add_add_fusion.1.mine_ref, f32[64,256]{1,0:T(8,128)S(1)} %collective-permute-done.20.other_ref, ...), custom_call_target="tpu_custom_call" | custom-call | tf_op jit(solution)/shard_map/pallas_call | solution.py:274
  84.6 3.0 %collective-permute-done.21 = f32[64,256]{1,0:T(8,128)S(1)} collective-permute-done((f32[64,256]{1,0:T(8,128)S(1)}, f32[64,256]{1,0:T(8,128)S(1)}, u32[]{:S(2)}, u32[]{:S(2)}) %collective-permute-start.21) | collective-permute-done | bytes 65568 | tf_op jit(solution)/shard_map/ppermute | solution.py:44
  87.5 1.5 collective-permute-start.24
  89.0 3.0 %collective-permute-start.23 = (f32[64,256]{1,0:T(8,128)S(1)}, f32[64,256]{1,0:T(8,128)S(1)}, u32[]{:S(2)}, u32[]{:S(2)}) collective-permute-start(f32[64,256]{1,0:T(8,128)S(1)} %add.116), channel_id=1, source_target_pairs={{0,128},{32,160},{64,192},{96,224},{128,0},{160,32},{192,64},{224,... | collective-permute-start | bytes 196616 | tf_op jit(solution)/shard_map/ppermute | solution.py:44
  92.0 1.6 %collective-permute-start.22 = (f32[64,256]{1,0:T(8,128)S(1)}, f32[64,256]{1,0:T(8,128)S(1)}, u32[]{:S(2)}, u32[]{:S(2)}) collective-permute-start(f32[64,256]{1,0:T(8,128)S(1)} %add.116), channel_id=1, source_target_pairs={{0,64},{32,96},{64,128},{96,160},{128,192},{160,224},{192,0},{224,... | collective-permute-start | bytes 196616 | tf_op jit(solution)/shard_map/ppermute | solution.py:44
  93.6 2.6 %collective-permute-done.23 = f32[64,256]{1,0:T(8,128)S(1)} collective-permute-done((f32[64,256]{1,0:T(8,128)S(1)}, f32[64,256]{1,0:T(8,128)S(1)}, u32[]{:S(2)}, u32[]{:S(2)}) %collective-permute-start.23) | collective-permute-done | bytes 65568 | tf_op jit(solution)/shard_map/ppermute | solution.py:44
  96.2 1.4 collective-permute-done.22
  97.6 1.4 collective-permute-start.25
  99.0 2.3 %collective-permute-done.25.other_ref = f32[64,256]{1,0:T(8,128)S(1)} collective-permute-done((f32[64,256]{1,0:T(8,128)S(1)}, f32[64,256]{1,0:T(8,128)S(1)}, u32[]{:S(2)}, u32[]{:S(2)}) %collective-permute-start.25) | collective-permute-done | bytes 65568 | tf_op jit(solution)/shard_map/ppermute | solution.py:44
  101.3 3.2 %shard_map.74 = (f32[128,256]{1,0:T(8,128)S(1)}, f32[128,256]{1,0:T(8,128)S(1)}, f32[128,128]{1,0:T(8,128)S(1)}, f32[8,128]{1,0:T(8,128)S(1)}) custom-call(s32[128]{0:T(128)S(1)} %reshape.98.row_ref, s32[1]{0:T(128)} %bitcast.place_ref, f32[64,256]{1,0:T(8,128)S(1)} %add_add_fusion.mine_ref, f32[64,256]{1,0:T(8,128)S(1)} %collective-permute-done.25.other_ref, ...), custom_call_target="tpu_custom_call" | custom-call | tf_op jit(solution)/shard_map/pallas_call | solution.py:274
  105.3 1.7 %collective-permute-done.26 = f32[8,128]{1,0:T(8,128)S(1)} collective-permute-done((f32[8,128]{1,0:T(8,128)S(1)}, f32[8,128]{1,0:T(8,128)S(1)}, u32[]{:S(2)}, u32[]{:S(2)}) %collective-permute-start.26) | collective-permute-done | bytes 4128 | tf_op jit(solution)/shard_map/ppermute | solution.py:44
  107.0 2.6 %collective-permute-start.27 = (f32[8,128]{1,0:T(8,128)S(1)}, f32[8,128]{1,0:T(8,128)S(1)}, u32[]{:S(2)}, u32[]{:S(2)}) collective-permute-start(f32[8,128]{1,0:T(8,128)S(1)} %add.120), channel_id=1, source_target_pairs={{0,64},{32,96},{64,0},{96,32},{128,192},{160,224},{192,128},{224,1... | collective-permute-start | bytes 12296 | tf_op jit(solution)/shard_map/ppermute | solution.py:44
  109.6 1.0 collective-permute-done.27
  110.6 2.2 %collective-permute-start.28 = (f32[8,128]{1,0:T(8,128)S(1)}, f32[8,128]{1,0:T(8,128)S(1)}, u32[]{:S(2)}, u32[]{:S(2)}) collective-permute-start(f32[8,128]{1,0:T(8,128)S(1)} %add.121), channel_id=1, source_target_pairs={{0,192},{32,224},{64,128},{96,160},{128,64},{160,96},{192,0},{224,... | collective-permute-start | bytes 12296 | tf_op jit(solution)/shard_map/ppermute | solution.py:44
  112.8 2.3 %collective-permute-done.28 = f32[8,128]{1,0:T(8,128)S(1)} collective-permute-done((f32[8,128]{1,0:T(8,128)S(1)}, f32[8,128]{1,0:T(8,128)S(1)}, u32[]{:S(2)}, u32[]{:S(2)}) %collective-permute-start.28) | collective-permute-done | bytes 4128 | tf_op jit(solution)/shard_map/ppermute | solution.py:44
  115.2 3.3 %shard_map.75 = (f32[16,256]{1,0:T(8,128)}, bf16[16,400,128]{2,1,0:T(8,128)(2,1)S(1)}) custom-call(s32[128]{0:T(128)S(1)} %reshape.98.row_ref, s32[1]{0:T(128)} %bitcast.place_ref, f32[8,128]{1,0:T(8,128)S(1)} %add.122.curve_ref, f32[128,256]{1,0:T(8,128)S(1)} %get-tuple-element.36.value_ref, f32[128,256]{1,0:T(8,128)S(1)} %get-tuple-element.37.direction_ref, ...), custom_call_target="tpu_custom_call" | custom-call | tf_op jit(solution)/shard_map/pallas_call | solution.py:274
  118.5 19.0 %all_to_all.5.got_ref = bf16[16,400,128]{2,1,0:T(8,128)(2,1)S(1)} all-to-all(bf16[16,400,128]{2,1,0:T(8,128)(2,1)S(1)} %get-tuple-element.41), channel_id=1, replica_groups=mesh['z'=8,'x'=4,'y'=4,'c'=2] {'x','y'}, dimensions={0} | all-to-all | bytes 3276800 | tf_op jit(solution)/shard_map/all_to_all | solution.py:408
  137.5 1.3 shard_map.76
  138.8 13.0 %collective-permute-start.29 = (f32[1024,256]{1,0:T(8,128)S(1)}, f32[1024,256]{1,0:T(8,128)S(1)}, u32[]{:S(2)}, u32[]{:S(2)}) collective-permute-start(f32[1024,256]{1,0:T(8,128)S(1)} %shard_map.76), channel_id=1, source_target_pairs={{0,1},{1,0},{2,3},{3,2},{4,5},{5,4},{6,7},{7,6},{8,9},{9,8},{10,11... | collective-permute-start | bytes 3145736 | tf_op jit(solution)/shard_map/ppermute | solution.py:67
  151.8 2.3 %collective-permute-done.29 = f32[1024,256]{1,0:T(8,128)S(1)} collective-permute-done((f32[1024,256]{1,0:T(8,128)S(1)}, f32[1024,256]{1,0:T(8,128)S(1)}, u32[]{:S(2)}, u32[]{:S(2)}) %collective-permute-start.29) | collective-permute-done | bytes 1048608 | tf_op jit(solution)/shard_map/ppermute | solution.py:67
  154.1 1.1 add.123
  (47 shorter events, 8.1 us)
Async XLA Ops:
  0.6 4.9 %copy-start = (bf16[1024,256]{1,0:T(8,128)(2,1)S(1)}, bf16[1024,256]{1,0:T(8,128)(2,1)}, u32[]{:S(2)}) copy-start(bf16[1024,256]{1,0:T(8,128)(2,1)} %param.5) | copy-start | bytes 1572868
  2.9 6.9 %collective-permute-start = (bf16[1,16,1536]{2,1,0:T(8,128)(2,1)S(1)}, bf16[1,16,1536]{2,1,0:T(8,128)(2,1)S(1)}, u32[]{:S(2)}, u32[]{:S(2)}) collective-permute-start(bf16[1,16,1536]{2,1,0:T(8,128)(2,1)S(1)} %fusion.4), channel_id=1, source_target_pairs={{0,32},{32,0},{64,96},{96,64},{128,160},{160,128},{192,224},{224,1... | collective-permute-start | bytes 147464 | tf_op jit(solution)/shard_map/ppermute | solution.py:44
  5.5 7.1 %collective-permute-start.5 = (bf16[512,256]{1,0:T(8,128)(2,1)S(1)}, bf16[512,256]{1,0:T(8,128)(2,1)S(1)}, u32[]{:S(2)}, u32[]{:S(2)}) collective-permute-start(bf16[512,256]{1,0:T(8,128)(2,1)S(1)} %constant_dynamic-slice_fusion.one), channel_id=1, source_target_pairs={{0,4},{1,17},{2,6},{3,19},{4,0},{5,21},{6,2},{7,23},{8,12},{9,25},... | collective-permute-start | bytes 786440 | tf_op jit(solution)/shard_map/ppermute | solution.py:306
  8.3 7.2 %collective-permute-start.4 = (bf16[512,256]{1,0:T(8,128)(2,1)S(1)}, bf16[512,256]{1,0:T(8,128)(2,1)S(1)}, u32[]{:S(2)}, u32[]{:S(2)}) collective-permute-start(bf16[512,256]{1,0:T(8,128)(2,1)S(1)} %constant_dynamic-slice_fusion.one), channel_id=1, source_target_pairs={{0,6},{1,25},{2,0},{3,27},{4,2},{5,29},{6,4},{7,31},{8,14},{9,1},{... | collective-permute-start | bytes 786440 | tf_op jit(solution)/shard_map/ppermute | solution.py:306
  9.2 6.7 %collective-permute-start.3 = (bf16[512,256]{1,0:T(8,128)(2,1)S(1)}, bf16[512,256]{1,0:T(8,128)(2,1)S(1)}, u32[]{:S(2)}, u32[]{:S(2)}) collective-permute-start(bf16[512,256]{1,0:T(8,128)(2,1)S(1)} %constant_dynamic-slice_fusion.one), channel_id=1, source_target_pairs={{0,2},{1,9},{2,4},{3,11},{4,6},{5,13},{6,0},{7,15},{8,10},{9,17},{... | collective-permute-start | bytes 786440 | tf_op jit(solution)/shard_map/ppermute | solution.py:306
  16.5 0.7 copy-start.1
  17.2 9.6 %collective-permute-start.6 = (bf16[1024,256]{1,0:T(8,128)(2,1)S(1)}, bf16[1024,256]{1,0:T(8,128)(2,1)S(1)}, u32[]{:S(2)}, u32[]{:S(2)}) collective-permute-start(bf16[1024,256]{1,0:T(8,128)(2,1)S(1)} %get-tuple-element.26.rest_0_), channel_id=1, source_target_pairs={{0,8},{1,3},{2,10},{3,5},{4,12},{5,7},{6,14},{7,1},{8,16},{9,11},{... | collective-permute-start | bytes 1572872 | tf_op jit(solution)/shard_map/ppermute | solution.py:319
  18.2 8.6 %collective-permute-start.9 = (bf16[1024,256]{1,0:T(8,128)(2,1)S(1)}, bf16[1024,256]{1,0:T(8,128)(2,1)S(1)}, u32[]{:S(2)}, u32[]{:S(2)}) collective-permute-start(bf16[1024,256]{1,0:T(8,128)(2,1)S(1)} %get-tuple-element.27.rest_1_), channel_id=1, source_target_pairs={{0,24},{1,7},{2,26},{3,1},{4,28},{5,3},{6,30},{7,5},{8,0},{9,15},{... | collective-permute-start | bytes 1572872 | tf_op jit(solution)/shard_map/ppermute | solution.py:320
  19.9 9.5 %collective-permute-start.1 = (bf16[2,16,1536]{2,1,0:T(8,128)(2,1)S(1)}, bf16[2,16,1536]{2,1,0:T(8,128)(2,1)S(1)}, u32[]{:S(2)}, u32[]{:S(2)}) collective-permute-start(bf16[2,16,1536]{2,1,0:T(8,128)(2,1)S(1)} %pad_maximum_fusion.1.after_ref), channel_id=1, source_target_pairs={{0,64},{32,96},{64,0},{96,32},{128,192},{160,224},{192,128},{224,1... | collective-permute-start | bytes 294920 | tf_op jit(solution)/shard_map/ppermute | solution.py:44
  22.9 16.5 %collective-permute-start.8 = (bf16[1024,256]{1,0:T(8,128)(2,1)S(1)}, bf16[1024,256]{1,0:T(8,128)(2,1)S(1)}, u32[]{:S(2)}, u32[]{:S(2)}) collective-permute-start(bf16[1024,256]{1,0:T(8,128)(2,1)S(1)} %get-tuple-element.26.rest_0_), channel_id=1, source_target_pairs={{0,24},{1,7},{2,26},{3,1},{4,28},{5,3},{6,30},{7,5},{8,0},{9,15},{... | collective-permute-start | bytes 1572872 | tf_op jit(solution)/shard_map/ppermute | solution.py:322
  24.4 15.0 %collective-permute-start.7 = (bf16[1024,256]{1,0:T(8,128)(2,1)S(1)}, bf16[1024,256]{1,0:T(8,128)(2,1)S(1)}, u32[]{:S(2)}, u32[]{:S(2)}) collective-permute-start(bf16[1024,256]{1,0:T(8,128)(2,1)S(1)} %get-tuple-element.27.rest_1_), channel_id=1, source_target_pairs={{0,8},{1,3},{2,10},{3,5},{4,12},{5,7},{6,14},{7,1},{8,16},{9,11},{... | collective-permute-start | bytes 1572872 | tf_op jit(solution)/shard_map/ppermute | solution.py:321
  26.8 12.8 %collective-permute-start.10 = (bf16[1024,256]{1,0:T(8,128)(2,1)S(1)}, bf16[1024,256]{1,0:T(8,128)(2,1)S(1)}, u32[]{:S(2)}, u32[]{:S(2)}) collective-permute-start(bf16[1024,256]{1,0:T(8,128)(2,1)S(1)} %collective-permute-done.6.refs_0_), channel_id=1, source_target_pairs={{0,8},{1,3},{2,10},{3,5},{4,12},{5,7},{6,14},{7,1},{8,16},{9,11},{... | collective-permute-start | bytes 1572872 | tf_op jit(solution)/shard_map/ppermute | solution.py:323
  26.8 12.8 %collective-permute-start.11 = (bf16[1024,256]{1,0:T(8,128)(2,1)S(1)}, bf16[1024,256]{1,0:T(8,128)(2,1)S(1)}, u32[]{:S(2)}, u32[]{:S(2)}) collective-permute-start(bf16[1024,256]{1,0:T(8,128)(2,1)S(1)} %collective-permute-done.9.refs_3_), channel_id=1, source_target_pairs={{0,24},{1,7},{2,26},{3,1},{4,28},{5,3},{6,30},{7,5},{8,0},{9,15},{... | collective-permute-start | bytes 1572872 | tf_op jit(solution)/shard_map/ppermute | solution.py:324
  29.5 9.9 %collective-permute-start.2 = (bf16[4,16,1536]{2,1,0:T(8,128)(2,1)S(1)}, bf16[4,16,1536]{2,1,0:T(8,128)(2,1)S(1)}, u32[]{:S(2)}, u32[]{:S(2)}) collective-permute-start(bf16[4,16,1536]{2,1,0:T(8,128)(2,1)S(1)} %pad_maximum_fusion.held_ref), channel_id=1, source_target_pairs={{0,192},{32,224},{64,128},{96,160},{128,64},{160,96},{192,0},{224,... | collective-permute-start | bytes 589832 | tf_op jit(solution)/shard_map/ppermute | solution.py:44
  41.4 12.0 %collective-permute-start.15 = (bf16[6144,256]{1,0:T(8,128)(2,1)}, bf16[6144,256]{1,0:T(8,128)(2,1)}, u32[]{:S(2)}, u32[]{:S(2)}) collective-permute-start(bf16[6144,256]{1,0:T(8,128)(2,1)} %shard_map.70.table.rest_2_), channel_id=1, source_target_pairs={{0,1},{1,0},{2,3},{3,2},{4,5},{5,4},{6,7},{7,6},{8,9},{9,8},{10,11... | collective-permute-start | bytes 9437192 | tf_op jit(solution)/shard_map/ppermute | solution.py:67
  46.1 6.7 %collective-permute-start.13 = (bf16[1024,256]{1,0:T(8,128)(2,1)S(1)}, bf16[1024,256]{1,0:T(8,128)(2,1)S(1)}, u32[]{:S(2)}, u32[]{:S(2)}) collective-permute-start(bf16[1024,256]{1,0:T(8,128)(2,1)S(1)} %get-tuple-element.26.rest_0_), channel_id=1, source_target_pairs={{0,1},{1,0},{2,3},{3,2},{4,5},{5,4},{6,7},{7,6},{8,9},{9,8},{10,11... | collective-permute-start | bytes 1572872 | tf_op jit(solution)/shard_map/ppermute | solution.py:67
  46.2 6.7 %collective-permute-start.14 = (bf16[1024,256]{1,0:T(8,128)(2,1)S(1)}, bf16[1024,256]{1,0:T(8,128)(2,1)}, u32[]{:S(2)}, u32[]{:S(2)}) collective-permute-start(bf16[1024,256]{1,0:T(8,128)(2,1)S(1)} %get-tuple-element.27.rest_1_), channel_id=1, source_target_pairs={{0,1},{1,0},{2,3},{3,2},{4,5},{5,4},{6,7},{7,6},{8,9},{9,8},{10,11... | collective-permute-start | bytes 1572872 | tf_op jit(solution)/shard_map/ppermute | solution.py:67
  46.6 0.9 copy-start.2
  50.5 2.9 %collective-permute-start.12 = (f32[256,256]{1,0:T(8,128)S(1)}, f32[256,256]{1,0:T(8,128)}, u32[]{:S(2)}, u32[]{:S(2)}) collective-permute-start(f32[256,256]{1,0:T(8,128)S(1)} %shard_map.71.gram_a), channel_id=1, source_target_pairs={{0,1},{1,0},{2,3},{3,2},{4,5},{5,4},{6,7},{7,6},{8,9},{9,8},{10,11... | collective-permute-start | bytes 786440 | tf_op jit(solution)/shard_map/ppermute | solution.py:67
  61.6 3.2 %collective-permute-start.16 = (f32[64,256]{1,0:T(8,128)S(1)}, f32[64,256]{1,0:T(8,128)S(1)}, u32[]{:S(2)}, u32[]{:S(2)}) collective-permute-start(f32[64,256]{1,0:T(8,128)S(1)} %get-tuple-element.29), channel_id=1, source_target_pairs={{0,32},{32,0},{64,96},{96,64},{128,160},{160,128},{192,224},{224,1... | collective-permute-start | bytes 196616 | tf_op jit(solution)/shard_map/ppermute | solution.py:44
  64.8 7.4 %collective-permute-start.19 = (f32[64,256]{1,0:T(8,128)S(1)}, f32[64,256]{1,0:T(8,128)S(1)}, u32[]{:S(2)}, u32[]{:S(2)}) collective-permute-start(f32[64,256]{1,0:T(8,128)S(1)} %add.112), channel_id=1, source_target_pairs={{0,192},{32,224},{64,0},{96,32},{128,64},{160,96},{192,128},{224,1... | collective-permute-start | bytes 196616 | tf_op jit(solution)/shard_map/ppermute | solution.py:44
  69.2 7.2 %collective-permute-start.18 = (f32[64,256]{1,0:T(8,128)S(1)}, f32[64,256]{1,0:T(8,128)S(1)}, u32[]{:S(2)}, u32[]{:S(2)}) collective-permute-start(f32[64,256]{1,0:T(8,128)S(1)} %add.112), channel_id=1, source_target_pairs={{0,128},{32,160},{64,192},{96,224},{128,0},{160,32},{192,64},{224,... | collective-permute-start | bytes 196616 | tf_op jit(solution)/shard_map/ppermute | solution.py:44
  70.3 6.7 %collective-permute-start.17 = (f32[64,256]{1,0:T(8,128)S(1)}, f32[64,256]{1,0:T(8,128)S(1)}, u32[]{:S(2)}, u32[]{:S(2)}) collective-permute-start(f32[64,256]{1,0:T(8,128)S(1)} %add.112), channel_id=1, source_target_pairs={{0,64},{32,96},{64,128},{96,160},{128,192},{160,224},{192,0},{224,... | collective-permute-start | bytes 196616 | tf_op jit(solution)/shard_map/ppermute | solution.py:44
  77.0 3.2 %collective-permute-start.20 = (f32[64,256]{1,0:T(8,128)S(1)}, f32[64,256]{1,0:T(8,128)S(1)}, u32[]{:S(2)}, u32[]{:S(2)}) collective-permute-start(f32[64,256]{1,0:T(8,128)S(1)} %add_add_fusion.1.mine_ref), channel_id=1, source_target_pairs={{0,32},{32,0},{64,96},{96,64},{128,160},{160,128},{192,224},{224,1... | collective-permute-start | bytes 196616 | tf_op jit(solution)/shard_map/ppermute | solution.py:44
  84.4 3.1 %collective-permute-start.21 = (f32[64,256]{1,0:T(8,128)S(1)}, f32[64,256]{1,0:T(8,128)S(1)}, u32[]{:S(2)}, u32[]{:S(2)}) collective-permute-start(f32[64,256]{1,0:T(8,128)S(1)} %get-tuple-element.33), channel_id=1, source_target_pairs={{0,32},{32,0},{64,96},{96,64},{128,160},{160,128},{192,224},{224,1... | collective-permute-start | bytes 196616 | tf_op jit(solution)/shard_map/ppermute | solution.py:44
  87.5 6.0 %collective-permute-start.24 = (f32[64,256]{1,0:T(8,128)S(1)}, f32[64,256]{1,0:T(8,128)S(1)}, u32[]{:S(2)}, u32[]{:S(2)}) collective-permute-start(f32[64,256]{1,0:T(8,128)S(1)} %add.116), channel_id=1, source_target_pairs={{0,192},{32,224},{64,0},{96,32},{128,64},{160,96},{192,128},{224,1... | collective-permute-start | bytes 196616 | tf_op jit(solution)/shard_map/ppermute | solution.py:44
  89.0 7.2 %collective-permute-start.23 = (f32[64,256]{1,0:T(8,128)S(1)}, f32[64,256]{1,0:T(8,128)S(1)}, u32[]{:S(2)}, u32[]{:S(2)}) collective-permute-start(f32[64,256]{1,0:T(8,128)S(1)} %add.116), channel_id=1, source_target_pairs={{0,128},{32,160},{64,192},{96,224},{128,0},{160,32},{192,64},{224,... | collective-permute-start | bytes 196616 | tf_op jit(solution)/shard_map/ppermute | solution.py:44
  92.0 5.6 %collective-permute-start.22 = (f32[64,256]{1,0:T(8,128)S(1)}, f32[64,256]{1,0:T(8,128)S(1)}, u32[]{:S(2)}, u32[]{:S(2)}) collective-permute-start(f32[64,256]{1,0:T(8,128)S(1)} %add.116), channel_id=1, source_target_pairs={{0,64},{32,96},{64,128},{96,160},{128,192},{160,224},{192,0},{224,... | collective-permute-start | bytes 196616 | tf_op jit(solution)/shard_map/ppermute | solution.py:44
  97.6 3.7 %collective-permute-start.25 = (f32[64,256]{1,0:T(8,128)S(1)}, f32[64,256]{1,0:T(8,128)S(1)}, u32[]{:S(2)}, u32[]{:S(2)}) collective-permute-start(f32[64,256]{1,0:T(8,128)S(1)} %add_add_fusion.mine_ref), channel_id=1, source_target_pairs={{0,32},{32,0},{64,96},{96,64},{128,160},{160,128},{192,224},{224,1... | collective-permute-start | bytes 196616 | tf_op jit(solution)/shard_map/ppermute | solution.py:44
  104.6 2.5 %collective-permute-start.26 = (f32[8,128]{1,0:T(8,128)S(1)}, f32[8,128]{1,0:T(8,128)S(1)}, u32[]{:S(2)}, u32[]{:S(2)}) collective-permute-start(f32[8,128]{1,0:T(8,128)S(1)} %get-tuple-element.35), channel_id=1, source_target_pairs={{0,32},{32,0},{64,96},{96,64},{128,160},{160,128},{192,224},{224,1... | collective-permute-start | bytes 12296 | tf_op jit(solution)/shard_map/ppermute | solution.py:44
  107.0 3.6 %collective-permute-start.27 = (f32[8,128]{1,0:T(8,128)S(1)}, f32[8,128]{1,0:T(8,128)S(1)}, u32[]{:S(2)}, u32[]{:S(2)}) collective-permute-start(f32[8,128]{1,0:T(8,128)S(1)} %add.120), channel_id=1, source_target_pairs={{0,64},{32,96},{64,0},{96,32},{128,192},{160,224},{192,128},{224,1... | collective-permute-start | bytes 12296 | tf_op jit(solution)/shard_map/ppermute | solution.py:44
  110.6 4.6 %collective-permute-start.28 = (f32[8,128]{1,0:T(8,128)S(1)}, f32[8,128]{1,0:T(8,128)S(1)}, u32[]{:S(2)}, u32[]{:S(2)}) collective-permute-start(f32[8,128]{1,0:T(8,128)S(1)} %add.121), channel_id=1, source_target_pairs={{0,192},{32,224},{64,128},{96,160},{128,64},{160,96},{192,0},{224,... | collective-permute-start | bytes 12296 | tf_op jit(solution)/shard_map/ppermute | solution.py:44
  138.8 15.3 %collective-permute-start.29 = (f32[1024,256]{1,0:T(8,128)S(1)}, f32[1024,256]{1,0:T(8,128)S(1)}, u32[]{:S(2)}, u32[]{:S(2)}) collective-permute-start(f32[1024,256]{1,0:T(8,128)S(1)} %shard_map.76), channel_id=1, source_target_pairs={{0,1},{1,0},{2,3},{3,2},{4,5},{5,4},{6,7},{7,6},{8,9},{9,8},{10,11... | collective-permute-start | bytes 3145736 | tf_op jit(solution)/shard_map/ppermute | solution.py:67
